TPU v7x, 32 devices: a whole 2x2x4 slice. The times are simulated.
32 devices in a mesh: member: 4 (over y, x), space: 8 (over z, core).
Axes of the slice: x: 2, y: 2, z: 4, core: 2. Of those that a mesh axis runs over, the one named last changes fastest.
Arguments:
- state: bfloat16 [8, 4, 16, 256, 1024], P('member', None, None, 'space'), may hold values from -4 to 4
Outputs:
- stepped: bfloat16 [8, 4, 16, 256, 1024], P('member', None, None, 'space')
- correlation: float32 [16, 256, 1024], P(None, 'space', 'member')
All inputs are finite; a program needn't handle non-finite values.
Results may differ from a plain program's by a relative error of at most 0.0041.
Values may be sent and summed in bfloat16 or wider, within the bound.
A program may use at most 320 MiB of HBM per device.

v0:
```python
import jax
import jax.numpy as jnp
from jax import lax
from jax.sharding import PartitionSpec as P

time_step = 0.2
viscosity = 0.1
var_floor = 0.25


def padded_2(cells, sides, width):
    for axis, dim in sides:
        count = lax.axis_size(axis)
        head = lax.slice_in_dim(cells, 0, width, axis=dim)
        tail = lax.slice_in_dim(cells, cells.shape[dim] - width, cells.shape[dim], axis=dim)
        cells = jnp.concatenate(
            [
                lax.ppermute(tail, axis, [(i, (i + 1) % count) for i in range(count)]),
                cells,
                lax.ppermute(head, axis, [((i + 1) % count, i) for i in range(count)]),
            ],
            axis=dim,
        )
    return cells


def advance(padded):
    whole = padded.astype(jnp.float32)
    center = whole[..., 2:-2, :]
    dxf = (
        8.0 * (whole[..., 3:-1, :] - whole[..., 1:-3, :]) - (whole[..., 4:, :] - whole[..., :-4, :])
    ) / 12.0
    yplus = jnp.roll(center, -1, -1)
    yminus = jnp.roll(center, 1, -1)
    dyf = (8.0 * (yplus - yminus) - (jnp.roll(center, -2, -1) - jnp.roll(center, 2, -1))) / 12.0
    zpad = jnp.pad(center, [(0, 0)] * (center.ndim - 3) + [(1, 1), (0, 0), (0, 0)])
    zup = zpad[..., 2:, :, :]
    zdown = zpad[..., :-2, :, :]
    dzf = (zup - zdown) * 0.5
    lap = whole[..., 3:-1, :] + whole[..., 1:-3, :] + yplus + yminus + zup + zdown - 6.0 * center
    uvel = center[..., 0:1, :, :, :]
    vvel = center[..., 1:2, :, :, :]
    wvel = center[..., 2:3, :, :, :]
    buoy = center[..., 3:4, :, :, :]
    tend = viscosity * lap - (uvel * dxf + vvel * dyf + wvel * dzf)
    force = jnp.concatenate([jnp.zeros_like(buoy), jnp.zeros_like(buoy), buoy, -wvel], axis=-4)
    return (center + time_step * (tend + force)).astype(jnp.bfloat16)


def correlate(sums, count):
    mean_b = sums[0] / count
    mean_w = sums[1] / count
    var_b = sums[2] / count - mean_b * mean_b
    var_w = sums[3] / count - mean_w * mean_w
    cov = sums[4] / count - mean_b * mean_w
    return cov / jnp.sqrt(jnp.maximum(var_b, var_floor) * jnp.maximum(var_w, var_floor))


def member_moments(wvel, buoy):
    return jnp.stack(
        [
            jnp.sum(buoy, 0),
            jnp.sum(wvel, 0),
            jnp.sum(buoy * buoy, 0),
            jnp.sum(wvel * wvel, 0),
            jnp.sum(buoy * wvel, 0),
        ]
    )


def on_device(state):
    current = state
    padded = padded_2(current, (("space", 3),), 2)
    current = advance(padded)
    count = jnp.float32(current.shape[0] * lax.axis_size("member"))
    terms = member_moments(current[:, 2].astype(jnp.float32), current[:, 3].astype(jnp.float32))
    sums = lax.psum_scatter(terms, "member", scatter_dimension=3, tiled=True)
    return (current, correlate(sums, count))


def solution(mesh):
    in_specs = (P("member", None, None, "space", None),)
    out_specs = (P("member", None, None, "space", None), P(None, "space", "member"))
    return jax.shard_map(
        on_device, mesh=mesh, in_specs=in_specs, out_specs=out_specs, check_vma=False
    )
```

profile of v0, /device:TPU:0, one launch (start us, length us, event | category | flops | bytes accessed | tf_op | source)
XLA Modules:
  0.0 309.5 jit_solution(38253112099421123)
XLA Ops:
  7.2 0.0 reduce-scatter.2.cloned.1.call-start
  7.2 3.3 %fusion.29 = (bf16[2,4,16,2,1024]{4,3,2,1,0:T(2,128)(2,1)S(1)}, bf16[2,4,16,2,1024]{4,3,2,1,0:T(2,128)(2,1)S(1)}) fusion(bf16[2,4,16,32,1024]{4,3,2,1,0:T(8,128)(2,1)} %param.1), kind=kLoop, calls=%fused_computation.55 | loop fusion | bytes 2097152 | tf_op jit(solution)/shard_map/slice | solution.py:15
  10.6 0.1 copy.8
  10.7 4.5 %collective-permute-start.1 = (bf16[2,4,16,2,1024]{4,2,3,1,0:T(8,128)(2,1)S(1)}, bf16[2,4,16,2,1024]{4,2,3,1,0:T(8,128)(2,1)S(1)}, u32[]{:S(2)}, u32[]{:S(2)}) collective-permute-start(bf16[2,4,16,2,1024]{4,2,3,1,0:T(8,128)(2,1)S(1)} %copy.8), channel_id=1, source_target_pairs={{1,0},{2,1},{3,2},{4,3},{5,4},{6,5},{7,6},{0,7},{9,8},{10,9},{11,1... | collective-permute-start | bytes 1572872 | tf_op jit(solution)/shard_map/ppermute | solution.py:20
  15.2 0.1 copy.7
  15.3 0.1 collective-permute-start
  15.4 10.3 %collective-permute-done.1 = bf16[2,4,16,2,1024]{4,2,3,1,0:T(8,128)(2,1)S(1)} collective-permute-done((bf16[2,4,16,2,1024]{4,2,3,1,0:T(8,128)(2,1)S(1)}, bf16[2,4,16,2,1024]{4,2,3,1,0:T(8,128)(2,1)S(1)}, u32[]{:S(2)}, u32[]{:S(2)}) %collective-permute-start.1) | collective-permute-done | bytes 524320 | tf_op jit(solution)/shard_map/ppermute | solution.py:20
  25.7 0.5 copy.6
  26.3 2.3 collective-permute-done
  28.6 0.5 copy.5
  29.1 6.6 %maximum_convert_fusion = f32[2,4,16,36,1024]{4,3,2,1,0:T(8,128)S(1)} fusion(bf16[2,4,16,2,1024]{4,3,2,1,0:T(2,128)(2,1)S(1)} %copy.6, bf16[2,4,16,32,1024]{4,3,2,1,0:T(8,128)(2,1)} %param.1, bf16[2,4,16,2,1024]{4,3,2,1,0:T(2,128)(2,1)S(1)} %copy.5), kind=kLoop, calls=%fused_computation.17 | loop fusion | flops 28311552 | bytes 28311552 | tf_op jit(solution)/shard_map/convert_element_type | solution.py:28
  35.7 0.0 copy-start
  35.8 2.8 fusion.26
  38.6 3.6 %fusion.27 = (f32[2,4,16,32,2]{4,3,2,1,0:T(8,128)}, f32[2,4,16,32,2]{4,3,2,1,0:T(8,128)}) fusion(f32[2,4,16,36,1024]{4,3,2,1,0:T(8,128)S(1)} %maximum_convert_fusion), kind=kLoop, calls=%fused_computation.53 | loop fusion | bytes 131072 | tf_op jit(solution)/shard_map/jit(_roll_static)/slice | solution.py:35
  42.2 2.7 copy-done
  44.9 8.3 %slice.134 = f32[2,4,16,32,1024]{4,3,2,1,0:T(8,128)} slice(f32[2,4,16,36,1024]{4,3,2,1,0:T(8,128)S(1)} %maximum_convert_fusion), slice={[0:2], [0:4], [0:16], [2:34], [0:1024]} | slice | bytes 33554432 | tf_op jit(solution)/shard_map/slice | solution.py:29
  53.2 15.9 %fusion.15 = (f32[2,16,32,1024]{3,2,1,0:T(8,128)}, f32[2,1,16,32,1024]{4,3,2,1,0:T(8,128)}, f32[2,1,16,32,1024]{4,3,2,1,0:T(8,128)}, f32[2,16,32,1024]{3,2,1,0:T(8,128)}, f32[2,16,32,1024]{3,2,1,0:T(8,128)}) fusion(f32[2,4,16,36,1024]{4,3,2,1,0:T(8,128)} %copy-done), kind=kLoop, calls=%fused_computation.29 | loop fusion | flops 4194304 | bytes 37748736 | tf_op jit(solution)/shard_map/mul | solution.py:45
  69.1 0.0 slice-start
  69.1 0.0 slice-start.1
  69.1 27.8 %fusion.25 = (f32[2,4,16,32,1023]{4,3,2,1,0:T(8,128)}, f32[2,4,16,32,1023]{4,3,2,1,0:T(8,128)}) fusion(f32[2,4,16,36,1024]{4,3,2,1,0:T(8,128)} %copy-done), kind=kLoop, calls=%fused_computation.51 | loop fusion | bytes 67043328 | tf_op jit(solution)/shard_map/jit(_roll_static)/slice | solution.py:33
  96.9 0.0 slice-start.2
  96.9 0.0 slice-start.3
  96.9 27.8 %fusion.28 = (f32[2,4,16,32,1022]{4,3,2,1,0:T(8,128)}, f32[2,4,16,32,1022]{4,3,2,1,0:T(8,128)}) fusion(f32[2,4,16,36,1024]{4,3,2,1,0:T(8,128)} %copy-done), kind=kLoop, calls=%fused_computation.54 | loop fusion | bytes 66977792 | tf_op jit(solution)/shard_map/jit(_roll_static)/slice | solution.py:35
  124.7 0.0 slice-done
  124.7 0.0 slice-done.1
  124.7 0.0 slice-done.2
  124.7 0.0 slice-done.3
  124.8 59.9 %fusion.8 = bf16[2,4,16,32,1024]{4,3,2,1,0:T(8,128)(2,1)} fusion(f32[2,4,16,32,1024]{4,3,2,1,0:T(8,128)S(1)} %bitcast.19, f32[2,4,16,36,1024]{4,3,2,1,0:T(8,128)} %copy-done, f32[2,4,16,32,2]{4,3,2,1,0:T(8,128)} %get-tuple-element.17, f32[2,4,16,32,1022]{4,3,2,1,0:T(8,128)} %get-tuple-element.19, f32[2,4,16,32,1022]{4,3,2,1,0:T(8,128)} %get-tuple-element.18, ...), kind=kLoop, calls=%fused_computation.11 | loop fusion | flops 138412032 | bytes 180355088 | tf_op jit(solution)/shard_map/convert_element_type | solution.py:47
  184.7 4.8 %fusion.13 = (f32[16,32,1024]{2,1,0:T(8,128)S(1)}, f32[16,32,1024]{2,1,0:T(8,128)S(1)}, f32[16,32,1024]{2,1,0:T(8,128)S(1)}, f32[16,32,1024]{2,1,0:T(8,128)S(1)}, f32[16,32,1024]{2,1,0:T(8,128)S(1)}) fusion(bf16[2,4,16,32,1024]{4,3,2,1,0:T(8,128)(2,1)} %fusion.8), kind=kLoop, calls=%fused_computation.25 | loop fusion | flops 7864320 | bytes 14680064 | tf_op jit(solution)/shard_map/reduce_sum | solution.py:66
  189.5 1.5 bitcast_dynamic-update-slice_fusion.4
  191.0 1.4 bitcast_dynamic-update-slice_fusion.3
  192.4 1.4 bitcast_dynamic-update-slice_fusion.2
  193.9 1.5 bitcast_dynamic-update-slice_fusion.1
  195.3 1.5 bitcast_dynamic-update-slice_fusion
  196.8 0.0 reduce-scatter.2.cloned.1.call-update
  196.9 103.0 %reduce-scatter.2.cloned.1.call-done = f32[5,16,32,256]{3,2,1,0:T(8,128)} async-done(((f32[5,16,32,1024]{3,2,1,0:T(8,128)}), f32[5,16,32,256]{3,2,1,0:T(8,128)}) %reduce-scatter.2.cloned.1.call-update) | async-done | bytes 2621456 | tf_op jit(solution)/shard_map/reduce_scatter | solution.py:77
  299.9 2.8 fusion.21
  (3 shorter events, 0.0 us)
Async XLA Ops:
  7.2 292.7 %reduce-scatter.2.cloned.1.call-start = ((), (), s32[]{:S(2)}) async-start(), calls=%async_computation.1 | async-start | bytes 13107200 | tf_op jit(solution)/shard_map/reduce_scatter | solution.py:77
  10.7 15.1 %collective-permute-start.1 = (bf16[2,4,16,2,1024]{4,2,3,1,0:T(8,128)(2,1)S(1)}, bf16[2,4,16,2,1024]{4,2,3,1,0:T(8,128)(2,1)S(1)}, u32[]{:S(2)}, u32[]{:S(2)}) collective-permute-start(bf16[2,4,16,2,1024]{4,2,3,1,0:T(8,128)(2,1)S(1)} %copy.8), channel_id=1, source_target_pairs={{1,0},{2,1},{3,2},{4,3},{5,4},{6,5},{7,6},{0,7},{9,8},{10,9},{11,1... | collective-permute-start | bytes 1572872 | tf_op jit(solution)/shard_map/ppermute | solution.py:20
  15.3 13.2 %collective-permute-start = (bf16[2,4,16,2,1024]{4,2,3,1,0:T(8,128)(2,1)S(1)}, bf16[2,4,16,2,1024]{4,2,3,1,0:T(8,128)(2,1)S(1)}, u32[]{:S(2)}, u32[]{:S(2)}) collective-permute-start(bf16[2,4,16,2,1024]{4,2,3,1,0:T(8,128)(2,1)S(1)} %copy.7), channel_id=1, source_target_pairs={{0,1},{1,2},{2,3},{3,4},{4,5},{5,6},{6,7},{7,0},{8,9},{9,10},{10,1... | collective-permute-start | bytes 1572872 | tf_op jit(solution)/shard_map/ppermute | solution.py:18
  35.7 9.2 %copy-start = (f32[2,4,16,36,1024]{4,3,2,1,0:T(8,128)}, f32[2,4,16,36,1024]{4,3,2,1,0:T(8,128)S(1)}, u32[]{:S(2)}) copy-start(f32[2,4,16,36,1024]{4,3,2,1,0:T(8,128)S(1)} %maximum_convert_fusion) | copy-start | bytes 56623108
  69.1 55.6 %slice-start = ((s8[16777216]{0:T(1024)(128)(4,1)}), s8[4194304]{0:T(1024)(128)(4,1)S(1)}, s32[]{:S(2)}) async-start(s8[16777216]{0:T(1024)(128)(4,1)} %bitcast.18), calls=%async_computation.2 | async-start | bytes 8388608
  69.1 55.6 %slice-start.1 = ((s8[16777216]{0:T(1024)(128)(4,1)}), s8[4194304]{0:T(1024)(128)(4,1)S(1)}, s32[]{:S(2)}) async-start(s8[16777216]{0:T(1024)(128)(4,1)} %bitcast.18), calls=%async_computation.3 | async-start | bytes 8388608
  96.9 27.8 %slice-start.2 = ((s8[16777216]{0:T(1024)(128)(4,1)}), s8[4194304]{0:T(1024)(128)(4,1)S(1)}, s32[]{:S(2)}) async-start(s8[16777216]{0:T(1024)(128)(4,1)} %bitcast.18), calls=%async_computation.4 | async-start | bytes 8388608
  96.9 27.8 %slice-start.3 = ((s8[16777216]{0:T(1024)(128)(4,1)}), s8[4194304]{0:T(1024)(128)(4,1)S(1)}, s32[]{:S(2)}) async-start(s8[16777216]{0:T(1024)(128)(4,1)} %bitcast.18), calls=%async_computation.5 | async-start | bytes 8388608
Sparse Core Ops, SparseCore 0:
  197.0 102.8 reduce-scatter.1
where the time goes:
time: 310 us; the launch traced here: 309 us
  waiting for transfers between devices  116 us (37%)
  other arithmetic  90 us (29%)
  local copies, waits for them, and re-layouts  85.1 us (27%)
  between operations  14.1 us (5%)
  starting transfers between devices  4.64 us (1%)
    reduce_scatter x1, waiting for transfers between devices, on_device(): sums = lax.psum_scatter(terms, 'member', scatter_dimension=3, tiled=True)  103 us
    convert_element_type x1, other arithmetic, advance(): return (center + time_step * (tend + force)).astype(jnp.bfloat16)  59.9 us
    slice x2, local copies, waits for them, and re-layouts, advance(): jnp.roll(center, 2, -1)  31.5 us
    slice x2, local copies, waits for them, and re-layouts, advance(): yplus = jnp.roll(center, -1, -1)  30.6 us
    mul x1, other arithmetic, advance(): tend = viscosity * lap - (uvel * dxf + vvel * dyf + wvel * dzf)  15.9 us
    ppermute x1, waiting for transfers between devices, padded_2(): lax.ppermute(head, axis, [((i + 1) % count, i) for i in range(count)])  10.3 us
    unnamed x16, local copies, waits for them, and re-layouts  8.75 us
    slice x1, local copies, waits for them, and re-layouts, advance(): center = whole[..., 2:-2, :]  8.34 us
  transfers between devices with their start and end apart: 3, of which 3 were waited for; matrix products, arithmetic and copies ran while one was open for 0% of the time, Pallas kernels for 0%

commit v1 on v0

v1 whole, which is shorter than its diff:
```python
import functools

import jax
import jax.numpy as jnp
import numpy as np
from jax import lax
from jax.experimental import pallas as pl
from jax.experimental.pallas import tpu as pltpu
from jax.sharding import PartitionSpec as P

time_step = 0.2
viscosity = 0.1
var_floor = 0.25
depth = 4


def stencil_matrix(levels, rows):
    chunks = levels // depth
    inner = (depth + 2) * rows
    a = np.zeros((chunks, 3, depth, rows, inner + 4 * levels), np.float32)

    def column(c, z, x):
        if x < 0:
            return inner + (c * depth + z) * 2 + x + 2
        if x >= rows:
            return inner + 2 * levels + (c * depth + z) * 2 + x - rows
        return (z + 1) * rows + x

    for c in range(chunks):
        for z in range(depth):
            for x in range(rows):
                for d, coef in ((1, 8), (-1, -8), (2, -1), (-2, 1)):
                    a[c, 0, z, x, column(c, z, x + d)] += coef
                a[c, 2, z, x, column(c, z, x + 1)] += 1
                a[c, 2, z, x, column(c, z, x - 1)] += 1
                a[c, 2, z, x, column(c, z, x)] -= 6
                for d in (1, -1):
                    if 0 <= c * depth + z + d < levels:
                        a[c, 1, z, x, (z + 1 + d) * rows + x] += d
                        a[c, 2, z, x, (z + 1 + d) * rows + x] += 1
    return a.reshape(chunks, 3 * depth * rows, -1).astype(jnp.bfloat16)


def step_kernel(first, parts, me_ref, a_ref, main, below, above, halo_lo, halo_hi, *rest):
    if first == 0:
        rest = rest[1:]
    out = rest[0]
    sends = rest[1:-1]
    res = rest[-1]
    rows, cols = main.shape[3], main.shape[4]
    half = 16
    per = rows // half
    for k in range(2):
        f = first + k
        w = jnp.concatenate(
            [below[0, k, 0]]
            + [main[0, f, z] for z in range(depth)]
            + [above[0, k, 0], halo_lo[0, k], halo_hi[0, k]],
            axis=0,
        )
        res[...] = jnp.dot(a_ref[0], w, preferred_element_type=jnp.float32)

        def tile(i, carry):
            z = i // per
            x = pl.multiple_of((i % per) * half, half)
            at = pl.multiple_of(i * half, half)
            span = depth * rows
            get = lambda g: main[0, g, z, pl.ds(x, half), :].astype(jnp.float32)
            u, v, wv = get(0), get(1), get(2)
            cen = get(f)
            dx = res[pl.ds(at, half), :]
            dz = res[pl.ds(span + at, half), :]
            lap = res[pl.ds(2 * span + at, half), :]
            yp = pltpu.roll(cen, cols - 1, 1)
            ym = pltpu.roll(cen, 1, 1)
            yp2 = pltpu.roll(cen, cols - 2, 1)
            ym2 = pltpu.roll(cen, 2, 1)
            dy = 8.0 * (yp - ym) - (yp2 - ym2)
            lap = lap + (yp + ym)
            s = time_step / 12.0
            new = cen + (time_step * viscosity) * lap - (s * (u * dx + v * dy) + (0.5 * time_step) * (wv * dz))
            if f == 2:
                new = new + time_step * get(3)
            elif f == 3:
                new = new - time_step * wv
            out[0, k, z, pl.ds(x, half), :] = new.astype(jnp.bfloat16)
            return carry

        lax.fori_loop(0, depth * per, tile, 0)
        part = cols // parts
        for j, send in enumerate(sends):
            q = me_ref[j]
            send[0, k] = out[0, k, :, :, pl.ds(pl.multiple_of(q * part, part), part)]


def run_step(first, parts, order, a, state, lo, hi, prior=None):
    m_, _, levels, rows, cols = state.shape
    chunks = levels // depth
    fb = first // 2
    sds = jax.ShapeDtypeStruct
    in_specs = [
        pl.BlockSpec((1,) + a.shape[1:], lambda m, c, me: (c, 0, 0)),
        pl.BlockSpec((1, 4, depth, rows, cols), lambda m, c, me: (m, 0, c, 0, 0)),
        pl.BlockSpec((1, 2, 1, rows, cols), lambda m, c, me: (m, fb, jnp.maximum(c * depth - 1, 0), 0, 0)),
        pl.BlockSpec((1, 2, 1, rows, cols), lambda m, c, me: (m, fb, jnp.minimum(c * depth + depth, levels - 1), 0, 0)),
        pl.BlockSpec((1, 2, 2 * levels, cols), lambda m, c, me: (m, fb, 0, 0)),
        pl.BlockSpec((1, 2, 2 * levels, cols), lambda m, c, me: (m, fb, 0, 0)),
    ]
    args = [order, a, state, state, state, lo, hi]
    out_shape = [sds(state.shape, state.dtype)]
    out_specs = [pl.BlockSpec((1, 2, depth, rows, cols), lambda m, c, me: (m, fb, c, 0, 0))]
    alias = {}
    if prior is not None:
        alias = {len(args): 0}
        args.append(prior)
        in_specs.append(pl.BlockSpec(memory_space=pl.ANY))
    else:
        for _ in range(parts):
            out_shape.append(sds((m_, 2, levels, rows, cols // parts), state.dtype))
            out_specs.append(pl.BlockSpec((1, 2, depth, rows, cols // parts), lambda m, c, me: (m, 0, c, 0, 0)))
    return pl.pallas_call(
        functools.partial(step_kernel, first, parts),
        out_shape=out_shape,
        grid_spec=pltpu.PrefetchScalarGridSpec(
            num_scalar_prefetch=1,
            grid=(m_, chunks),
            in_specs=in_specs,
            out_specs=out_specs,
            scratch_shapes=[pltpu.VMEM((3 * depth * rows, cols), jnp.float32)],
        ),
        input_output_aliases=alias,
        compiler_params=pltpu.CompilerParams(vmem_limit_bytes=40 * 2**20),
        cost_estimate=pl.CostEstimate(flops=20 * 10**9, bytes_accessed=16 * 2**20, transcendentals=0),
    )(*args)


def correlate_kernel(count, *refs):
    out = refs[-1]
    for z in range(out.shape[0]):
        sb = sw = sbb = sww = sbw = None
        for ref in refs[:-1]:
            for m in range(ref.shape[0]):
                w = ref[m, 0, z].astype(jnp.float32)
                b = ref[m, 1, z].astype(jnp.float32)
                if sb is None:
                    sb, sw, sbb, sww, sbw = b, w, b * b, w * w, b * w
                else:
                    sb, sw, sbb, sww, sbw = sb + b, sw + w, sbb + b * b, sww + w * w, sbw + b * w
        inv = 1.0 / count
        mb, mw = sb * inv, sw * inv
        vb = sbb * inv - mb * mb
        vw = sww * inv - mw * mw
        cov = sbw * inv - mb * mw
        out[z] = cov * lax.rsqrt(jnp.maximum(vb, var_floor) * jnp.maximum(vw, var_floor))


def run_correlate(count, blocks):
    m_, _, levels, rows, part = blocks[0].shape
    return pl.pallas_call(
        functools.partial(correlate_kernel, count),
        out_shape=jax.ShapeDtypeStruct((levels, rows, part), jnp.float32),
        grid=(levels // depth,),
        in_specs=[pl.BlockSpec((m_, 2, depth, rows, part), lambda c: (0, 0, c, 0, 0))] * len(blocks),
        out_specs=pl.BlockSpec((depth, rows, part), lambda c: (c, 0, 0)),
        compiler_params=pltpu.CompilerParams(vmem_limit_bytes=40 * 2**20),
        cost_estimate=pl.CostEstimate(flops=10**8, bytes_accessed=5 * 2**20, transcendentals=0),
    )(*blocks)


def partner(i, k, parts):
    if parts & (parts - 1) == 0:
        return i ^ k
    return (i + k) % parts


def on_device(parts, count, state):
    m_, _, levels, rows, cols = state.shape
    a = jnp.asarray(stencil_matrix(levels, rows))
    head = state[:, :, :, :2, :].reshape(m_, 4, 2 * levels, cols)
    tail = state[:, :, :, rows - 2 :, :].reshape(m_, 4, 2 * levels, cols)
    lo = lax.ppermute(tail, "space", [(i, (i + 1) % count) for i in range(count)])
    hi = lax.ppermute(head, "space", [((i + 1) % count, i) for i in range(count)])
    me = lax.axis_index("member")
    order = jnp.stack([jnp.asarray(partner(me, k, parts), jnp.int32) for k in range(parts)])
    stepped, *blocks = run_step(2, parts, order, a, state, lo, hi)
    got = [blocks[0]]
    for k in range(1, parts):
        got.append(lax.ppermute(blocks[k], "member", [(i, partner(i, k, parts)) for i in range(parts)]))
    (stepped,) = run_step(0, parts, order, a, state, lo, hi, stepped)
    return stepped, run_correlate(float(m_ * parts), got)


def solution(mesh):
    in_specs = (P("member", None, None, "space", None),)
    out_specs = (P("member", None, None, "space", None), P(None, "space", "member"))
    return jax.shard_map(
        functools.partial(on_device, mesh.shape["member"], mesh.shape["space"]),
        mesh=mesh, in_specs=in_specs, out_specs=out_specs, check_vma=False,
    )
```

time: 310 us -> 103 us (0.33)
  other arithmetic: 90 us -> 0.08 us
  waiting for transfers between devices: 116 us -> 28.6 us
  local copies, waits for them, and re-layouts: 85.1 us -> 8.94 us
  Pallas kernels: 0 us -> 55.1 us
  between operations: 14.1 us -> 0.67 us
  starting transfers between devices: 4.64 us -> 8.1 us
    reduce_scatter x1 -> x0, waiting for transfers between devices: 103 us -> none  [on_device(): sums = lax.psum_scatter(terms, 'member', scatter_dimension=3, tiled=True)]
    slice x6 -> x3, local copies, waits for them, and re-layouts: 73.8 us -> 4.11 us  [the longest x2 3.7 us: on_device(): head = state[:, :, :, :2, :].reshape(m_, 4, 2 * levels, cols)]
    convert_element_type x2 -> x0, other arithmetic: 66.6 us -> none  [the longest x1 59.9 us: advance(): return (center + time_step * (tend + force)).astype(jnp.bfloat16)]
    pallas_call x0 -> x3, Pallas kernels: none -> 55.1 us  [the longest x2 52.4 us: run_step(): pl.pallas_call(functools.partial(step_kernel, first, parts), out_shape=ou...]
    ppermute x2 -> x5, waiting for transfers between devices: 12.6 us -> 28.6 us  [the longest x3 19 us: on_device(): lax.ppermute(blocks[k], 'member', [(i, partner(i, k, parts)) for i in ran...]
    mul x1 -> x0, other arithmetic: 15.9 us -> none  [advance(): tend = viscosity * lap - (uvel * dxf + vvel * dyf + wvel * dzf)]
    reduce_sum x1 -> x0, other arithmetic: 4.79 us -> none  [member_moments(): jnp.sum(buoy * wvel, 0)]
    unnamed x16 -> x6, local copies, waits for them, and re-layouts: 8.75 us -> 4.52 us
  transfers between devices with their start and end apart: 3 -> 5, of which waited for: 3 -> 3; matrix products, arithmetic and copies ran while one was open for 0% -> 1% of each run, Pallas kernels for 0% -> 25%
where the time goes in v1:
time: 103 us; the launch traced here: 101 us
  Pallas kernels  55.1 us (53%)
  waiting for transfers between devices  28.6 us (28%)
  local copies, waits for them, and re-layouts  8.94 us (9%)
  starting transfers between devices  8.1 us (8%)
    pallas_call x2, Pallas kernels, run_step(): pl.pallas_call(functools.partial(step_kernel, first, parts), out_shape=ou...  52.4 us
    ppermute x3, waiting for transfers between devices, on_device(): lax.ppermute(blocks[k], 'member', [(i, partner(i, k, parts)) for i in ran...  19 us
    ppermute x1, waiting for transfers between devices, on_device(): lax.ppermute(tail, 'space', [(i, (i + 1) % count) for i in range(count)])  8.47 us
    unnamed x6, local copies, waits for them, and re-layouts  4.52 us
    ppermute x1, starting transfers between devices, on_device(): lax.ppermute(head, 'space', [((i + 1) % count, i) for i in range(count)])  4.11 us
    slice x2, local copies, waits for them, and re-layouts, on_device(): head = state[:, :, :, :2, :].reshape(m_, 4, 2 * levels, cols)  3.7 us
    ppermute x3, starting transfers between devices, on_device(): lax.ppermute(blocks[k], 'member', [(i, partner(i, k, parts)) for i in ran...  3.49 us
    pallas_call x1, Pallas kernels, run_correlate(): pl.pallas_call(functools.partial(correlate_kernel, count), out_shape=jax....  2.64 us
  transfers between devices with their start and end apart: 5, of which 3 were waited for; matrix products, arithmetic and copies ran while one was open for 1% of the time, Pallas kernels for 25%

profile of v1, /device:TPU:0, one launch (start us, length us, event | category | flops | bytes accessed | tf_op | source)
XLA Modules:
  0.0 101.5 jit_solution(4250664646015352772)
XLA Ops:
  0.6 3.3 %fusion = (bf16[2,4,16,2,1024]{4,3,2,1,0:T(2,128)(2,1)S(1)}, bf16[2,4,16,2,1024]{4,3,2,1,0:T(2,128)(2,1)S(1)}) fusion(bf16[2,4,16,32,1024]{4,3,2,1,0:T(8,128)(2,1)} %above.3), kind=kLoop, calls=%fused_computation.1 | loop fusion | bytes 2097152 | tf_op jit(solution)/shard_map/slice | solution.py:179
  3.9 0.4 copy.5
  4.3 0.2 copy.6
  4.5 0.5 collective-permute-start
  5.0 0.4 copy.7
  5.4 0.2 copy.8
  5.6 4.1 %collective-permute-start.1 = (bf16[2,4,32,1024]{3,2,1,0:T(8,128)(2,1)S(1)}, bf16[2,4,32,1024]{3,2,1,0:T(8,128)(2,1)S(1)}, u32[]{:S(2)}, u32[]{:S(2)}) collective-permute-start(bf16[2,4,32,1024]{3,2,1,0:T(8,128)(2,1)S(1)} %copy.8), channel_id=1, source_target_pairs={{1,0},{2,1},{3,2},{4,3},{5,4},{6,5},{7,6},{0,7},{9,8},{10,9},{11,1... | collective-permute-start | bytes 1572872 | tf_op jit(solution)/shard_map/ppermute | solution.py:182
  9.7 0.1 pad_add_fusion.me_ref
  9.8 8.5 %collective-permute-done.halo_lo = bf16[2,4,32,1024]{3,2,1,0:T(8,128)(2,1)S(1)} collective-permute-done((bf16[2,4,32,1024]{3,2,1,0:T(8,128)(2,1)S(1)}, bf16[2,4,32,1024]{3,2,1,0:T(8,128)(2,1)S(1)}, u32[]{:S(2)}, u32[]{:S(2)}) %collective-permute-start) | collective-permute-done | bytes 524320 | tf_op jit(solution)/shard_map/ppermute | solution.py:181
  18.2 1.1 %collective-permute-done.1.halo_hi = bf16[2,4,32,1024]{3,2,1,0:T(8,128)(2,1)S(1)} collective-permute-done((bf16[2,4,32,1024]{3,2,1,0:T(8,128)(2,1)S(1)}, bf16[2,4,32,1024]{3,2,1,0:T(8,128)(2,1)S(1)}, u32[]{:S(2)}, u32[]{:S(2)}) %collective-permute-start.1) | collective-permute-done | bytes 524320 | tf_op jit(solution)/shard_map/ppermute | solution.py:182
  19.4 0.0 copy-start
  19.4 3.4 %copy-done = bf16[2,4,16,32,1024]{4,3,2,1,0:T(8,128)(2,1)S(1)} copy-done((bf16[2,4,16,32,1024]{4,3,2,1,0:T(8,128)(2,1)S(1)}, bf16[2,4,16,32,1024]{4,3,2,1,0:T(8,128)(2,1)}, u32[]{:S(2)}) %copy-start) | copy-done | bytes 8388632
  22.8 0.0 copy-start.2
  22.8 1.1 %copy-done.2 = bf16[4,384,256]{2,1,0:T(8,128)(2,1)S(1)} copy-done((bf16[4,384,256]{2,1,0:T(8,128)(2,1)S(1)}, bf16[4,384,256]{2,1,0:T(8,128)(2,1)}, u32[]{:S(2)}) %copy-start.2) | copy-done | bytes 786456
  23.9 0.0 copy-start.1
  23.9 27.0 %shard_map.41 = (bf16[2,4,16,32,1024]{4,3,2,1,0:T(8,128)(2,1)}, bf16[2,2,16,32,256]{4,3,2,1,0:T(8,128)(2,1)S(1)}, bf16[2,2,16,32,256]{4,3,2,1,0:T(8,128)(2,1)S(1...) custom-call(s32[4]{0:T(128)S(1)} %pad_add_fusion.me_ref, bf16[4,384,256]{2,1,0:T(8,128)(2,1)S(1)} %copy-done.2, ...), custom_call_target="tpu_custom_call" | custom-call | flops 20000000000 | bytes 16777216 | tf_op jit(solution)/shard_map/pallas_call | solution.py:121
  50.9 1.5 %collective-permute-start.2 = (bf16[2,2,16,32,256]{4,3,2,1,0:T(8,128)(2,1)S(1)}, bf16[2,2,16,32,256]{4,3,2,1,0:T(8,128)(2,1)S(1)}, u32[]{:S(2)}, u32[]{:S(2)}) collective-permute-start(bf16[2,2,16,32,256]{4,3,2,1,0:T(8,128)(2,1)S(1)} %get-tuple-element.9), channel_id=1, source_target_pairs={{0,8},{8,0},{16,24},{24,16},{1,9},{9,1},{17,25},{25,17},{2,10},{10... | collective-permute-start | bytes 3145736 | tf_op jit(solution)/shard_map/ppermute | solution.py:188
  52.4 1.5 %collective-permute-start.3 = (bf16[2,2,16,32,256]{4,3,2,1,0:T(8,128)(2,1)S(1)}, bf16[2,2,16,32,256]{4,3,2,1,0:T(8,128)(2,1)S(1)}, u32[]{:S(2)}, u32[]{:S(2)}) collective-permute-start(bf16[2,2,16,32,256]{4,3,2,1,0:T(8,128)(2,1)S(1)} %get-tuple-element.10), channel_id=1, source_target_pairs={{0,16},{8,24},{16,0},{24,8},{1,17},{9,25},{17,1},{25,9},{2,18},{10... | collective-permute-start | bytes 3145736 | tf_op jit(solution)/shard_map/ppermute | solution.py:188
  53.9 0.5 collective-permute-start.4
  54.4 0.0 copy-done.1
  54.4 25.4 %shard_map.42 = bf16[2,4,16,32,1024]{4,3,2,1,0:T(8,128)(2,1)} custom-call(s32[4]{0:T(128)S(1)} %pad_add_fusion.me_ref, bf16[4,384,256]{2,1,0:T(8,128)(2,1)S(1)} %copy-done.2, bf16[2,4,16,32,1024]{4,3,2,1,0:T(8,128)(2,1)S(1)} %copy-done.1, bf16[2,4,16,32,1024]{4,3,2,1,0:T(8,128)(2,1)S(1)} %copy-done.1, ...), custom_call_target="tpu_custom_call", output_to_operand_aliasing={{}: (7, {})} | custom-call | flops 20000000000 | bytes 16777216 | tf_op jit(solution)/shard_map/pallas_call | solution.py:121
  79.8 0.0 collective-permute-done.2.refs_1_
  79.8 0.0 collective-permute-done.3.refs_2_
  79.8 19.0 %collective-permute-done.4.refs_3_ = bf16[2,2,16,32,256]{4,3,2,1,0:T(8,128)(2,1)S(1)} collective-permute-done((bf16[2,2,16,32,256]{4,3,2,1,0:T(8,128)(2,1)S(1)}, bf16[2,2,16,32,256]{4,3,2,1,0:T(8,128)(2,1)S(1)}, u32[]{:S(2)}, u32[]{:S(2)}) %collective-permute-start.4) | collective-permute-done | bytes 1048608 | tf_op jit(solution)/shard_map/ppermute | solution.py:188
  98.8 2.6 %shard_map.43 = f32[16,32,256]{2,1,0:T(8,128)} custom-call(bf16[2,2,16,32,256]{4,3,2,1,0:T(8,128)(2,1)S(1)} %get-tuple-element.8.refs_0_, bf16[2,2,16,32,256]{4,3,2,1,0:T(8,128)(2,1)S(1)} %collective-permute-done.2.refs_1_, bf16[2,2,16,32,256]{4,3,2,1,0:T(8,128)(2,1)S(1)} %collective-permute-done.3.refs_2_, ...), custom_call_target="tpu_custom_call" | custom-call | flops 100000000 | bytes 5242880 | tf_op jit(solution)/shard_map/pallas_call | solution.py:159
Async XLA Ops:
  4.5 13.7 %collective-permute-start = (bf16[2,4,32,1024]{3,2,1,0:T(8,128)(2,1)S(1)}, bf16[2,4,32,1024]{3,2,1,0:T(8,128)(2,1)S(1)}, u32[]{:S(2)}, u32[]{:S(2)}) collective-permute-start(bf16[2,4,32,1024]{3,2,1,0:T(8,128)(2,1)S(1)} %copy.6), channel_id=1, source_target_pairs={{0,1},{1,2},{2,3},{3,4},{4,5},{5,6},{6,7},{7,0},{8,9},{9,10},{10,1... | collective-permute-start | bytes 1572872 | tf_op jit(solution)/shard_map/ppermute | solution.py:181
  5.6 13.8 %collective-permute-start.1 = (bf16[2,4,32,1024]{3,2,1,0:T(8,128)(2,1)S(1)}, bf16[2,4,32,1024]{3,2,1,0:T(8,128)(2,1)S(1)}, u32[]{:S(2)}, u32[]{:S(2)}) collective-permute-start(bf16[2,4,32,1024]{3,2,1,0:T(8,128)(2,1)S(1)} %copy.8), channel_id=1, source_target_pairs={{1,0},{2,1},{3,2},{4,3},{5,4},{6,5},{7,6},{0,7},{9,8},{10,9},{11,1... | collective-permute-start | bytes 1572872 | tf_op jit(solution)/shard_map/ppermute | solution.py:182
  19.4 3.4 %copy-start = (bf16[2,4,16,32,1024]{4,3,2,1,0:T(8,128)(2,1)S(1)}, bf16[2,4,16,32,1024]{4,3,2,1,0:T(8,128)(2,1)}, u32[]{:S(2)}) copy-start(bf16[2,4,16,32,1024]{4,3,2,1,0:T(8,128)(2,1)} %above.3) | copy-start | bytes 25165828
  22.8 1.1 %copy-start.2 = (bf16[4,384,256]{2,1,0:T(8,128)(2,1)S(1)}, bf16[4,384,256]{2,1,0:T(8,128)(2,1)}, u32[]{:S(2)}) copy-start(bf16[4,384,256]{2,1,0:T(8,128)(2,1)} %constant.13.clone.a_ref) | copy-start | bytes 2359300
  23.9 30.5 %copy-start.1 = (bf16[2,4,16,32,1024]{4,3,2,1,0:T(8,128)(2,1)S(1)}, bf16[2,4,16,32,1024]{4,3,2,1,0:T(8,128)(2,1)}, u32[]{:S(2)}) copy-start(bf16[2,4,16,32,1024]{4,3,2,1,0:T(8,128)(2,1)} %above.3) | copy-start | bytes 25165828
  50.9 28.9 %collective-permute-start.2 = (bf16[2,2,16,32,256]{4,3,2,1,0:T(8,128)(2,1)S(1)}, bf16[2,2,16,32,256]{4,3,2,1,0:T(8,128)(2,1)S(1)}, u32[]{:S(2)}, u32[]{:S(2)}) collective-permute-start(bf16[2,2,16,32,256]{4,3,2,1,0:T(8,128)(2,1)S(1)} %get-tuple-element.9), channel_id=1, source_target_pairs={{0,8},{8,0},{16,24},{24,16},{1,9},{9,1},{17,25},{25,17},{2,10},{10... | collective-permute-start | bytes 3145736 | tf_op jit(solution)/shard_map/ppermute | solution.py:188
  52.4 27.5 %collective-permute-start.3 = (bf16[2,2,16,32,256]{4,3,2,1,0:T(8,128)(2,1)S(1)}, bf16[2,2,16,32,256]{4,3,2,1,0:T(8,128)(2,1)S(1)}, u32[]{:S(2)}, u32[]{:S(2)}) collective-permute-start(bf16[2,2,16,32,256]{4,3,2,1,0:T(8,128)(2,1)S(1)} %get-tuple-element.10), channel_id=1, source_target_pairs={{0,16},{8,24},{16,0},{24,8},{1,17},{9,25},{17,1},{25,9},{2,18},{10... | collective-permute-start | bytes 3145736 | tf_op jit(solution)/shard_map/ppermute | solution.py:188
  53.9 45.0 %collective-permute-start.4 = (bf16[2,2,16,32,256]{4,3,2,1,0:T(8,128)(2,1)S(1)}, bf16[2,2,16,32,256]{4,3,2,1,0:T(8,128)(2,1)S(1)}, u32[]{:S(2)}, u32[]{:S(2)}) collective-permute-start(bf16[2,2,16,32,256]{4,3,2,1,0:T(8,128)(2,1)S(1)} %get-tuple-element.11), channel_id=1, source_target_pairs={{0,24},{8,16},{16,8},{24,0},{1,25},{9,17},{17,9},{25,1},{2,26},{10... | collective-permute-start | bytes 3145736 | tf_op jit(solution)/shard_map/ppermute | solution.py:188

commit v2 on v1

v2 whole, which is shorter than its diff:
```python
import functools

import jax
import jax.numpy as jnp
import numpy as np
from jax import lax
from jax.experimental import pallas as pl
from jax.experimental.pallas import tpu as pltpu
from jax.sharding import PartitionSpec as P

time_step = 0.2
viscosity = 0.1
var_floor = 0.25
depth = 4
edge = 8
vmem = 56 * 2**20


def stencil_matrix(levels, rows, spans, halos):
    chunks = levels // depth
    inner = (depth + 2) * rows
    xs = [x for start, stop in spans for x in range(start, stop)]
    a = np.zeros((chunks, 3, depth, len(xs), inner + (4 * levels if halos else 0)), np.float32)

    def column(c, z, x):
        if x < 0:
            return inner + (c * depth + z) * 2 + x + 2
        if x >= rows:
            return inner + 2 * levels + (c * depth + z) * 2 + x - rows
        return (z + 1) * rows + x

    for c in range(chunks):
        for z in range(depth):
            for n, x in enumerate(xs):
                for d, coef in ((1, 8), (-1, -8), (2, -1), (-2, 1)):
                    a[c, 0, z, n, column(c, z, x + d)] += coef
                a[c, 2, z, n, column(c, z, x + 1)] += 1
                a[c, 2, z, n, column(c, z, x - 1)] += 1
                a[c, 2, z, n, column(c, z, x)] -= 6
                for d in (1, -1):
                    if 0 <= c * depth + z + d < levels:
                        a[c, 1, z, n, (z + 1 + d) * rows + x] += d
                        a[c, 2, z, n, (z + 1 + d) * rows + x] += 1
    return jnp.asarray(a.reshape(chunks, 3 * depth * len(xs), -1).astype(jnp.bfloat16))


def step_kernel(kind, first, parts, spans, me_ref, a_ref, main, below, above, *rest):
    rest = list(rest)
    halos = [rest.pop(0), rest.pop(0)] if kind != "mid" else []
    mid = rest.pop(0) if kind == "edge" else None
    res = rest.pop()
    held = rest.pop() if kind == "edge" else None
    if kind == "edge":
        out, sends = rest[-1 - parts], rest[-parts:]
    elif kind == "mid":
        out, sends = rest[0], rest[1:]
    else:
        out, sends = rest[-1], []
    rows, cols = main.shape[3], main.shape[4]
    count = sum(stop - start for start, stop in spans)
    total = depth * count
    for k in range(2):
        f = first + k
        w = jnp.concatenate(
            [below[0, k, 0]] + [main[0, f, z] for z in range(depth)] + [above[0, k, 0]] + [h[0, k] for h in halos],
            axis=0,
        )
        res[...] = jnp.dot(a_ref[0], w, preferred_element_type=jnp.float32)

        def level(z, carry):
            def get(g, start, stop):
                if kind == "rest":
                    return main[0, g, z, start:stop, :].astype(jnp.float32)
                return main[0, g, z].astype(jnp.float32)[start:stop]

            news = []
            at = 0
            for start, stop in spans:
                base = pl.multiple_of(z * count, 16) + at
                at += stop - start
                u, v, wv = get(0, start, stop), get(1, start, stop), get(2, start, stop)
                cen = get(f, start, stop)
                size = stop - start
                dx = res[pl.ds(pl.multiple_of(base, 8), size), :]
                dz = res[pl.ds(pl.multiple_of(total + base, 8), size), :]
                lap = res[pl.ds(pl.multiple_of(2 * total + base, 8), size), :]
                yp = pltpu.roll(cen, cols - 1, 1)
                ym = pltpu.roll(cen, 1, 1)
                yp2 = pltpu.roll(cen, cols - 2, 1)
                ym2 = pltpu.roll(cen, 2, 1)
                dy = 8.0 * (yp - ym) - (yp2 - ym2)
                lap = lap + (yp + ym)
                s = time_step / 12.0
                new = cen + (time_step * viscosity) * lap - (s * (u * dx + v * dy) + (0.5 * time_step) * (wv * dz))
                if f == 2:
                    new = new + time_step * get(3, start, stop)
                elif f == 3:
                    new = new - time_step * wv
                if kind == "rest":
                    out[0, k, z, start:stop, :] = new.astype(jnp.bfloat16)
                news.append(new)
            if kind == "mid":
                out[0, k, z] = jnp.concatenate(news, axis=0).astype(jnp.bfloat16)
            elif kind == "edge":
                held[z] = jnp.concatenate(news, axis=0).astype(jnp.bfloat16)
                inner = mid[0, k, z].astype(jnp.float32)
                out[0, k, z] = jnp.concatenate([news[0], inner, news[1]], axis=0).astype(jnp.bfloat16)
            return carry

        lax.fori_loop(0, depth, level, 0)
        part = cols // parts
        for j, send in enumerate(sends):
            at = pl.ds(pl.multiple_of(me_ref[j] * part, part), part)
            send[0, k] = held[:, :, at] if kind == "edge" else out[0, k, :, :, at]


def run_step(kind, first, members, parts, spans, order, state, lo=None, hi=None, mid=None, prior=None):
    _, _, levels, rows, cols = state.shape
    chunks = levels // depth
    fb = first // 2
    m0, m1 = members
    a = stencil_matrix(levels, rows, spans, kind != "mid")
    count = sum(stop - start for start, stop in spans)
    sds = jax.ShapeDtypeStruct
    in_specs = [
        pl.BlockSpec((1,) + a.shape[1:], lambda m, c, me: (c, 0, 0)),
        pl.BlockSpec((1, 4, depth, rows, cols), lambda m, c, me: (m + m0, 0, c, 0, 0)),
        pl.BlockSpec((1, 2, 1, rows, cols), lambda m, c, me: (m + m0, fb, jnp.maximum(c * depth - 1, 0), 0, 0)),
        pl.BlockSpec((1, 2, 1, rows, cols), lambda m, c, me: (m + m0, fb, jnp.minimum(c * depth + depth, levels - 1), 0, 0)),
    ]
    args = [order, a, state, state, state]
    if kind != "mid":
        in_specs += [pl.BlockSpec((1, 2, 2 * levels, cols), lambda m, c, me: (m + m0, fb, 0, 0))] * 2
        args += [lo, hi]
    if kind == "edge":
        in_specs.append(pl.BlockSpec((1, 2, depth, rows - count, cols), lambda m, c, me: (m, 0, c, 0, 0)))
        args.append(mid)
    alias = {}
    if prior is not None:
        alias = {len(args): 0}
        args.append(prior)
        in_specs.append(pl.BlockSpec(memory_space=pl.ANY))
    if kind == "mid":
        out_shape = [sds((m1 - m0, 2, levels, count, cols), state.dtype)]
        out_specs = [pl.BlockSpec((1, 2, depth, count, cols), lambda m, c, me: (m, 0, c, 0, 0))]
    else:
        out_shape = [sds(state.shape, state.dtype)]
        out_specs = [pl.BlockSpec((1, 2, depth, rows, cols), lambda m, c, me: (m + m0, fb, c, 0, 0))]
    if kind != "rest":
        out_shape += [sds((m1 - m0, 2, levels, count, cols // parts), state.dtype)] * parts
        out_specs += [pl.BlockSpec((1, 2, depth, count, cols // parts), lambda m, c, me: (m, 0, c, 0, 0))] * parts
    scratch = [pltpu.VMEM((3 * depth * count, cols), jnp.float32)]
    if kind == "edge":
        scratch.insert(0, pltpu.VMEM((depth, count, cols), jnp.bfloat16))
    share = (m1 - m0) * count
    return pl.pallas_call(
        functools.partial(step_kernel, kind, first, parts, spans),
        out_shape=out_shape,
        grid_spec=pltpu.PrefetchScalarGridSpec(
            num_scalar_prefetch=1, grid=(m1 - m0, chunks), in_specs=in_specs, out_specs=out_specs, scratch_shapes=scratch
        ),
        input_output_aliases=alias,
        compiler_params=pltpu.CompilerParams(vmem_limit_bytes=vmem),
        cost_estimate=pl.CostEstimate(flops=share * 4 * 10**8, bytes_accessed=share * 2**18, transcendentals=0),
    )(*args)


def correlate_kernel(count, *refs):
    out = refs[-1]
    n = (len(refs) - 1) // 2
    inv = 1.0 / count

    def rows_of(blocks, z):
        sums = None
        for ref in blocks:
            for m in range(ref.shape[0]):
                w = ref[m, 0, z].astype(jnp.float32)
                b = ref[m, 1, z].astype(jnp.float32)
                terms = (b, w, b * b, w * w, b * w)
                sums = terms if sums is None else [p + q for p, q in zip(sums, terms)]
        mb, mw = sums[0] * inv, sums[1] * inv
        vb = sums[2] * inv - mb * mb
        vw = sums[3] * inv - mw * mw
        cov = sums[4] * inv - mb * mw
        return cov * lax.rsqrt(jnp.maximum(vb, var_floor) * jnp.maximum(vw, var_floor))

    for z in range(out.shape[0]):
        inner = rows_of(refs[:n], z)
        outer = rows_of(refs[n:-1], z)
        out[z] = jnp.concatenate([outer[:edge], inner, outer[edge:]], axis=0)


def run_correlate(count, mids, edges):
    _, _, levels, middle, part = mids[0].shape
    rows = middle + 2 * edge
    specs = [pl.BlockSpec(b.shape[:2] + (depth,) + b.shape[3:], lambda c: (0, 0, c, 0, 0)) for b in mids + edges]
    return pl.pallas_call(
        functools.partial(correlate_kernel, count),
        out_shape=jax.ShapeDtypeStruct((levels, rows, part), jnp.float32),
        grid=(levels // depth,),
        in_specs=specs,
        out_specs=pl.BlockSpec((depth, rows, part), lambda c: (c, 0, 0)),
        compiler_params=pltpu.CompilerParams(vmem_limit_bytes=vmem),
        cost_estimate=pl.CostEstimate(flops=10**8, bytes_accessed=5 * 2**20, transcendentals=0),
    )(*mids, *edges)


def partner(i, k, parts):
    if parts & (parts - 1) == 0:
        return i ^ k
    return (i + k) % parts


def on_device(parts, count, state):
    m_, _, levels, rows, cols = state.shape
    head = state[:, :, :, :2, :].reshape(m_, 4, 2 * levels, cols)
    tail = state[:, :, :, rows - 2 :, :].reshape(m_, 4, 2 * levels, cols)
    lo = lax.ppermute(tail, "space", [(i, (i + 1) % count) for i in range(count)])
    hi = lax.ppermute(head, "space", [((i + 1) % count, i) for i in range(count)])
    me = lax.axis_index("member")
    order = jnp.stack([jnp.asarray(partner(me, k, parts), jnp.int32) for k in range(parts)])

    def exchange(blocks):
        got = [blocks[0]]
        for k in range(1, parts):
            got.append(lax.ppermute(blocks[k], "member", [(i, partner(i, k, parts)) for i in range(parts)]))
        return got

    inner = ((edge, rows - edge),)
    outer = ((0, edge), (rows - edge, rows))
    halves = tuple((x, x + 16) for x in range(0, rows, 16))
    middles, mids, edges = [], [], []
    for m in range(m_):
        middle, *blocks = run_step("mid", 2, (m, m + 1), parts, inner, order, state)
        middles.append(middle)
        mids += exchange(blocks)
    stepped = None
    for m in range(m_):
        stepped, *blocks = run_step("edge", 2, (m, m + 1), parts, outer, order, state, lo, hi, middles[m], stepped)
        edges += exchange(blocks)
    (stepped,) = run_step("rest", 0, (0, m_), parts, halves, order, state, lo, hi, None, stepped)
    return stepped, run_correlate(float(m_ * parts), mids, edges)


def solution(mesh):
    in_specs = (P("member", None, None, "space", None),)
    out_specs = (P("member", None, None, "space", None), P(None, "space", "member"))
    return jax.shard_map(
        functools.partial(on_device, mesh.shape["member"], mesh.shape["space"]),
        mesh=mesh, in_specs=in_specs, out_specs=out_specs, check_vma=False,
    )
```

time: 103 us -> 100 us (0.971); the launches traced: 101 us -> 99.8 us
  waiting for transfers between devices: 28.6 us -> 8.54 us
  starting transfers between devices: 8.1 us -> 19.6 us
  Pallas kernels: 55.1 us -> 64.8 us
  local copies, waits for them, and re-layouts: 8.94 us -> 5.46 us
    ppermute x3 -> x12, starting transfers between devices: 3.49 us -> 14.9 us  [exchange(): lax.ppermute(blocks[k], 'member', [(i, partner(i, k, parts)) for i in ran...]
    ppermute x3 -> x12, waiting for transfers between devices: 19 us -> 8.54 us  [exchange(): lax.ppermute(blocks[k], 'member', [(i, partner(i, k, parts)) for i in ran...]
    ppermute x1, waiting for transfers between devices: 8.47 us -> 0.01 us  [on_device(): lax.ppermute(tail, 'space', [(i, (i + 1) % count) for i in range(count)])]
    pallas_call x2 -> x5, Pallas kernels: 52.4 us -> 60.3 us  [run_step(): pl.pallas_call(functools.partial(step_kernel, kind, first, parts, spans),...]
    unnamed x6 -> x36, local copies, waits for them, and re-layouts: 4.52 us -> 1.04 us
    pallas_call x1, Pallas kernels: 2.64 us -> 4.49 us  [run_correlate(): pl.pallas_call(functools.partial(correlate_kernel, count), out_shape=jax....]
    ppermute x1, waiting for transfers between devices: 1.13 us -> 0.01 us  [on_device(): lax.ppermute(head, 'space', [((i + 1) % count, i) for i in range(count)])]
  transfers between devices with their start and end apart: 5 -> 14, of which waited for: 3 -> 2; matrix products, arithmetic and copies ran while one was open for 1% -> 1% of each run, Pallas kernels for 25% -> 60%
where the time goes in v2:
time: 100 us; the launch traced here: 99.8 us
  Pallas kernels  64.8 us (65%)
  starting transfers between devices  19.6 us (20%)
  waiting for transfers between devices  8.54 us (9%)
  local copies, waits for them, and re-layouts  5.46 us (5%)
    pallas_call x5, Pallas kernels, run_step(): pl.pallas_call(functools.partial(step_kernel, kind, first, parts, spans),...  60.3 us
    ppermute x12, starting transfers between devices, exchange(): lax.ppermute(blocks[k], 'member', [(i, partner(i, k, parts)) for i in ran...  14.9 us
    ppermute x12, waiting for transfers between devices, exchange(): lax.ppermute(blocks[k], 'member', [(i, partner(i, k, parts)) for i in ran...  8.54 us
    pallas_call x1, Pallas kernels, run_correlate(): pl.pallas_call(functools.partial(correlate_kernel, count), out_shape=jax....  4.49 us
    ppermute x1, starting transfers between devices, on_device(): lax.ppermute(head, 'space', [((i + 1) % count, i) for i in range(count)])  4.11 us
    slice x2, local copies, waits for them, and re-layouts, on_device(): head = state[:, :, :, :2, :].reshape(m_, 4, 2 * levels, cols)  3.7 us
  transfers between devices with their start and end apart: 14, of which 2 were waited for; matrix products, arithmetic and copies ran while one was open for 1% of the time, Pallas kernels for 60%

profile of v2, /device:TPU:0, one launch (start us, length us, event | category | flops | bytes accessed | tf_op | source)
XLA Modules:
  0.0 99.8 jit_solution(9017948918262114743)
XLA Ops:
  0.6 3.3 %fusion = (bf16[2,4,16,2,1024]{4,3,2,1,0:T(2,128)(2,1)S(1)}, bf16[2,4,16,2,1024]{4,3,2,1,0:T(2,128)(2,1)S(1)}) fusion(bf16[2,4,16,32,1024]{4,3,2,1,0:T(8,128)(2,1)} %above.9), kind=kLoop, calls=%fused_computation.1 | loop fusion | bytes 2097152 | tf_op jit(solution)/shard_map/slice | solution.py:216
  3.9 0.4 copy.10
  4.3 0.2 copy.11
  4.5 0.5 collective-permute-start
  5.0 0.4 copy.12
  5.4 0.2 copy.13
  5.6 4.1 %collective-permute-start.1 = (bf16[2,4,32,1024]{3,2,1,0:T(8,128)(2,1)S(1)}, bf16[2,4,32,1024]{3,2,1,0:T(8,128)(2,1)S(1)}, u32[]{:S(2)}, u32[]{:S(2)}) collective-permute-start(bf16[2,4,32,1024]{3,2,1,0:T(8,128)(2,1)S(1)} %copy.13), channel_id=1, source_target_pairs={{1,0},{2,1},{3,2},{4,3},{5,4},{6,5},{7,6},{0,7},{9,8},{10,9},{11,1... | collective-permute-start | bytes 1572872 | tf_op jit(solution)/shard_map/ppermute | solution.py:219
  9.7 0.7 pad_add_fusion.me_ref
  10.4 9.5 %shard_map.78 = (bf16[1,2,16,16,1024]{4,3,2,1,0:T(8,128)(2,1)}, bf16[1,2,16,16,256]{4,3,2,1,0:T(8,128)(2,1)}, bf16[1,2,16,16,256]{4,3,2,1,0:T(8,128)(2,1)}, bf16...) custom-call(s32[4]{0:T(128)} %pad_add_fusion.me_ref, bf16[4,192,192]{2,1,0:T(8,128)(2,1)} %constant.17.clone.a_ref, ...), custom_call_target="tpu_custom_call" | custom-call | flops 6400000000 | bytes 4194304 | tf_op jit(solution)/shard_map/pallas_call | solution.py:156
  19.9 2.0 %collective-permute-start.2 = (bf16[1,2,16,16,256]{4,3,2,1,0:T(8,128)(2,1)}, bf16[1,2,16,16,256]{4,3,2,1,0:T(8,128)(2,1)S(1)}, u32[]{:S(2)}, u32[]{:S(2)}) collective-permute-start(bf16[1,2,16,16,256]{4,3,2,1,0:T(8,128)(2,1)} %get-tuple-element.27), channel_id=1, source_target_pairs={{0,8},{8,0},{16,24},{24,16},{1,9},{9,1},{17,25},{25,17},{2,10},{10... | collective-permute-start | bytes 786440 | tf_op jit(solution)/shard_map/ppermute | solution.py:226
  21.9 1.5 %collective-permute-start.3 = (bf16[1,2,16,16,256]{4,3,2,1,0:T(8,128)(2,1)}, bf16[1,2,16,16,256]{4,3,2,1,0:T(8,128)(2,1)S(1)}, u32[]{:S(2)}, u32[]{:S(2)}) collective-permute-start(bf16[1,2,16,16,256]{4,3,2,1,0:T(8,128)(2,1)} %get-tuple-element.28), channel_id=1, source_target_pairs={{0,16},{8,24},{16,0},{24,8},{1,17},{9,25},{17,1},{25,9},{2,18},{10... | collective-permute-start | bytes 786440 | tf_op jit(solution)/shard_map/ppermute | solution.py:226
  23.4 0.0 collective-permute-start.4
  23.5 9.6 %shard_map.77 = (bf16[1,2,16,16,1024]{4,3,2,1,0:T(8,128)(2,1)}, bf16[1,2,16,16,256]{4,3,2,1,0:T(8,128)(2,1)}, bf16[1,2,16,16,256]{4,3,2,1,0:T(8,128)(2,1)}, bf16...) custom-call(s32[4]{0:T(128)} %pad_add_fusion.me_ref, bf16[4,192,192]{2,1,0:T(8,128)(2,1)} %constant.17.clone.a_ref, ...), custom_call_target="tpu_custom_call" | custom-call | flops 6400000000 | bytes 4194304 | tf_op jit(solution)/shard_map/pallas_call | solution.py:156
  33.1 0.0 collective-permute-done.rest_0_
  33.1 0.0 copy-start
  33.1 2.0 %collective-permute-start.5 = (bf16[1,2,16,16,256]{4,3,2,1,0:T(8,128)(2,1)}, bf16[1,2,16,16,256]{4,3,2,1,0:T(8,128)(2,1)S(1)}, u32[]{:S(2)}, u32[]{:S(2)}) collective-permute-start(bf16[1,2,16,16,256]{4,3,2,1,0:T(8,128)(2,1)} %get-tuple-element.31), channel_id=1, source_target_pairs={{0,8},{8,0},{16,24},{24,16},{1,9},{9,1},{17,25},{25,17},{2,10},{10... | collective-permute-start | bytes 786440 | tf_op jit(solution)/shard_map/ppermute | solution.py:226
  35.1 0.0 collective-permute-done.1.rest_1_
  35.1 1.5 %collective-permute-start.6 = (bf16[1,2,16,16,256]{4,3,2,1,0:T(8,128)(2,1)}, bf16[1,2,16,16,256]{4,3,2,1,0:T(8,128)(2,1)S(1)}, u32[]{:S(2)}, u32[]{:S(2)}) collective-permute-start(bf16[1,2,16,16,256]{4,3,2,1,0:T(8,128)(2,1)} %get-tuple-element.32), channel_id=1, source_target_pairs={{0,16},{8,24},{16,0},{24,8},{1,17},{9,25},{17,1},{25,9},{2,18},{10... | collective-permute-start | bytes 786440 | tf_op jit(solution)/shard_map/ppermute | solution.py:226
  36.6 0.0 copy-done
  36.6 0.0 copy-done.1
  36.6 9.8 %shard_map.79 = (bf16[2,4,16,32,1024]{4,3,2,1,0:T(8,128)(2,1)}, bf16[1,2,16,16,256]{4,3,2,1,0:T(8,128)(2,1)}, bf16[1,2,16,16,256]{4,3,2,1,0:T(8,128)(2,1)}, bf16...) custom-call(s32[4]{0:T(128)} %pad_add_fusion.me_ref, bf16[4,192,256]{2,1,0:T(8,128)(2,1)} %constant.18.clone.a_ref, ...), custom_call_target="tpu_custom_call" | custom-call | flops 6400000000 | bytes 4194304 | tf_op jit(solution)/shard_map/pallas_call | solution.py:156
  46.4 0.0 copy-start.16
  46.4 0.0 copy-start.15
  46.4 0.0 copy-start.14
  46.4 9.9 %shard_map.80 = (bf16[2,4,16,32,1024]{4,3,2,1,0:T(8,128)(2,1)}, bf16[1,2,16,16,256]{4,3,2,1,0:T(8,128)(2,1)}, bf16[1,2,16,16,256]{4,3,2,1,0:T(8,128)(2,1)}, bf16...) custom-call(s32[4]{0:T(128)} %pad_add_fusion.me_ref, ...), custom_call_target="tpu_custom_call", output_to_operand_aliasing={{0}: (8, {})} | custom-call | flops 6400000000 | bytes 4194304 | tf_op jit(solution)/shard_map/pallas_call | solution.py:156
  56.3 0.0 collective-permute-done.2.refs_1_
  56.3 0.0 copy-start.2
  56.3 0.0 copy-done.17
  56.3 0.8 collective-permute-start.7
  57.2 0.0 collective-permute-done.3.refs_2_
  57.2 1.5 %collective-permute-start.11 = (bf16[1,2,16,16,256]{4,3,2,1,0:T(8,128)(2,1)}, bf16[1,2,16,16,256]{4,3,2,1,0:T(8,128)(2,1)S(1)}, u32[]{:S(2)}, u32[]{:S(2)}) collective-permute-start(bf16[1,2,16,16,256]{4,3,2,1,0:T(8,128)(2,1)} %get-tuple-element.39), channel_id=1, source_target_pairs={{0,8},{8,0},{16,24},{24,16},{1,9},{9,1},{17,25},{25,17},{2,10},{10... | collective-permute-start | bytes 786440 | tf_op jit(solution)/shard_map/ppermute | solution.py:226
  58.7 0.0 collective-permute-done.4.refs_3_
  58.7 1.2 %collective-permute-start.12 = (bf16[1,2,16,16,256]{4,3,2,1,0:T(8,128)(2,1)}, bf16[1,2,16,16,256]{4,3,2,1,0:T(8,128)(2,1)S(1)}, u32[]{:S(2)}, u32[]{:S(2)}) collective-permute-start(bf16[1,2,16,16,256]{4,3,2,1,0:T(8,128)(2,1)} %get-tuple-element.40), channel_id=1, source_target_pairs={{0,16},{8,24},{16,0},{24,8},{1,17},{9,25},{17,1},{25,9},{2,18},{10... | collective-permute-start | bytes 786440 | tf_op jit(solution)/shard_map/ppermute | solution.py:226
  59.9 0.0 collective-permute-done.5.refs_5_
  59.9 0.8 collective-permute-start.13
  60.7 0.0 collective-permute-done.6.refs_6_
  60.7 0.0 copy-done.16
  60.7 1.6 %collective-permute-start.8 = (bf16[1,2,16,16,256]{4,3,2,1,0:T(8,128)(2,1)S(1)}, bf16[1,2,16,16,256]{4,3,2,1,0:T(8,128)(2,1)S(1)}, u32[]{:S(2)}, u32[]{:S(2)}) collective-permute-start(bf16[1,2,16,16,256]{4,3,2,1,0:T(8,128)(2,1)S(1)} %copy-done.16), channel_id=1, source_target_pairs={{0,8},{8,0},{16,24},{24,16},{1,9},{9,1},{17,25},{25,17},{2,10},{10... | collective-permute-start | bytes 786440 | tf_op jit(solution)/shard_map/ppermute | solution.py:226
  62.2 4.4 %collective-permute-done.7.refs_7_ = bf16[1,2,16,16,256]{4,3,2,1,0:T(8,128)(2,1)S(1)} collective-permute-done((bf16[1,2,16,16,256]{4,3,2,1,0:T(8,128)(2,1)S(1)}, bf16[1,2,16,16,256]{4,3,2,1,0:T(8,128)(2,1)S(1)}, u32[]{:S(2)}, u32[]{:S(2)}) %collective-permute-start.7) | collective-permute-done | bytes 262176 | tf_op jit(solution)/shard_map/ppermute | solution.py:226
  66.7 0.0 copy-done.15
  66.7 0.8 collective-permute-start.9
  67.4 4.1 %collective-permute-done.11.refs_13_ = bf16[1,2,16,16,256]{4,3,2,1,0:T(8,128)(2,1)S(1)} collective-permute-done((bf16[1,2,16,16,256]{4,3,2,1,0:T(8,128)(2,1)}, bf16[1,2,16,16,256]{4,3,2,1,0:T(8,128)(2,1)S(1)}, u32[]{:S(2)}, u32[]{:S(2)}) %collective-permute-start.11) | collective-permute-done | bytes 262176 | tf_op jit(solution)/shard_map/ppermute | solution.py:226
  71.5 0.0 copy-done.14
  71.5 1.2 %collective-permute-start.10 = (bf16[1,2,16,16,256]{4,3,2,1,0:T(8,128)(2,1)S(1)}, bf16[1,2,16,16,256]{4,3,2,1,0:T(8,128)(2,1)S(1)}, u32[]{:S(2)}, u32[]{:S(2)}) collective-permute-start(bf16[1,2,16,16,256]{4,3,2,1,0:T(8,128)(2,1)S(1)} %copy-done.14), channel_id=1, source_target_pairs={{0,24},{8,16},{16,8},{24,0},{1,25},{9,17},{17,9},{25,1},{2,26},{10... | collective-permute-start | bytes 786440 | tf_op jit(solution)/shard_map/ppermute | solution.py:226
  72.8 21.4 %shard_map.81 = bf16[2,4,16,32,1024]{4,3,2,1,0:T(8,128)(2,1)} custom-call(s32[4]{0:T(128)} %pad_add_fusion.me_ref, bf16[4,384,256]{2,1,0:T(8,128)(2,1)} %constant.19.clone.a_ref, bf16[2,4,16,32,1024]{4,3,2,1,0:T(8,128)(2,1)} %above.9, bf16[2,4,16,32,1024]{4,3,2,1,0:T(8,128)(2,1)} %above.9, ...), custom_call_target="tpu_custom_call", output_to_operand_aliasing={{}: (7, {})} | custom-call | flops 25600000000 | bytes 16777216 | tf_op jit(solution)/shard_map/pallas_call | solution.py:156
  94.2 0.0 copy-done.2
  94.2 0.0 copy-done.3
  94.2 0.0 copy-done.4
  94.2 0.0 copy-done.5
  94.2 0.0 copy-done.6
  94.2 0.0 copy-done.7
  94.3 0.0 collective-permute-done.12.refs_14_
  94.3 0.0 collective-permute-done.13.refs_15_
  94.3 0.0 copy-start.10
  94.3 0.0 collective-permute-done.8.refs_9_
  94.3 0.0 collective-permute-done.9.refs_10_
  94.3 0.0 collective-permute-done.10.refs_11_
  94.4 0.0 copy-start.13
  94.4 0.6 copy-done.9
  95.0 0.1 copy-done.10
  95.1 0.1 copy-done.11
  95.2 0.1 copy-done.12
  95.3 0.1 copy-done.13
  95.4 4.5 %shard_map.82 = f32[16,32,256]{2,1,0:T(8,128)} custom-call(bf16[1,2,16,16,256]{4,3,2,1,0:T(8,128)(2,1)} %get-tuple-element.26.refs_0_, bf16[1,2,16,16,256]{4,3,2,1,0:T(8,128)(2,1)} %copy-done.2, bf16[1,2,16,16,256]{4,3,2,1,0:T(8,128)(2,1)} %copy-done.3, bf16[1,2,16,16,256]{4,3,2,1,0:T(8,128)(2,1)} %copy-done.4, ...), custom_call_target="tpu_custom_call" | custom-call | flops 100000000 | bytes 5242880 | tf_op jit(solution)/shard_map/pallas_call | solution.py:197
  (12 shorter events, 0.0 us)
Async XLA Ops:
  4.5 28.6 %collective-permute-start = (bf16[2,4,32,1024]{3,2,1,0:T(8,128)(2,1)S(1)}, bf16[2,4,32,1024]{3,2,1,0:T(8,128)(2,1)S(1)}, u32[]{:S(2)}, u32[]{:S(2)}) collective-permute-start(bf16[2,4,32,1024]{3,2,1,0:T(8,128)(2,1)S(1)} %copy.11), channel_id=1, source_target_pairs={{0,1},{1,2},{2,3},{3,4},{4,5},{5,6},{6,7},{7,0},{8,9},{9,10},{10,1... | collective-permute-start | bytes 1572872 | tf_op jit(solution)/shard_map/ppermute | solution.py:218
  5.6 29.5 %collective-permute-start.1 = (bf16[2,4,32,1024]{3,2,1,0:T(8,128)(2,1)S(1)}, bf16[2,4,32,1024]{3,2,1,0:T(8,128)(2,1)S(1)}, u32[]{:S(2)}, u32[]{:S(2)}) collective-permute-start(bf16[2,4,32,1024]{3,2,1,0:T(8,128)(2,1)S(1)} %copy.13), channel_id=1, source_target_pairs={{1,0},{2,1},{3,2},{4,3},{5,4},{6,5},{7,6},{0,7},{9,8},{10,9},{11,1... | collective-permute-start | bytes 1572872 | tf_op jit(solution)/shard_map/ppermute | solution.py:219
  19.9 36.4 %collective-permute-start.2 = (bf16[1,2,16,16,256]{4,3,2,1,0:T(8,128)(2,1)}, bf16[1,2,16,16,256]{4,3,2,1,0:T(8,128)(2,1)S(1)}, u32[]{:S(2)}, u32[]{:S(2)}) collective-permute-start(bf16[1,2,16,16,256]{4,3,2,1,0:T(8,128)(2,1)} %get-tuple-element.27), channel_id=1, source_target_pairs={{0,8},{8,0},{16,24},{24,16},{1,9},{9,1},{17,25},{25,17},{2,10},{10... | collective-permute-start | bytes 786440 | tf_op jit(solution)/shard_map/ppermute | solution.py:226
  21.9 35.3 %collective-permute-start.3 = (bf16[1,2,16,16,256]{4,3,2,1,0:T(8,128)(2,1)}, bf16[1,2,16,16,256]{4,3,2,1,0:T(8,128)(2,1)S(1)}, u32[]{:S(2)}, u32[]{:S(2)}) collective-permute-start(bf16[1,2,16,16,256]{4,3,2,1,0:T(8,128)(2,1)} %get-tuple-element.28), channel_id=1, source_target_pairs={{0,16},{8,24},{16,0},{24,8},{1,17},{9,25},{17,1},{25,9},{2,18},{10... | collective-permute-start | bytes 786440 | tf_op jit(solution)/shard_map/ppermute | solution.py:226
  23.4 35.2 %collective-permute-start.4 = (bf16[1,2,16,16,256]{4,3,2,1,0:T(8,128)(2,1)}, bf16[1,2,16,16,256]{4,3,2,1,0:T(8,128)(2,1)S(1)}, u32[]{:S(2)}, u32[]{:S(2)}) collective-permute-start(bf16[1,2,16,16,256]{4,3,2,1,0:T(8,128)(2,1)} %get-tuple-element.29), channel_id=1, source_target_pairs={{0,24},{8,16},{16,8},{24,0},{1,25},{9,17},{17,9},{25,1},{2,26},{10... | collective-permute-start | bytes 786440 | tf_op jit(solution)/shard_map/ppermute | solution.py:226
  33.1 3.5 %copy-start = (bf16[2,4,32,1024]{3,2,1,0:T(8,128)(2,1)}, bf16[2,4,32,1024]{3,2,1,0:T(8,128)(2,1)S(1)}, u32[]{:S(2)}) copy-start(bf16[2,4,32,1024]{3,2,1,0:T(8,128)(2,1)S(1)} %collective-permute-done.rest_0_) | copy-start | bytes 1572868
  33.1 26.8 %collective-permute-start.5 = (bf16[1,2,16,16,256]{4,3,2,1,0:T(8,128)(2,1)}, bf16[1,2,16,16,256]{4,3,2,1,0:T(8,128)(2,1)S(1)}, u32[]{:S(2)}, u32[]{:S(2)}) collective-permute-start(bf16[1,2,16,16,256]{4,3,2,1,0:T(8,128)(2,1)} %get-tuple-element.31), channel_id=1, source_target_pairs={{0,8},{8,0},{16,24},{24,16},{1,9},{9,1},{17,25},{25,17},{2,10},{10... | collective-permute-start | bytes 786440 | tf_op jit(solution)/shard_map/ppermute | solution.py:226
  35.1 1.5 %copy-start.1 = (bf16[2,4,32,1024]{3,2,1,0:T(8,128)(2,1)}, bf16[2,4,32,1024]{3,2,1,0:T(8,128)(2,1)S(1)}, u32[]{:S(2)}) copy-start(bf16[2,4,32,1024]{3,2,1,0:T(8,128)(2,1)S(1)} %collective-permute-done.1.rest_1_) | copy-start | bytes 1572868
  35.1 25.6 %collective-permute-start.6 = (bf16[1,2,16,16,256]{4,3,2,1,0:T(8,128)(2,1)}, bf16[1,2,16,16,256]{4,3,2,1,0:T(8,128)(2,1)S(1)}, u32[]{:S(2)}, u32[]{:S(2)}) collective-permute-start(bf16[1,2,16,16,256]{4,3,2,1,0:T(8,128)(2,1)} %get-tuple-element.32), channel_id=1, source_target_pairs={{0,16},{8,24},{16,0},{24,8},{1,17},{9,25},{17,1},{25,9},{2,18},{10... | collective-permute-start | bytes 786440 | tf_op jit(solution)/shard_map/ppermute | solution.py:226
  46.4 10.0 %copy-start.17 = (bf16[1,2,16,16,256]{4,3,2,1,0:T(8,128)(2,1)S(1)}, bf16[1,2,16,16,256]{4,3,2,1,0:T(8,128)(2,1)}, u32[]{:S(2)}) copy-start(bf16[1,2,16,16,256]{4,3,2,1,0:T(8,128)(2,1)} %get-tuple-element.33) | copy-start | bytes 786436
  46.4 14.3 %copy-start.16 = (bf16[1,2,16,16,256]{4,3,2,1,0:T(8,128)(2,1)S(1)}, bf16[1,2,16,16,256]{4,3,2,1,0:T(8,128)(2,1)}, u32[]{:S(2)}) copy-start(bf16[1,2,16,16,256]{4,3,2,1,0:T(8,128)(2,1)} %get-tuple-element.35) | copy-start | bytes 786436
  46.4 20.3 %copy-start.15 = (bf16[1,2,16,16,256]{4,3,2,1,0:T(8,128)(2,1)S(1)}, bf16[1,2,16,16,256]{4,3,2,1,0:T(8,128)(2,1)}, u32[]{:S(2)}) copy-start(bf16[1,2,16,16,256]{4,3,2,1,0:T(8,128)(2,1)} %get-tuple-element.36) | copy-start | bytes 786436
  46.4 25.1 %copy-start.14 = (bf16[1,2,16,16,256]{4,3,2,1,0:T(8,128)(2,1)S(1)}, bf16[1,2,16,16,256]{4,3,2,1,0:T(8,128)(2,1)}, u32[]{:S(2)}) copy-start(bf16[1,2,16,16,256]{4,3,2,1,0:T(8,128)(2,1)} %get-tuple-element.37) | copy-start | bytes 786436
  56.3 37.9 %copy-start.2 = (bf16[1,2,16,16,256]{4,3,2,1,0:T(8,128)(2,1)}, bf16[1,2,16,16,256]{4,3,2,1,0:T(8,128)(2,1)S(1)}, u32[]{:S(2)}) copy-start(bf16[1,2,16,16,256]{4,3,2,1,0:T(8,128)(2,1)S(1)} %collective-permute-done.2.refs_1_) | copy-start | bytes 786436
  56.3 10.3 %collective-permute-start.7 = (bf16[1,2,16,16,256]{4,3,2,1,0:T(8,128)(2,1)S(1)}, bf16[1,2,16,16,256]{4,3,2,1,0:T(8,128)(2,1)S(1)}, u32[]{:S(2)}, u32[]{:S(2)}) collective-permute-start(bf16[1,2,16,16,256]{4,3,2,1,0:T(8,128)(2,1)S(1)} %copy-done.17), channel_id=1, source_target_pairs={{0,24},{8,16},{16,8},{24,0},{1,25},{9,17},{17,9},{25,1},{2,26},{10... | collective-permute-start | bytes 786440 | tf_op jit(solution)/shard_map/ppermute | solution.py:226
  57.2 37.0 %copy-start.3 = (bf16[1,2,16,16,256]{4,3,2,1,0:T(8,128)(2,1)}, bf16[1,2,16,16,256]{4,3,2,1,0:T(8,128)(2,1)S(1)}, u32[]{:S(2)}) copy-start(bf16[1,2,16,16,256]{4,3,2,1,0:T(8,128)(2,1)S(1)} %collective-permute-done.3.refs_2_) | copy-start | bytes 786436
  57.2 14.4 %collective-permute-start.11 = (bf16[1,2,16,16,256]{4,3,2,1,0:T(8,128)(2,1)}, bf16[1,2,16,16,256]{4,3,2,1,0:T(8,128)(2,1)S(1)}, u32[]{:S(2)}, u32[]{:S(2)}) collective-permute-start(bf16[1,2,16,16,256]{4,3,2,1,0:T(8,128)(2,1)} %get-tuple-element.39), channel_id=1, source_target_pairs={{0,8},{8,0},{16,24},{24,16},{1,9},{9,1},{17,25},{25,17},{2,10},{10... | collective-permute-start | bytes 786440 | tf_op jit(solution)/shard_map/ppermute | solution.py:226
  58.7 35.5 %copy-start.4 = (bf16[1,2,16,16,256]{4,3,2,1,0:T(8,128)(2,1)}, bf16[1,2,16,16,256]{4,3,2,1,0:T(8,128)(2,1)S(1)}, u32[]{:S(2)}) copy-start(bf16[1,2,16,16,256]{4,3,2,1,0:T(8,128)(2,1)S(1)} %collective-permute-done.4.refs_3_) | copy-start | bytes 786436
  58.7 35.6 %collective-permute-start.12 = (bf16[1,2,16,16,256]{4,3,2,1,0:T(8,128)(2,1)}, bf16[1,2,16,16,256]{4,3,2,1,0:T(8,128)(2,1)S(1)}, u32[]{:S(2)}, u32[]{:S(2)}) collective-permute-start(bf16[1,2,16,16,256]{4,3,2,1,0:T(8,128)(2,1)} %get-tuple-element.40), channel_id=1, source_target_pairs={{0,16},{8,24},{16,0},{24,8},{1,17},{9,25},{17,1},{25,9},{2,18},{10... | collective-permute-start | bytes 786440 | tf_op jit(solution)/shard_map/ppermute | solution.py:226
  59.9 34.3 %copy-start.5 = (bf16[1,2,16,16,256]{4,3,2,1,0:T(8,128)(2,1)}, bf16[1,2,16,16,256]{4,3,2,1,0:T(8,128)(2,1)S(1)}, u32[]{:S(2)}) copy-start(bf16[1,2,16,16,256]{4,3,2,1,0:T(8,128)(2,1)S(1)} %collective-permute-done.5.refs_5_) | copy-start | bytes 786436
  59.9 34.4 %collective-permute-start.13 = (bf16[1,2,16,16,256]{4,3,2,1,0:T(8,128)(2,1)}, bf16[1,2,16,16,256]{4,3,2,1,0:T(8,128)(2,1)S(1)}, u32[]{:S(2)}, u32[]{:S(2)}) collective-permute-start(bf16[1,2,16,16,256]{4,3,2,1,0:T(8,128)(2,1)} %get-tuple-element.41), channel_id=1, source_target_pairs={{0,24},{8,16},{16,8},{24,0},{1,25},{9,17},{17,9},{25,1},{2,26},{10... | collective-permute-start | bytes 786440 | tf_op jit(solution)/shard_map/ppermute | solution.py:226
  60.7 33.6 %copy-start.6 = (bf16[1,2,16,16,256]{4,3,2,1,0:T(8,128)(2,1)}, bf16[1,2,16,16,256]{4,3,2,1,0:T(8,128)(2,1)S(1)}, u32[]{:S(2)}) copy-start(bf16[1,2,16,16,256]{4,3,2,1,0:T(8,128)(2,1)S(1)} %collective-permute-done.6.refs_6_) | copy-start | bytes 786436
  60.7 33.6 %collective-permute-start.8 = (bf16[1,2,16,16,256]{4,3,2,1,0:T(8,128)(2,1)S(1)}, bf16[1,2,16,16,256]{4,3,2,1,0:T(8,128)(2,1)S(1)}, u32[]{:S(2)}, u32[]{:S(2)}) collective-permute-start(bf16[1,2,16,16,256]{4,3,2,1,0:T(8,128)(2,1)S(1)} %copy-done.16), channel_id=1, source_target_pairs={{0,8},{8,0},{16,24},{24,16},{1,9},{9,1},{17,25},{25,17},{2,10},{10... | collective-permute-start | bytes 786440 | tf_op jit(solution)/shard_map/ppermute | solution.py:226
  66.7 27.6 %copy-start.7 = (bf16[1,2,16,16,256]{4,3,2,1,0:T(8,128)(2,1)}, bf16[1,2,16,16,256]{4,3,2,1,0:T(8,128)(2,1)S(1)}, u32[]{:S(2)}) copy-start(bf16[1,2,16,16,256]{4,3,2,1,0:T(8,128)(2,1)S(1)} %collective-permute-done.7.refs_7_) | copy-start | bytes 786436
  66.7 27.7 %collective-permute-start.9 = (bf16[1,2,16,16,256]{4,3,2,1,0:T(8,128)(2,1)S(1)}, bf16[1,2,16,16,256]{4,3,2,1,0:T(8,128)(2,1)S(1)}, u32[]{:S(2)}, u32[]{:S(2)}) collective-permute-start(bf16[1,2,16,16,256]{4,3,2,1,0:T(8,128)(2,1)S(1)} %copy-done.15), channel_id=1, source_target_pairs={{0,16},{8,24},{16,0},{24,8},{1,17},{9,25},{17,1},{25,9},{2,18},{10... | collective-permute-start | bytes 786440 | tf_op jit(solution)/shard_map/ppermute | solution.py:226
  71.5 22.7 %copy-start.8 = (bf16[1,2,16,16,256]{4,3,2,1,0:T(8,128)(2,1)}, bf16[1,2,16,16,256]{4,3,2,1,0:T(8,128)(2,1)S(1)}, u32[]{:S(2)}) copy-start(bf16[1,2,16,16,256]{4,3,2,1,0:T(8,128)(2,1)S(1)} %collective-permute-done.11.refs_13_) | copy-start | bytes 786436
  71.5 22.8 %collective-permute-start.10 = (bf16[1,2,16,16,256]{4,3,2,1,0:T(8,128)(2,1)S(1)}, bf16[1,2,16,16,256]{4,3,2,1,0:T(8,128)(2,1)S(1)}, u32[]{:S(2)}, u32[]{:S(2)}) collective-permute-start(bf16[1,2,16,16,256]{4,3,2,1,0:T(8,128)(2,1)S(1)} %copy-done.14), channel_id=1, source_target_pairs={{0,24},{8,16},{16,8},{24,0},{1,25},{9,17},{17,9},{25,1},{2,26},{10... | collective-permute-start | bytes 786440 | tf_op jit(solution)/shard_map/ppermute | solution.py:226
  94.3 0.7 copy-start.9
  94.3 0.8 copy-start.10
  94.3 0.9 copy-start.11
  94.3 1.0 copy-start.12
  94.4 1.0 copy-start.13

commit v3 on v2

--- a/solution.py
+++ b/solution.py
@@ -13,7 +13,8 @@
 var_floor = 0.25
 depth = 4
 edge = 8
-vmem = 56 * 2**20
+wide = 256
+vmem = 50 * 2**20
 
 
 def stencil_matrix(levels, rows, spans, halos):
@@ -36,18 +37,31 @@
                     a[c, 0, z, n, column(c, z, x + d)] += coef
                 a[c, 2, z, n, column(c, z, x + 1)] += 1
                 a[c, 2, z, n, column(c, z, x - 1)] += 1
-                a[c, 2, z, n, column(c, z, x)] -= 6
+                a[c, 2, z, n, column(c, z, x)] += 44
                 for d in (1, -1):
                     if 0 <= c * depth + z + d < levels:
-                        a[c, 1, z, n, (z + 1 + d) * rows + x] += d
+                        a[c, 1, z, n, (z + 1 + d) * rows + x] += 6 * d
                         a[c, 2, z, n, (z + 1 + d) * rows + x] += 1
     return jnp.asarray(a.reshape(chunks, 3 * depth * len(xs), -1).astype(jnp.bfloat16))
 
 
-def step_kernel(kind, first, parts, spans, me_ref, a_ref, main, below, above, *rest):
+def column_matrix():
+    b = np.zeros((2 * wide, 2 * wide), np.float32)
+    for n in range(wide):
+        for d, coef in ((1, 8), (-1, -8), (2, -1), (-2, 1)):
+            y = n + d
+            row = y + wide + 128 if y < 0 else y if y < wide else y + 128
+            b[row, n] += coef
+            if d * d == 1:
+                b[row, wide + n] += 1
+    return jnp.asarray(b.astype(jnp.bfloat16))
+
+
+def step_kernel(kind, first, parts, spans, me_ref, a_ref, b_ref, main, below, above, *rest):
     rest = list(rest)
     halos = [rest.pop(0), rest.pop(0)] if kind != "mid" else []
     mid = rest.pop(0) if kind == "edge" else None
+    resy = rest.pop()
     res = rest.pop()
     held = rest.pop() if kind == "edge" else None
     if kind == "edge":
@@ -61,50 +75,51 @@
     total = depth * count
     for k in range(2):
         f = first + k
-        w = jnp.concatenate(
-            [below[0, k, 0]] + [main[0, f, z] for z in range(depth)] + [above[0, k, 0]] + [h[0, k] for h in halos],
-            axis=0,
-        )
+        m = jnp.concatenate([main[0, f, z] for z in range(depth)], axis=0)
+        w = jnp.concatenate([below[0, k, 0], m, above[0, k, 0]] + [h[0, k] for h in halos], axis=0)
         res[...] = jnp.dot(a_ref[0], w, preferred_element_type=jnp.float32)
+        for j in range(cols // wide):
+            lo = (j * wide - 128) % cols
+            hi = (j * wide + wide) % cols
+            block = jnp.concatenate([m[:, j * wide : (j + 1) * wide], m[:, lo : lo + 128], m[:, hi : hi + 128]], axis=1)
+            resy[:, 2 * j * wide : 2 * (j + 1) * wide] = jnp.dot(block, b_ref[...], preferred_element_type=jnp.float32)
 
         def level(z, carry):
-            def get(g, start, stop):
-                if kind == "rest":
-                    return main[0, g, z, start:stop, :].astype(jnp.float32)
-                return main[0, g, z].astype(jnp.float32)[start:stop]
-
-            news = []
-            at = 0
-            for start, stop in spans:
-                base = pl.multiple_of(z * count, 16) + at
-                at += stop - start
-                u, v, wv = get(0, start, stop), get(1, start, stop), get(2, start, stop)
-                cen = get(f, start, stop)
-                size = stop - start
-                dx = res[pl.ds(pl.multiple_of(base, 8), size), :]
-                dz = res[pl.ds(pl.multiple_of(total + base, 8), size), :]
-                lap = res[pl.ds(pl.multiple_of(2 * total + base, 8), size), :]
-                yp = pltpu.roll(cen, cols - 1, 1)
-                ym = pltpu.roll(cen, 1, 1)
-                yp2 = pltpu.roll(cen, cols - 2, 1)
-                ym2 = pltpu.roll(cen, 2, 1)
-                dy = 8.0 * (yp - ym) - (yp2 - ym2)
-                lap = lap + (yp + ym)
-                s = time_step / 12.0
-                new = cen + (time_step * viscosity) * lap - (s * (u * dx + v * dy) + (0.5 * time_step) * (wv * dz))
-                if f == 2:
-                    new = new + time_step * get(3, start, stop)
-                elif f == 3:
-                    new = new - time_step * wv
-                if kind == "rest":
-                    out[0, k, z, start:stop, :] = new.astype(jnp.bfloat16)
-                news.append(new)
-            if kind == "mid":
-                out[0, k, z] = jnp.concatenate(news, axis=0).astype(jnp.bfloat16)
-            elif kind == "edge":
-                held[z] = jnp.concatenate(news, axis=0).astype(jnp.bfloat16)
-                inner = mid[0, k, z].astype(jnp.float32)
-                out[0, k, z] = jnp.concatenate([news[0], inner, news[1]], axis=0).astype(jnp.bfloat16)
+            for j in range(cols // wide):
+                seg = slice(j * wide, (j + 1) * wide)
+
+                def get(g, start, stop):
+                    if kind == "rest":
+                        return main[0, g, z, start:stop, seg].astype(jnp.float32)
+                    return main[0, g, z, :, seg].astype(jnp.float32)[start:stop]
+
+                news = []
+                at = 0
+                for start, stop in spans:
+                    base = pl.multiple_of(z * count + at, 8)
+                    row = pl.multiple_of(z * rows + start, 8)
+                    size = stop - start
+                    at += size
+                    u, v, wv = get(0, start, stop), get(1, start, stop), get(2, start, stop)
+                    dx = res[pl.ds(base, size), seg]
+                    dz = res[pl.ds(pl.multiple_of(total + base, 8), size), seg]
+                    lap = res[pl.ds(pl.multiple_of(2 * total + base, 8), size), seg]
+                    dy = resy[pl.ds(row, size), 2 * j * wide : (2 * j + 1) * wide]
+                    lap = lap + resy[pl.ds(row, size), (2 * j + 1) * wide : (2 * j + 2) * wide]
+                    new = (time_step * viscosity) * lap - (time_step / 12.0) * (u * dx + v * dy + wv * dz)
+                    if f == 2:
+                        new = new + time_step * get(3, start, stop)
+                    elif f == 3:
+                        new = new - time_step * wv
+                    if kind == "rest":
+                        out[0, k, z, start:stop, seg] = new.astype(jnp.bfloat16)
+                    news.append(new)
+                if kind == "mid":
+                    out[0, k, z, :, seg] = jnp.concatenate(news, axis=0).astype(jnp.bfloat16)
+                elif kind == "edge":
+                    held[z, :, seg] = jnp.concatenate(news, axis=0).astype(jnp.bfloat16)
+                    inner = mid[0, k, z, :, seg].astype(jnp.float32)
+                    out[0, k, z, :, seg] = jnp.concatenate([news[0], inner, news[1]], axis=0).astype(jnp.bfloat16)
             return carry
 
         lax.fori_loop(0, depth, level, 0)
@@ -124,11 +139,12 @@
     sds = jax.ShapeDtypeStruct
     in_specs = [
         pl.BlockSpec((1,) + a.shape[1:], lambda m, c, me: (c, 0, 0)),
+        pl.BlockSpec((2 * wide, 2 * wide), lambda m, c, me: (0, 0)),
         pl.BlockSpec((1, 4, depth, rows, cols), lambda m, c, me: (m + m0, 0, c, 0, 0)),
         pl.BlockSpec((1, 2, 1, rows, cols), lambda m, c, me: (m + m0, fb, jnp.maximum(c * depth - 1, 0), 0, 0)),
         pl.BlockSpec((1, 2, 1, rows, cols), lambda m, c, me: (m + m0, fb, jnp.minimum(c * depth + depth, levels - 1), 0, 0)),
     ]
-    args = [order, a, state, state, state]
+    args = [order, a, column_matrix(), state, state, state]
     if kind != "mid":
         in_specs += [pl.BlockSpec((1, 2, 2 * levels, cols), lambda m, c, me: (m + m0, fb, 0, 0))] * 2
         args += [lo, hi]
@@ -149,7 +165,10 @@
     if kind != "rest":
         out_shape += [sds((m1 - m0, 2, levels, count, cols // parts), state.dtype)] * parts
         out_specs += [pl.BlockSpec((1, 2, depth, count, cols // parts), lambda m, c, me: (m, 0, c, 0, 0))] * parts
-    scratch = [pltpu.VMEM((3 * depth * count, cols), jnp.float32)]
+    scratch = [
+        pltpu.VMEM((3 * depth * count, cols), jnp.float32),
+        pltpu.VMEM((depth * rows, 2 * cols), jnp.float32),
+    ]
     if kind == "edge":
         scratch.insert(0, pltpu.VMEM((depth, count, cols), jnp.bfloat16))
     share = (m1 - m0) * count
@@ -229,16 +248,12 @@
     inner = ((edge, rows - edge),)
     outer = ((0, edge), (rows - edge, rows))
     halves = tuple((x, x + 16) for x in range(0, rows, 16))
-    middles, mids, edges = [], [], []
-    for m in range(m_):
-        middle, *blocks = run_step("mid", 2, (m, m + 1), parts, inner, order, state)
-        middles.append(middle)
-        mids += exchange(blocks)
-    stepped = None
-    for m in range(m_):
-        stepped, *blocks = run_step("edge", 2, (m, m + 1), parts, outer, order, state, lo, hi, middles[m], stepped)
-        edges += exchange(blocks)
-    (stepped,) = run_step("rest", 0, (0, m_), parts, halves, order, state, lo, hi, None, stepped)
+    both = (0, m_)
+    middle, *blocks = run_step("mid", 2, both, parts, inner, order, state)
+    mids = exchange(blocks)
+    stepped, *blocks = run_step("edge", 2, both, parts, outer, order, state, lo, hi, middle)
+    edges = exchange(blocks)
+    (stepped,) = run_step("rest", 0, both, parts, halves, order, state, lo, hi, None, stepped)
     return stepped, run_correlate(float(m_ * parts), mids, edges)
 
 

time: 100 us -> 79 us (0.79)
  Pallas kernels: 64.8 us -> 51 us
  starting transfers between devices: 19.6 us -> 11.6 us
  local copies, waits for them, and re-layouts: 5.46 us -> 7.27 us
    pallas_call x5 -> x3, Pallas kernels: 60.3 us -> 47 us  [run_step(): pl.pallas_call(functools.partial(step_kernel, kind, first, parts, spans),...]
    ppermute x12 -> x6, starting transfers between devices: 14.9 us -> 6.99 us  [exchange(): lax.ppermute(blocks[k], 'member', [(i, partner(i, k, parts)) for i in ran...]
    unnamed x36 -> x12, local copies, waits for them, and re-layouts: 1.04 us -> 2.85 us
    ppermute x12 -> x6, waiting for transfers between devices: 8.54 us -> 8.05 us  [exchange(): lax.ppermute(blocks[k], 'member', [(i, partner(i, k, parts)) for i in ran...]
  transfers between devices with their start and end apart: 14 -> 8, of which waited for: 2 -> 1; matrix products, arithmetic and copies ran while one was open for 1% -> 1% of each run, Pallas kernels for 60% -> 60%
where the time goes in v3:
time: 79 us; the launch traced here: 78.7 us
  Pallas kernels  51 us (65%)
  starting transfers between devices  11.6 us (15%)
  waiting for transfers between devices  8.05 us (10%)
  local copies, waits for them, and re-layouts  7.27 us (9%)
    pallas_call x3, Pallas kernels, run_step(): pl.pallas_call(functools.partial(step_kernel, kind, first, parts, spans),...  47 us
    ppermute x6, waiting for transfers between devices, exchange(): lax.ppermute(blocks[k], 'member', [(i, partner(i, k, parts)) for i in ran...  8.05 us
    ppermute x6, starting transfers between devices, exchange(): lax.ppermute(blocks[k], 'member', [(i, partner(i, k, parts)) for i in ran...  6.99 us
    ppermute x1, starting transfers between devices, on_device(): lax.ppermute(head, 'space', [((i + 1) % count, i) for i in range(count)])  4.11 us
    pallas_call x1, Pallas kernels, run_correlate(): pl.pallas_call(functools.partial(correlate_kernel, count), out_shape=jax....  3.94 us
    slice x2, local copies, waits for them, and re-layouts, on_device(): head = state[:, :, :, :2, :].reshape(m_, 4, 2 * levels, cols)  3.7 us
    unnamed x12, local copies, waits for them, and re-layouts  2.85 us
  transfers between devices with their start and end apart: 8, of which 1 were waited for; matrix products, arithmetic and copies ran while one was open for 1% of the time, Pallas kernels for 60%

profile of v3, /device:TPU:0, one launch (start us, length us, event | category | flops | bytes accessed | tf_op | source)
XLA Modules:
  0.0 78.7 jit_solution(17638214360246945136)
XLA Ops:
  0.6 3.3 %fusion = (bf16[2,4,16,2,1024]{4,3,2,1,0:T(2,128)(2,1)S(1)}, bf16[2,4,16,2,1024]{4,3,2,1,0:T(2,128)(2,1)S(1)}) fusion(bf16[2,4,16,32,1024]{4,3,2,1,0:T(8,128)(2,1)} %above.5), kind=kLoop, calls=%fused_computation.1 | loop fusion | bytes 2097152 | tf_op jit(solution)/shard_map/slice | solution.py:235
  3.9 0.4 copy.10
  4.3 0.2 copy.11
  4.5 0.5 collective-permute-start
  5.0 0.4 copy.12
  5.4 0.2 copy.13
  5.6 4.1 %collective-permute-start.1 = (bf16[2,4,32,1024]{3,2,1,0:T(8,128)(2,1)S(1)}, bf16[2,4,32,1024]{3,2,1,0:T(8,128)(2,1)S(1)}, u32[]{:S(2)}, u32[]{:S(2)}) collective-permute-start(bf16[2,4,32,1024]{3,2,1,0:T(8,128)(2,1)S(1)} %copy.13), channel_id=1, source_target_pairs={{1,0},{2,1},{3,2},{4,3},{5,4},{6,5},{7,6},{0,7},{9,8},{10,9},{11,1... | collective-permute-start | bytes 1572872 | tf_op jit(solution)/shard_map/ppermute | solution.py:238
  9.7 0.1 pad_add_fusion.me_ref
  9.8 0.0 copy-start.1
  9.8 1.0 %copy-done.1 = bf16[512,512]{1,0:T(8,128)(2,1)S(1)} copy-done((bf16[512,512]{1,0:T(8,128)(2,1)S(1)}, bf16[512,512]{1,0:T(8,128)(2,1)}, u32[]{:S(2)}) %copy-start.1) | copy-done | bytes 524312
  10.8 0.0 copy-start.4
  10.8 1.0 %copy-done.4 = bf16[4,192,192]{2,1,0:T(8,128)(2,1)S(1)} copy-done((bf16[4,192,192]{2,1,0:T(8,128)(2,1)S(1)}, bf16[4,192,192]{2,1,0:T(8,128)(2,1)}, u32[]{:S(2)}) %copy-start.4) | copy-done | bytes 294936
  11.8 0.0 copy-start.2
  11.8 0.0 copy-start.3
  11.8 14.7 %shard_map.86 = (bf16[2,2,16,16,1024]{4,3,2,1,0:T(8,128)(2,1)}, bf16[2,2,16,16,256]{4,3,2,1,0:T(8,128)(2,1)S(1)}, bf16[2,2,16,16,256]{4,3,2,1,0:T(8,128)(2,1)S(1...) custom-call(s32[4]{0:T(128)S(1)} %pad_add_fusion.me_ref, bf16[4,192,192]{2,1,0:T(8,128)(2,1)S(1)} %copy-done.4, ...), custom_call_target="tpu_custom_call" | custom-call | flops 12800000000 | bytes 8388608 | tf_op jit(solution)/shard_map/pallas_call | solution.py:175
  26.6 2.0 %collective-permute-start.2 = (bf16[2,2,16,16,256]{4,3,2,1,0:T(8,128)(2,1)S(1)}, bf16[2,2,16,16,256]{4,3,2,1,0:T(8,128)(2,1)S(1)}, u32[]{:S(2)}, u32[]{:S(2)}) collective-permute-start(bf16[2,2,16,16,256]{4,3,2,1,0:T(8,128)(2,1)S(1)} %get-tuple-element.15), channel_id=1, source_target_pairs={{0,8},{8,0},{16,24},{24,16},{1,9},{9,1},{17,25},{25,17},{2,10},{10... | collective-permute-start | bytes 1572872 | tf_op jit(solution)/shard_map/ppermute | solution.py:245
  28.5 1.5 %collective-permute-start.3 = (bf16[2,2,16,16,256]{4,3,2,1,0:T(8,128)(2,1)S(1)}, bf16[2,2,16,16,256]{4,3,2,1,0:T(8,128)(2,1)S(1)}, u32[]{:S(2)}, u32[]{:S(2)}) collective-permute-start(bf16[2,2,16,16,256]{4,3,2,1,0:T(8,128)(2,1)S(1)} %get-tuple-element.16), channel_id=1, source_target_pairs={{0,16},{8,24},{16,0},{24,8},{1,17},{9,25},{17,1},{25,9},{2,18},{10... | collective-permute-start | bytes 1572872 | tf_op jit(solution)/shard_map/ppermute | solution.py:245
  30.0 0.0 collective-permute-start.4
  30.0 0.0 collective-permute-done.rest_0_
  30.0 0.0 collective-permute-done.1.rest_1_
  30.0 0.0 copy-done.2
  30.1 0.0 copy-done.3
  30.1 0.0 copy-start
  30.1 15.0 %shard_map.87 = (bf16[2,4,16,32,1024]{4,3,2,1,0:T(8,128)(2,1)}, bf16[2,2,16,16,256]{4,3,2,1,0:T(8,128)(2,1)S(1)}, bf16[2,2,16,16,256]{4,3,2,1,0:T(8,128)(2,1)S(1...) custom-call(s32[4]{0:T(128)S(1)} %pad_add_fusion.me_ref, bf16[4,192,256]{2,1,0:T(8,128)(2,1)S(1)} %copy-done.3, ...), custom_call_target="tpu_custom_call" | custom-call | flops 12800000000 | bytes 8388608 | tf_op jit(solution)/shard_map/pallas_call | solution.py:175
  45.1 2.0 %collective-permute-start.5 = (bf16[2,2,16,16,256]{4,3,2,1,0:T(8,128)(2,1)S(1)}, bf16[2,2,16,16,256]{4,3,2,1,0:T(8,128)(2,1)S(1)}, u32[]{:S(2)}, u32[]{:S(2)}) collective-permute-start(bf16[2,2,16,16,256]{4,3,2,1,0:T(8,128)(2,1)S(1)} %get-tuple-element.19), channel_id=1, source_target_pairs={{0,8},{8,0},{16,24},{24,16},{1,9},{9,1},{17,25},{25,17},{2,10},{10... | collective-permute-start | bytes 1572872 | tf_op jit(solution)/shard_map/ppermute | solution.py:245
  47.0 1.5 %collective-permute-start.6 = (bf16[2,2,16,16,256]{4,3,2,1,0:T(8,128)(2,1)S(1)}, bf16[2,2,16,16,256]{4,3,2,1,0:T(8,128)(2,1)S(1)}, u32[]{:S(2)}, u32[]{:S(2)}) collective-permute-start(bf16[2,2,16,16,256]{4,3,2,1,0:T(8,128)(2,1)S(1)} %get-tuple-element.20), channel_id=1, source_target_pairs={{0,16},{8,24},{16,0},{24,8},{1,17},{9,25},{17,1},{25,9},{2,18},{10... | collective-permute-start | bytes 1572872 | tf_op jit(solution)/shard_map/ppermute | solution.py:245
  48.6 0.0 collective-permute-done.2.refs_1_
  48.6 0.0 collective-permute-start.7
  48.6 0.0 copy-done
  48.6 17.3 %shard_map.88 = bf16[2,4,16,32,1024]{4,3,2,1,0:T(8,128)(2,1)} custom-call(s32[4]{0:T(128)S(1)} %pad_add_fusion.me_ref, bf16[4,384,256]{2,1,0:T(8,128)(2,1)S(1)} %copy-done, bf16[512,512]{1,0:T(8,128)(2,1)S(1)} %copy-done.2, bf16[2,4,16,32,1024]{4,3,2,1,0:T(8,128)(2,1)} %above.5, bf16[2,4,16,32,1024]{4,3,2,1,0:T(8,128)(2,1)} %above.5, ...), custom_call_target="tpu_custom_call", output_to_operand_aliasing={{}: (8, {})} | custom-call | flops 25600000000 | bytes 16777216 | tf_op jit(solution)/shard_map/pallas_call | solution.py:175
  65.9 0.0 collective-permute-done.3.refs_2_
  65.9 0.0 collective-permute-done.4.refs_3_
  65.9 0.0 collective-permute-done.5.refs_5_
  65.9 8.0 %collective-permute-done.6.refs_6_ = bf16[2,2,16,16,256]{4,3,2,1,0:T(8,128)(2,1)S(1)} collective-permute-done((bf16[2,2,16,16,256]{4,3,2,1,0:T(8,128)(2,1)S(1)}, bf16[2,2,16,16,256]{4,3,2,1,0:T(8,128)(2,1)S(1)}, u32[]{:S(2)}, u32[]{:S(2)}) %collective-permute-start.6) | collective-permute-done | bytes 524320 | tf_op jit(solution)/shard_map/ppermute | solution.py:245
  73.9 0.0 collective-permute-done.7.refs_7_
  73.9 0.0 copy-start.5
  73.9 0.8 %copy-done.5 = bf16[2,2,16,16,256]{4,3,2,1,0:T(8,128)(2,1)} copy-done((bf16[2,2,16,16,256]{4,3,2,1,0:T(8,128)(2,1)}, bf16[2,2,16,16,256]{4,3,2,1,0:T(8,128)(2,1)S(1)}, u32[]{:S(2)}) %copy-start.5) | copy-done | bytes 524312
  74.7 3.9 %shard_map.89 = f32[16,32,256]{2,1,0:T(8,128)} custom-call(bf16[2,2,16,16,256]{4,3,2,1,0:T(8,128)(2,1)S(1)} %get-tuple-element.14.refs_0_, bf16[2,2,16,16,256]{4,3,2,1,0:T(8,128)(2,1)S(1)} %collective-permute-done.2.refs_1_, bf16[2,2,16,16,256]{4,3,2,1,0:T(8,128)(2,1)S(1)} %collective-permute-done.3.refs_2_, ...), custom_call_target="tpu_custom_call" | custom-call | flops 100000000 | bytes 5242880 | tf_op jit(solution)/shard_map/pallas_call | solution.py:216
Async XLA Ops:
  4.5 25.5 %collective-permute-start = (bf16[2,4,32,1024]{3,2,1,0:T(8,128)(2,1)S(1)}, bf16[2,4,32,1024]{3,2,1,0:T(8,128)(2,1)S(1)}, u32[]{:S(2)}, u32[]{:S(2)}) collective-permute-start(bf16[2,4,32,1024]{3,2,1,0:T(8,128)(2,1)S(1)} %copy.11), channel_id=1, source_target_pairs={{0,1},{1,2},{2,3},{3,4},{4,5},{5,6},{6,7},{7,0},{8,9},{9,10},{10,1... | collective-permute-start | bytes 1572872 | tf_op jit(solution)/shard_map/ppermute | solution.py:237
  5.6 24.5 %collective-permute-start.1 = (bf16[2,4,32,1024]{3,2,1,0:T(8,128)(2,1)S(1)}, bf16[2,4,32,1024]{3,2,1,0:T(8,128)(2,1)S(1)}, u32[]{:S(2)}, u32[]{:S(2)}) collective-permute-start(bf16[2,4,32,1024]{3,2,1,0:T(8,128)(2,1)S(1)} %copy.13), channel_id=1, source_target_pairs={{1,0},{2,1},{3,2},{4,3},{5,4},{6,5},{7,6},{0,7},{9,8},{10,9},{11,1... | collective-permute-start | bytes 1572872 | tf_op jit(solution)/shard_map/ppermute | solution.py:238
  9.8 1.0 %copy-start.1 = (bf16[512,512]{1,0:T(8,128)(2,1)S(1)}, bf16[512,512]{1,0:T(8,128)(2,1)}, u32[]{:S(2)}) copy-start(bf16[512,512]{1,0:T(8,128)(2,1)} %constant.20.clone.b_ref) | copy-start | bytes 1572868
  10.8 1.0 %copy-start.4 = (bf16[4,192,192]{2,1,0:T(8,128)(2,1)S(1)}, bf16[4,192,192]{2,1,0:T(8,128)(2,1)}, u32[]{:S(2)}) copy-start(bf16[4,192,192]{2,1,0:T(8,128)(2,1)} %constant.19.clone.a_ref) | copy-start | bytes 884740
  11.8 18.2 %copy-start.2 = (bf16[512,512]{1,0:T(8,128)(2,1)S(1)}, bf16[512,512]{1,0:T(8,128)(2,1)}, u32[]{:S(2)}) copy-start(bf16[512,512]{1,0:T(8,128)(2,1)} %constant.20.clone.b_ref) | copy-start | bytes 1572868
  11.8 18.2 %copy-start.3 = (bf16[4,192,256]{2,1,0:T(8,128)(2,1)S(1)}, bf16[4,192,256]{2,1,0:T(8,128)(2,1)}, u32[]{:S(2)}) copy-start(bf16[4,192,256]{2,1,0:T(8,128)(2,1)} %constant.21.clone.a_ref) | copy-start | bytes 1179652
  26.6 22.0 %collective-permute-start.2 = (bf16[2,2,16,16,256]{4,3,2,1,0:T(8,128)(2,1)S(1)}, bf16[2,2,16,16,256]{4,3,2,1,0:T(8,128)(2,1)S(1)}, u32[]{:S(2)}, u32[]{:S(2)}) collective-permute-start(bf16[2,2,16,16,256]{4,3,2,1,0:T(8,128)(2,1)S(1)} %get-tuple-element.15), channel_id=1, source_target_pairs={{0,8},{8,0},{16,24},{24,16},{1,9},{9,1},{17,25},{25,17},{2,10},{10... | collective-permute-start | bytes 1572872 | tf_op jit(solution)/shard_map/ppermute | solution.py:245
  28.5 37.4 %collective-permute-start.3 = (bf16[2,2,16,16,256]{4,3,2,1,0:T(8,128)(2,1)S(1)}, bf16[2,2,16,16,256]{4,3,2,1,0:T(8,128)(2,1)S(1)}, u32[]{:S(2)}, u32[]{:S(2)}) collective-permute-start(bf16[2,2,16,16,256]{4,3,2,1,0:T(8,128)(2,1)S(1)} %get-tuple-element.16), channel_id=1, source_target_pairs={{0,16},{8,24},{16,0},{24,8},{1,17},{9,25},{17,1},{25,9},{2,18},{10... | collective-permute-start | bytes 1572872 | tf_op jit(solution)/shard_map/ppermute | solution.py:245
  30.0 35.9 %collective-permute-start.4 = (bf16[2,2,16,16,256]{4,3,2,1,0:T(8,128)(2,1)S(1)}, bf16[2,2,16,16,256]{4,3,2,1,0:T(8,128)(2,1)S(1)}, u32[]{:S(2)}, u32[]{:S(2)}) collective-permute-start(bf16[2,2,16,16,256]{4,3,2,1,0:T(8,128)(2,1)S(1)} %get-tuple-element.17), channel_id=1, source_target_pairs={{0,24},{8,16},{16,8},{24,0},{1,25},{9,17},{17,9},{25,1},{2,26},{10... | collective-permute-start | bytes 1572872 | tf_op jit(solution)/shard_map/ppermute | solution.py:245
  30.1 18.5 %copy-start = (bf16[4,384,256]{2,1,0:T(8,128)(2,1)S(1)}, bf16[4,384,256]{2,1,0:T(8,128)(2,1)}, u32[]{:S(2)}) copy-start(bf16[4,384,256]{2,1,0:T(8,128)(2,1)} %constant.22.clone.a_ref) | copy-start | bytes 2359300
  45.1 20.8 %collective-permute-start.5 = (bf16[2,2,16,16,256]{4,3,2,1,0:T(8,128)(2,1)S(1)}, bf16[2,2,16,16,256]{4,3,2,1,0:T(8,128)(2,1)S(1)}, u32[]{:S(2)}, u32[]{:S(2)}) collective-permute-start(bf16[2,2,16,16,256]{4,3,2,1,0:T(8,128)(2,1)S(1)} %get-tuple-element.19), channel_id=1, source_target_pairs={{0,8},{8,0},{16,24},{24,16},{1,9},{9,1},{17,25},{25,17},{2,10},{10... | collective-permute-start | bytes 1572872 | tf_op jit(solution)/shard_map/ppermute | solution.py:245
  47.0 26.9 %collective-permute-start.6 = (bf16[2,2,16,16,256]{4,3,2,1,0:T(8,128)(2,1)S(1)}, bf16[2,2,16,16,256]{4,3,2,1,0:T(8,128)(2,1)S(1)}, u32[]{:S(2)}, u32[]{:S(2)}) collective-permute-start(bf16[2,2,16,16,256]{4,3,2,1,0:T(8,128)(2,1)S(1)} %get-tuple-element.20), channel_id=1, source_target_pairs={{0,16},{8,24},{16,0},{24,8},{1,17},{9,25},{17,1},{25,9},{2,18},{10... | collective-permute-start | bytes 1572872 | tf_op jit(solution)/shard_map/ppermute | solution.py:245
  48.6 25.4 %collective-permute-start.7 = (bf16[2,2,16,16,256]{4,3,2,1,0:T(8,128)(2,1)S(1)}, bf16[2,2,16,16,256]{4,3,2,1,0:T(8,128)(2,1)S(1)}, u32[]{:S(2)}, u32[]{:S(2)}) collective-permute-start(bf16[2,2,16,16,256]{4,3,2,1,0:T(8,128)(2,1)S(1)} %get-tuple-element.21), channel_id=1, source_target_pairs={{0,24},{8,16},{16,8},{24,0},{1,25},{9,17},{17,9},{25,1},{2,26},{10... | collective-permute-start | bytes 1572872 | tf_op jit(solution)/shard_map/ppermute | solution.py:245
  73.9 0.8 %copy-start.5 = (bf16[2,2,16,16,256]{4,3,2,1,0:T(8,128)(2,1)}, bf16[2,2,16,16,256]{4,3,2,1,0:T(8,128)(2,1)S(1)}, u32[]{:S(2)}) copy-start(bf16[2,2,16,16,256]{4,3,2,1,0:T(8,128)(2,1)S(1)} %collective-permute-done.7.refs_7_) | copy-start | bytes 1572868

commit v4 on v3

--- a/solution.py
+++ b/solution.py
@@ -64,7 +64,7 @@
     resy = rest.pop()
     res = rest.pop()
     held = rest.pop() if kind == "edge" else None
-    if kind == "edge":
+    if kind in ("edge", "full"):
         out, sends = rest[-1 - parts], rest[-parts:]
     elif kind == "mid":
         out, sends = rest[0], rest[1:]
@@ -73,23 +73,25 @@
     rows, cols = main.shape[3], main.shape[4]
     count = sum(stop - start for start, stop in spans)
     total = depth * count
+    blocks = []
+    for k in range(2):
+        m = jnp.concatenate([main[0, first + k, z] for z in range(depth)], axis=0)
+        for j in range(cols // wide):
+            lo = (j * wide - 128) % cols
+            hi = (j * wide + wide) % cols
+            blocks.append(jnp.concatenate([m[:, j * wide : (j + 1) * wide], m[:, lo : lo + 128], m[:, hi : hi + 128]], axis=1))
+    resy[...] = jnp.dot(jnp.concatenate(blocks, axis=0), b_ref[...], preferred_element_type=jnp.float32)
     for k in range(2):
         f = first + k
         m = jnp.concatenate([main[0, f, z] for z in range(depth)], axis=0)
         w = jnp.concatenate([below[0, k, 0], m, above[0, k, 0]] + [h[0, k] for h in halos], axis=0)
         res[...] = jnp.dot(a_ref[0], w, preferred_element_type=jnp.float32)
-        for j in range(cols // wide):
-            lo = (j * wide - 128) % cols
-            hi = (j * wide + wide) % cols
-            block = jnp.concatenate([m[:, j * wide : (j + 1) * wide], m[:, lo : lo + 128], m[:, hi : hi + 128]], axis=1)
-            resy[:, 2 * j * wide : 2 * (j + 1) * wide] = jnp.dot(block, b_ref[...], preferred_element_type=jnp.float32)
-
         def level(z, carry):
             for j in range(cols // wide):
                 seg = slice(j * wide, (j + 1) * wide)
 
                 def get(g, start, stop):
-                    if kind == "rest":
+                    if kind in ("rest", "full"):
                         return main[0, g, z, start:stop, seg].astype(jnp.float32)
                     return main[0, g, z, :, seg].astype(jnp.float32)[start:stop]
 
@@ -97,21 +99,21 @@
                 at = 0
                 for start, stop in spans:
                     base = pl.multiple_of(z * count + at, 8)
-                    row = pl.multiple_of(z * rows + start, 8)
+                    row = pl.multiple_of((k * (cols // wide) + j) * depth * rows + z * rows + start, 8)
                     size = stop - start
                     at += size
                     u, v, wv = get(0, start, stop), get(1, start, stop), get(2, start, stop)
                     dx = res[pl.ds(base, size), seg]
                     dz = res[pl.ds(pl.multiple_of(total + base, 8), size), seg]
                     lap = res[pl.ds(pl.multiple_of(2 * total + base, 8), size), seg]
-                    dy = resy[pl.ds(row, size), 2 * j * wide : (2 * j + 1) * wide]
-                    lap = lap + resy[pl.ds(row, size), (2 * j + 1) * wide : (2 * j + 2) * wide]
+                    dy = resy[pl.ds(row, size), :wide]
+                    lap = lap + resy[pl.ds(row, size), wide:]
                     new = (time_step * viscosity) * lap - (time_step / 12.0) * (u * dx + v * dy + wv * dz)
                     if f == 2:
                         new = new + time_step * get(3, start, stop)
                     elif f == 3:
                         new = new - time_step * wv
-                    if kind == "rest":
+                    if kind in ("rest", "full"):
                         out[0, k, z, start:stop, seg] = new.astype(jnp.bfloat16)
                     news.append(new)
                 if kind == "mid":
@@ -167,7 +169,7 @@
         out_specs += [pl.BlockSpec((1, 2, depth, count, cols // parts), lambda m, c, me: (m, 0, c, 0, 0))] * parts
     scratch = [
         pltpu.VMEM((3 * depth * count, cols), jnp.float32),
-        pltpu.VMEM((depth * rows, 2 * cols), jnp.float32),
+        pltpu.VMEM((2 * (cols // wide) * depth * rows, 2 * wide), jnp.float32),
     ]
     if kind == "edge":
         scratch.insert(0, pltpu.VMEM((depth, count, cols), jnp.bfloat16))
@@ -184,44 +186,47 @@
     )(*args)
 
 
-def correlate_kernel(count, *refs):
+def correlate_kernel(count, n, *refs):
     out = refs[-1]
-    n = (len(refs) - 1) // 2
     inv = 1.0 / count
 
-    def rows_of(blocks, z):
+    def fields(z):
+        for middle, outer in zip(refs[:n], refs[n : 2 * n]):
+            for m in range(middle.shape[0]):
+                pair = []
+                for k in range(2):
+                    o = outer[m, k, z].astype(jnp.float32)
+                    pair.append(jnp.concatenate([o[:edge], middle[m, k, z].astype(jnp.float32), o[edge:]], axis=0))
+                yield pair
+        for whole in refs[2 * n : -1]:
+            for m in range(whole.shape[0]):
+                yield whole[m, 0, z].astype(jnp.float32), whole[m, 1, z].astype(jnp.float32)
+
+    for z in range(out.shape[0]):
         sums = None
-        for ref in blocks:
-            for m in range(ref.shape[0]):
-                w = ref[m, 0, z].astype(jnp.float32)
-                b = ref[m, 1, z].astype(jnp.float32)
-                terms = (b, w, b * b, w * w, b * w)
-                sums = terms if sums is None else [p + q for p, q in zip(sums, terms)]
+        for w, b in fields(z):
+            terms = (b, w, b * b, w * w, b * w)
+            sums = terms if sums is None else [p + q for p, q in zip(sums, terms)]
         mb, mw = sums[0] * inv, sums[1] * inv
         vb = sums[2] * inv - mb * mb
         vw = sums[3] * inv - mw * mw
         cov = sums[4] * inv - mb * mw
-        return cov * lax.rsqrt(jnp.maximum(vb, var_floor) * jnp.maximum(vw, var_floor))
-
-    for z in range(out.shape[0]):
-        inner = rows_of(refs[:n], z)
-        outer = rows_of(refs[n:-1], z)
-        out[z] = jnp.concatenate([outer[:edge], inner, outer[edge:]], axis=0)
-
-
-def run_correlate(count, mids, edges):
+        out[z] = cov * lax.rsqrt(jnp.maximum(vb, var_floor) * jnp.maximum(vw, var_floor))
+
+
+def run_correlate(count, mids, edges, wholes):
     _, _, levels, middle, part = mids[0].shape
     rows = middle + 2 * edge
-    specs = [pl.BlockSpec(b.shape[:2] + (depth,) + b.shape[3:], lambda c: (0, 0, c, 0, 0)) for b in mids + edges]
+    args = mids + edges + wholes
     return pl.pallas_call(
-        functools.partial(correlate_kernel, count),
+        functools.partial(correlate_kernel, count, len(mids)),
         out_shape=jax.ShapeDtypeStruct((levels, rows, part), jnp.float32),
         grid=(levels // depth,),
-        in_specs=specs,
+        in_specs=[pl.BlockSpec(b.shape[:2] + (depth,) + b.shape[3:], lambda c: (0, 0, c, 0, 0)) for b in args],
         out_specs=pl.BlockSpec((depth, rows, part), lambda c: (c, 0, 0)),
         compiler_params=pltpu.CompilerParams(vmem_limit_bytes=vmem),
         cost_estimate=pl.CostEstimate(flops=10**8, bytes_accessed=5 * 2**20, transcendentals=0),
-    )(*mids, *edges)
+    )(*args)
 
 
 def partner(i, k, parts):
@@ -248,13 +253,16 @@
     inner = ((edge, rows - edge),)
     outer = ((0, edge), (rows - edge, rows))
     halves = tuple((x, x + 16) for x in range(0, rows, 16))
-    both = (0, m_)
-    middle, *blocks = run_step("mid", 2, both, parts, inner, order, state)
+    middle, *blocks = run_step("mid", 2, (0, 1), parts, inner, order, state)
     mids = exchange(blocks)
-    stepped, *blocks = run_step("edge", 2, both, parts, outer, order, state, lo, hi, middle)
+    stepped, *blocks = run_step("edge", 2, (0, 1), parts, outer, order, state, lo, hi, middle)
     edges = exchange(blocks)
-    (stepped,) = run_step("rest", 0, both, parts, halves, order, state, lo, hi, None, stepped)
-    return stepped, run_correlate(float(m_ * parts), mids, edges)
+    wholes = []
+    if m_ > 1:
+        stepped, *blocks = run_step("full", 2, (1, m_), parts, halves, order, state, lo, hi, None, stepped)
+        wholes = exchange(blocks)
+    (stepped,) = run_step("rest", 0, (0, m_), parts, halves, order, state, lo, hi, None, stepped)
+    return stepped, run_correlate(float(m_ * parts), mids, edges, wholes)
 
 
 def solution(mesh):

time: 79 us -> 80.5 us (1.019)
  starting transfers between devices: 11.6 us -> 15.2 us
  Pallas kernels: 51 us -> 48.6 us
    ppermute x6 -> x9, starting transfers between devices: 6.99 us -> 10.6 us  [exchange(): lax.ppermute(blocks[k], 'member', [(i, partner(i, k, parts)) for i in ran...]
    pallas_call x3 -> x4, Pallas kernels: 47 us -> 44.6 us  [run_step(): pl.pallas_call(functools.partial(step_kernel, kind, first, parts, spans),...]
    ppermute x6 -> x9, waiting for transfers between devices: 8.05 us -> 8.27 us  [exchange(): lax.ppermute(blocks[k], 'member', [(i, partner(i, k, parts)) for i in ran...]
  transfers between devices with their start and end apart: 8 -> 11, of which waited for: 1 -> 2; matrix products, arithmetic and copies ran while one was open for 1% -> 1% of each run, Pallas kernels for 60% -> 56%
where the time goes in v4:
time: 80.5 us; the launch traced here: 80.2 us
  Pallas kernels  48.6 us (60%)
  starting transfers between devices  15.2 us (19%)
  waiting for transfers between devices  8.28 us (10%)
  local copies, waits for them, and re-layouts  7.26 us (9%)
    pallas_call x4, Pallas kernels, run_step(): pl.pallas_call(functools.partial(step_kernel, kind, first, parts, spans),...  44.6 us
    ppermute x9, starting transfers between devices, exchange(): lax.ppermute(blocks[k], 'member', [(i, partner(i, k, parts)) for i in ran...  10.6 us
    ppermute x9, waiting for transfers between devices, exchange(): lax.ppermute(blocks[k], 'member', [(i, partner(i, k, parts)) for i in ran...  8.27 us
    ppermute x1, starting transfers between devices, on_device(): lax.ppermute(head, 'space', [((i + 1) % count, i) for i in range(count)])  4.11 us
    pallas_call x1, Pallas kernels, run_correlate(): pl.pallas_call(functools.partial(correlate_kernel, count, len(mids)), out...  4.05 us
    slice x2, local copies, waits for them, and re-layouts, on_device(): head = state[:, :, :, :2, :].reshape(m_, 4, 2 * levels, cols)  3.7 us
    unnamed x12, local copies, waits for them, and re-layouts  2.84 us
  transfers between devices with their start and end apart: 11, of which 2 were waited for; matrix products, arithmetic and copies ran while one was open for 1% of the time, Pallas kernels for 56%

profile of v4, /device:TPU:0, one launch (start us, length us, event | category | flops | bytes accessed | tf_op | source)
XLA Modules:
  0.0 80.2 jit_solution(1646364423370700076)
XLA Ops:
  0.6 3.3 %fusion = (bf16[2,4,16,2,1024]{4,3,2,1,0:T(2,128)(2,1)S(1)}, bf16[2,4,16,2,1024]{4,3,2,1,0:T(2,128)(2,1)S(1)}) fusion(bf16[2,4,16,32,1024]{4,3,2,1,0:T(8,128)(2,1)} %above.7), kind=kLoop, calls=%fused_computation.1 | loop fusion | bytes 2097152 | tf_op jit(solution)/shard_map/slice | solution.py:240
  3.9 0.4 copy.13
  4.3 0.2 copy.14
  4.5 0.5 collective-permute-start
  5.0 0.4 copy.15
  5.4 0.2 copy.16
  5.6 4.1 %collective-permute-start.1 = (bf16[2,4,32,1024]{3,2,1,0:T(8,128)(2,1)S(1)}, bf16[2,4,32,1024]{3,2,1,0:T(8,128)(2,1)S(1)}, u32[]{:S(2)}, u32[]{:S(2)}) collective-permute-start(bf16[2,4,32,1024]{3,2,1,0:T(8,128)(2,1)S(1)} %copy.16), channel_id=1, source_target_pairs={{1,0},{2,1},{3,2},{4,3},{5,4},{6,5},{7,6},{0,7},{9,8},{10,9},{11,1... | collective-permute-start | bytes 1572872 | tf_op jit(solution)/shard_map/ppermute | solution.py:243
  9.7 0.1 pad_add_fusion.me_ref
  9.8 0.0 copy-start
  9.8 1.0 %copy-done = bf16[512,512]{1,0:T(8,128)(2,1)S(1)} copy-done((bf16[512,512]{1,0:T(8,128)(2,1)S(1)}, bf16[512,512]{1,0:T(8,128)(2,1)}, u32[]{:S(2)}) %copy-start) | copy-done | bytes 524312
  10.8 0.0 copy-start.2
  10.8 1.0 %copy-done.2 = bf16[4,192,192]{2,1,0:T(8,128)(2,1)S(1)} copy-done((bf16[4,192,192]{2,1,0:T(8,128)(2,1)S(1)}, bf16[4,192,192]{2,1,0:T(8,128)(2,1)}, u32[]{:S(2)}) %copy-start.2) | copy-done | bytes 294936
  11.8 0.0 copy-start.1
  11.8 0.0 copy-start.3
  11.8 7.8 %shard_map.104 = (bf16[1,2,16,16,1024]{4,3,2,1,0:T(8,128)(2,1)S(1)}, bf16[1,2,16,16,256]{4,3,2,1,0:T(8,128)(2,1)S(1)}, bf16[1,2,16,16,256]{4,3,2,1,0:T(8,128)(2,...) custom-call(s32[4]{0:T(128)S(1)} %pad_add_fusion.me_ref, ...), custom_call_target="tpu_custom_call" | custom-call | flops 6400000000 | bytes 4194304 | tf_op jit(solution)/shard_map/pallas_call | solution.py:177
  19.6 2.1 %collective-permute-start.2 = (bf16[1,2,16,16,256]{4,3,2,1,0:T(8,128)(2,1)S(1)}, bf16[1,2,16,16,256]{4,3,2,1,0:T(8,128)(2,1)S(1)}, u32[]{:S(2)}, u32[]{:S(2)}) collective-permute-start(bf16[1,2,16,16,256]{4,3,2,1,0:T(8,128)(2,1)S(1)} %get-tuple-element.21), channel_id=1, source_target_pairs={{0,8},{8,0},{16,24},{24,16},{1,9},{9,1},{17,25},{25,17},{2,10},{10... | collective-permute-start | bytes 786440 | tf_op jit(solution)/shard_map/ppermute | solution.py:250
  21.7 1.5 %collective-permute-start.3 = (bf16[1,2,16,16,256]{4,3,2,1,0:T(8,128)(2,1)S(1)}, bf16[1,2,16,16,256]{4,3,2,1,0:T(8,128)(2,1)S(1)}, u32[]{:S(2)}, u32[]{:S(2)}) collective-permute-start(bf16[1,2,16,16,256]{4,3,2,1,0:T(8,128)(2,1)S(1)} %get-tuple-element.22), channel_id=1, source_target_pairs={{0,16},{8,24},{16,0},{24,8},{1,17},{9,25},{17,1},{25,9},{2,18},{10... | collective-permute-start | bytes 786440 | tf_op jit(solution)/shard_map/ppermute | solution.py:250
  23.2 0.0 collective-permute-start.4
  23.2 0.0 collective-permute-done.rest_0_
  23.2 0.0 collective-permute-done.1.rest_1_
  23.2 0.0 copy-done.1
  23.2 0.0 copy-done.3
  23.2 8.7 %shard_map.105 = (bf16[2,4,16,32,1024]{4,3,2,1,0:T(8,128)(2,1)}, bf16[1,2,16,16,256]{4,3,2,1,0:T(8,128)(2,1)S(1)}, bf16[1,2,16,16,256]{4,3,2,1,0:T(8,128)(2,1)S(...) custom-call(s32[4]{0:T(128)S(1)} %pad_add_fusion.me_ref, bf16[4,192,256]{2,1,0:T(8,128)(2,1)S(1)} %copy-done.3, ...), custom_call_target="tpu_custom_call" | custom-call | flops 6400000000 | bytes 4194304 | tf_op jit(solution)/shard_map/pallas_call | solution.py:177
  31.9 2.0 %collective-permute-start.5 = (bf16[1,2,16,16,256]{4,3,2,1,0:T(8,128)(2,1)S(1)}, bf16[1,2,16,16,256]{4,3,2,1,0:T(8,128)(2,1)S(1)}, u32[]{:S(2)}, u32[]{:S(2)}) collective-permute-start(bf16[1,2,16,16,256]{4,3,2,1,0:T(8,128)(2,1)S(1)} %get-tuple-element.25), channel_id=1, source_target_pairs={{0,8},{8,0},{16,24},{24,16},{1,9},{9,1},{17,25},{25,17},{2,10},{10... | collective-permute-start | bytes 786440 | tf_op jit(solution)/shard_map/ppermute | solution.py:250
  33.9 1.5 %collective-permute-start.6 = (bf16[1,2,16,16,256]{4,3,2,1,0:T(8,128)(2,1)S(1)}, bf16[1,2,16,16,256]{4,3,2,1,0:T(8,128)(2,1)S(1)}, u32[]{:S(2)}, u32[]{:S(2)}) collective-permute-start(bf16[1,2,16,16,256]{4,3,2,1,0:T(8,128)(2,1)S(1)} %get-tuple-element.26), channel_id=1, source_target_pairs={{0,16},{8,24},{16,0},{24,8},{1,17},{9,25},{17,1},{25,9},{2,18},{10... | collective-permute-start | bytes 786440 | tf_op jit(solution)/shard_map/ppermute | solution.py:250
  35.4 0.0 copy-start.4
  35.4 10.7 %shard_map.106 = (bf16[2,4,16,32,1024]{4,3,2,1,0:T(8,128)(2,1)}, bf16[1,2,16,32,256]{4,3,2,1,0:T(8,128)(2,1)S(1)}, bf16[1,2,16,32,256]{4,3,2,1,0:T(8,128)(2,1)S(...) custom-call(s32[4]{0:T(128)S(1)} %pad_add_fusion.me_ref, ...), custom_call_target="tpu_custom_call", output_to_operand_aliasing={{0}: (8, {})} | custom-call | flops 12800000000 | bytes 8388608 | tf_op jit(solution)/shard_map/pallas_call | solution.py:177
  46.1 0.0 collective-permute-done.2.refs_1_
  46.1 0.0 collective-permute-start.7
  46.2 0.0 collective-permute-done.3.refs_2_
  46.2 2.0 %collective-permute-start.8 = (bf16[1,2,16,32,256]{4,3,2,1,0:T(8,128)(2,1)S(1)}, bf16[1,2,16,32,256]{4,3,2,1,0:T(8,128)(2,1)S(1)}, u32[]{:S(2)}, u32[]{:S(2)}) collective-permute-start(bf16[1,2,16,32,256]{4,3,2,1,0:T(8,128)(2,1)S(1)} %get-tuple-element.29), channel_id=1, source_target_pairs={{0,8},{8,0},{16,24},{24,16},{1,9},{9,1},{17,25},{25,17},{2,10},{10... | collective-permute-start | bytes 1572872 | tf_op jit(solution)/shard_map/ppermute | solution.py:250
  48.1 0.0 collective-permute-done.4.refs_3_
  48.1 1.5 %collective-permute-start.9 = (bf16[1,2,16,32,256]{4,3,2,1,0:T(8,128)(2,1)S(1)}, bf16[1,2,16,32,256]{4,3,2,1,0:T(8,128)(2,1)S(1)}, u32[]{:S(2)}, u32[]{:S(2)}) collective-permute-start(bf16[1,2,16,32,256]{4,3,2,1,0:T(8,128)(2,1)S(1)} %get-tuple-element.30), channel_id=1, source_target_pairs={{0,16},{8,24},{16,0},{24,8},{1,17},{9,25},{17,1},{25,9},{2,18},{10... | collective-permute-start | bytes 1572872 | tf_op jit(solution)/shard_map/ppermute | solution.py:250
  49.6 0.0 collective-permute-done.5.refs_5_
  49.6 0.1 collective-permute-start.10
  49.7 0.0 copy-done.4
  49.7 17.4 %shard_map.107 = bf16[2,4,16,32,1024]{4,3,2,1,0:T(8,128)(2,1)} custom-call(s32[4]{0:T(128)S(1)} %pad_add_fusion.me_ref, bf16[4,384,256]{2,1,0:T(8,128)(2,1)S(1)} %copy-done.4, bf16[512,512]{1,0:T(8,128)(2,1)S(1)} %copy-done.1, bf16[2,4,16,32,1024]{4,3,2,1,0:T(8,128)(2,1)} %above.7, ...), custom_call_target="tpu_custom_call", output_to_operand_aliasing={{}: (8, {})} | custom-call | flops 25600000000 | bytes 16777216 | tf_op jit(solution)/shard_map/pallas_call | solution.py:177
  67.1 0.0 collective-permute-done.6.refs_6_
  67.1 0.0 collective-permute-done.7.refs_7_
  67.1 0.0 collective-permute-done.8.refs_9_
  67.1 0.3 collective-permute-done.9.refs_10_
  67.4 7.9 %collective-permute-done.10.refs_11_ = bf16[1,2,16,32,256]{4,3,2,1,0:T(8,128)(2,1)S(1)} collective-permute-done((bf16[1,2,16,32,256]{4,3,2,1,0:T(8,128)(2,1)S(1)}, bf16[1,2,16,32,256]{4,3,2,1,0:T(8,128)(2,1)S(1)}, u32[]{:S(2)}, u32[]{:S(2)}) %collective-permute-start.10) | collective-permute-done | bytes 524320 | tf_op jit(solution)/shard_map/ppermute | solution.py:250
  75.3 0.0 copy-start.5
  75.4 0.8 copy-done.5
  76.1 4.0 %shard_map.108 = f32[16,32,256]{2,1,0:T(8,128)} custom-call(bf16[1,2,16,16,256]{4,3,2,1,0:T(8,128)(2,1)S(1)} %get-tuple-element.20.refs_0_, bf16[1,2,16,16,256]{4,3,2,1,0:T(8,128)(2,1)S(1)} %collective-permute-done.2.refs_1_, bf16[1,2,16,16,256]{4,3,2,1,0:T(8,128)(2,1)S(1)} %collective-permute-done.3.refs_2_, ...), custom_call_target="tpu_custom_call" | custom-call | flops 100000000 | bytes 5242880 | tf_op jit(solution)/shard_map/pallas_call | solution.py:221
Async XLA Ops:
  4.5 18.7 %collective-permute-start = (bf16[2,4,32,1024]{3,2,1,0:T(8,128)(2,1)S(1)}, bf16[2,4,32,1024]{3,2,1,0:T(8,128)(2,1)S(1)}, u32[]{:S(2)}, u32[]{:S(2)}) collective-permute-start(bf16[2,4,32,1024]{3,2,1,0:T(8,128)(2,1)S(1)} %copy.14), channel_id=1, source_target_pairs={{0,1},{1,2},{2,3},{3,4},{4,5},{5,6},{6,7},{7,0},{8,9},{9,10},{10,1... | collective-permute-start | bytes 1572872 | tf_op jit(solution)/shard_map/ppermute | solution.py:242
  5.6 17.6 %collective-permute-start.1 = (bf16[2,4,32,1024]{3,2,1,0:T(8,128)(2,1)S(1)}, bf16[2,4,32,1024]{3,2,1,0:T(8,128)(2,1)S(1)}, u32[]{:S(2)}, u32[]{:S(2)}) collective-permute-start(bf16[2,4,32,1024]{3,2,1,0:T(8,128)(2,1)S(1)} %copy.16), channel_id=1, source_target_pairs={{1,0},{2,1},{3,2},{4,3},{5,4},{6,5},{7,6},{0,7},{9,8},{10,9},{11,1... | collective-permute-start | bytes 1572872 | tf_op jit(solution)/shard_map/ppermute | solution.py:243
  9.8 1.0 %copy-start = (bf16[512,512]{1,0:T(8,128)(2,1)S(1)}, bf16[512,512]{1,0:T(8,128)(2,1)}, u32[]{:S(2)}) copy-start(bf16[512,512]{1,0:T(8,128)(2,1)} %constant.20.clone.b_ref) | copy-start | bytes 1572868
  10.8 1.0 %copy-start.2 = (bf16[4,192,192]{2,1,0:T(8,128)(2,1)S(1)}, bf16[4,192,192]{2,1,0:T(8,128)(2,1)}, u32[]{:S(2)}) copy-start(bf16[4,192,192]{2,1,0:T(8,128)(2,1)} %constant.19.clone.a_ref) | copy-start | bytes 884740
  11.8 11.4 %copy-start.1 = (bf16[512,512]{1,0:T(8,128)(2,1)S(1)}, bf16[512,512]{1,0:T(8,128)(2,1)}, u32[]{:S(2)}) copy-start(bf16[512,512]{1,0:T(8,128)(2,1)} %constant.20.clone.b_ref) | copy-start | bytes 1572868
  11.8 11.4 %copy-start.3 = (bf16[4,192,256]{2,1,0:T(8,128)(2,1)S(1)}, bf16[4,192,256]{2,1,0:T(8,128)(2,1)}, u32[]{:S(2)}) copy-start(bf16[4,192,256]{2,1,0:T(8,128)(2,1)} %constant.21.clone.a_ref) | copy-start | bytes 1179652
  19.6 26.5 %collective-permute-start.2 = (bf16[1,2,16,16,256]{4,3,2,1,0:T(8,128)(2,1)S(1)}, bf16[1,2,16,16,256]{4,3,2,1,0:T(8,128)(2,1)S(1)}, u32[]{:S(2)}, u32[]{:S(2)}) collective-permute-start(bf16[1,2,16,16,256]{4,3,2,1,0:T(8,128)(2,1)S(1)} %get-tuple-element.21), channel_id=1, source_target_pairs={{0,8},{8,0},{16,24},{24,16},{1,9},{9,1},{17,25},{25,17},{2,10},{10... | collective-permute-start | bytes 786440 | tf_op jit(solution)/shard_map/ppermute | solution.py:250
  21.7 24.5 %collective-permute-start.3 = (bf16[1,2,16,16,256]{4,3,2,1,0:T(8,128)(2,1)S(1)}, bf16[1,2,16,16,256]{4,3,2,1,0:T(8,128)(2,1)S(1)}, u32[]{:S(2)}, u32[]{:S(2)}) collective-permute-start(bf16[1,2,16,16,256]{4,3,2,1,0:T(8,128)(2,1)S(1)} %get-tuple-element.22), channel_id=1, source_target_pairs={{0,16},{8,24},{16,0},{24,8},{1,17},{9,25},{17,1},{25,9},{2,18},{10... | collective-permute-start | bytes 786440 | tf_op jit(solution)/shard_map/ppermute | solution.py:250
  23.2 24.9 %collective-permute-start.4 = (bf16[1,2,16,16,256]{4,3,2,1,0:T(8,128)(2,1)S(1)}, bf16[1,2,16,16,256]{4,3,2,1,0:T(8,128)(2,1)S(1)}, u32[]{:S(2)}, u32[]{:S(2)}) collective-permute-start(bf16[1,2,16,16,256]{4,3,2,1,0:T(8,128)(2,1)S(1)} %get-tuple-element.23), channel_id=1, source_target_pairs={{0,24},{8,16},{16,8},{24,0},{1,25},{9,17},{17,9},{25,1},{2,26},{10... | collective-permute-start | bytes 786440 | tf_op jit(solution)/shard_map/ppermute | solution.py:250
  31.9 17.7 %collective-permute-start.5 = (bf16[1,2,16,16,256]{4,3,2,1,0:T(8,128)(2,1)S(1)}, bf16[1,2,16,16,256]{4,3,2,1,0:T(8,128)(2,1)S(1)}, u32[]{:S(2)}, u32[]{:S(2)}) collective-permute-start(bf16[1,2,16,16,256]{4,3,2,1,0:T(8,128)(2,1)S(1)} %get-tuple-element.25), channel_id=1, source_target_pairs={{0,8},{8,0},{16,24},{24,16},{1,9},{9,1},{17,25},{25,17},{2,10},{10... | collective-permute-start | bytes 786440 | tf_op jit(solution)/shard_map/ppermute | solution.py:250
  33.9 33.2 %collective-permute-start.6 = (bf16[1,2,16,16,256]{4,3,2,1,0:T(8,128)(2,1)S(1)}, bf16[1,2,16,16,256]{4,3,2,1,0:T(8,128)(2,1)S(1)}, u32[]{:S(2)}, u32[]{:S(2)}) collective-permute-start(bf16[1,2,16,16,256]{4,3,2,1,0:T(8,128)(2,1)S(1)} %get-tuple-element.26), channel_id=1, source_target_pairs={{0,16},{8,24},{16,0},{24,8},{1,17},{9,25},{17,1},{25,9},{2,18},{10... | collective-permute-start | bytes 786440 | tf_op jit(solution)/shard_map/ppermute | solution.py:250
  35.4 14.3 %copy-start.4 = (bf16[4,384,256]{2,1,0:T(8,128)(2,1)S(1)}, bf16[4,384,256]{2,1,0:T(8,128)(2,1)}, u32[]{:S(2)}) copy-start(bf16[4,384,256]{2,1,0:T(8,128)(2,1)} %constant.22.clone.a_ref) | copy-start | bytes 2359300
  46.1 20.9 %collective-permute-start.7 = (bf16[1,2,16,16,256]{4,3,2,1,0:T(8,128)(2,1)S(1)}, bf16[1,2,16,16,256]{4,3,2,1,0:T(8,128)(2,1)S(1)}, u32[]{:S(2)}, u32[]{:S(2)}) collective-permute-start(bf16[1,2,16,16,256]{4,3,2,1,0:T(8,128)(2,1)S(1)} %get-tuple-element.27), channel_id=1, source_target_pairs={{0,24},{8,16},{16,8},{24,0},{1,25},{9,17},{17,9},{25,1},{2,26},{10... | collective-permute-start | bytes 786440 | tf_op jit(solution)/shard_map/ppermute | solution.py:250
  46.2 20.9 %collective-permute-start.8 = (bf16[1,2,16,32,256]{4,3,2,1,0:T(8,128)(2,1)S(1)}, bf16[1,2,16,32,256]{4,3,2,1,0:T(8,128)(2,1)S(1)}, u32[]{:S(2)}, u32[]{:S(2)}) collective-permute-start(bf16[1,2,16,32,256]{4,3,2,1,0:T(8,128)(2,1)S(1)} %get-tuple-element.29), channel_id=1, source_target_pairs={{0,8},{8,0},{16,24},{24,16},{1,9},{9,1},{17,25},{25,17},{2,10},{10... | collective-permute-start | bytes 1572872 | tf_op jit(solution)/shard_map/ppermute | solution.py:250
  48.1 19.3 %collective-permute-start.9 = (bf16[1,2,16,32,256]{4,3,2,1,0:T(8,128)(2,1)S(1)}, bf16[1,2,16,32,256]{4,3,2,1,0:T(8,128)(2,1)S(1)}, u32[]{:S(2)}, u32[]{:S(2)}) collective-permute-start(bf16[1,2,16,32,256]{4,3,2,1,0:T(8,128)(2,1)S(1)} %get-tuple-element.30), channel_id=1, source_target_pairs={{0,16},{8,24},{16,0},{24,8},{1,17},{9,25},{17,1},{25,9},{2,18},{10... | collective-permute-start | bytes 1572872 | tf_op jit(solution)/shard_map/ppermute | solution.py:250
  49.6 25.7 %collective-permute-start.10 = (bf16[1,2,16,32,256]{4,3,2,1,0:T(8,128)(2,1)S(1)}, bf16[1,2,16,32,256]{4,3,2,1,0:T(8,128)(2,1)S(1)}, u32[]{:S(2)}, u32[]{:S(2)}) collective-permute-start(bf16[1,2,16,32,256]{4,3,2,1,0:T(8,128)(2,1)S(1)} %get-tuple-element.31), channel_id=1, source_target_pairs={{0,24},{8,16},{16,8},{24,0},{1,25},{9,17},{17,9},{25,1},{2,26},{10... | collective-permute-start | bytes 1572872 | tf_op jit(solution)/shard_map/ppermute | solution.py:250
  75.3 0.8 copy-start.5

commit v5 on v4

--- a/solution.py
+++ b/solution.py
@@ -82,11 +82,13 @@
             blocks.append(jnp.concatenate([m[:, j * wide : (j + 1) * wide], m[:, lo : lo + 128], m[:, hi : hi + 128]], axis=1))
     resy[...] = jnp.dot(jnp.concatenate(blocks, axis=0), b_ref[...], preferred_element_type=jnp.float32)
     for k in range(2):
+        m = jnp.concatenate([main[0, first + k, z] for z in range(depth)], axis=0)
+        w = jnp.concatenate([below[0, k, 0], m, above[0, k, 0]] + [h[0, k] for h in halos], axis=0)
+        res[k] = jnp.dot(a_ref[0], w, preferred_element_type=jnp.float32)
+    for k in range(2):
         f = first + k
-        m = jnp.concatenate([main[0, f, z] for z in range(depth)], axis=0)
-        w = jnp.concatenate([below[0, k, 0], m, above[0, k, 0]] + [h[0, k] for h in halos], axis=0)
-        res[...] = jnp.dot(a_ref[0], w, preferred_element_type=jnp.float32)
-        def level(z, carry):
+
+        def level(z):
             for j in range(cols // wide):
                 seg = slice(j * wide, (j + 1) * wide)
 
@@ -98,14 +100,14 @@
                 news = []
                 at = 0
                 for start, stop in spans:
-                    base = pl.multiple_of(z * count + at, 8)
-                    row = pl.multiple_of((k * (cols // wide) + j) * depth * rows + z * rows + start, 8)
+                    base = z * count + at
+                    row = (k * (cols // wide) + j) * depth * rows + z * rows + start
                     size = stop - start
                     at += size
                     u, v, wv = get(0, start, stop), get(1, start, stop), get(2, start, stop)
-                    dx = res[pl.ds(base, size), seg]
-                    dz = res[pl.ds(pl.multiple_of(total + base, 8), size), seg]
-                    lap = res[pl.ds(pl.multiple_of(2 * total + base, 8), size), seg]
+                    dx = res[k, pl.ds(base, size), seg]
+                    dz = res[k, pl.ds(total + base, size), seg]
+                    lap = res[k, pl.ds(2 * total + base, size), seg]
                     dy = resy[pl.ds(row, size), :wide]
                     lap = lap + resy[pl.ds(row, size), wide:]
                     new = (time_step * viscosity) * lap - (time_step / 12.0) * (u * dx + v * dy + wv * dz)
@@ -122,9 +124,9 @@
                     held[z, :, seg] = jnp.concatenate(news, axis=0).astype(jnp.bfloat16)
                     inner = mid[0, k, z, :, seg].astype(jnp.float32)
                     out[0, k, z, :, seg] = jnp.concatenate([news[0], inner, news[1]], axis=0).astype(jnp.bfloat16)
-            return carry
-
-        lax.fori_loop(0, depth, level, 0)
+
+        for z in range(depth):
+            level(z)
         part = cols // parts
         for j, send in enumerate(sends):
             at = pl.ds(pl.multiple_of(me_ref[j] * part, part), part)
@@ -168,7 +170,7 @@
         out_shape += [sds((m1 - m0, 2, levels, count, cols // parts), state.dtype)] * parts
         out_specs += [pl.BlockSpec((1, 2, depth, count, cols // parts), lambda m, c, me: (m, 0, c, 0, 0))] * parts
     scratch = [
-        pltpu.VMEM((3 * depth * count, cols), jnp.float32),
+        pltpu.VMEM((2, 3 * depth * count, cols), jnp.float32),
         pltpu.VMEM((2 * (cols // wide) * depth * rows, 2 * wide), jnp.float32),
     ]
     if kind == "edge":

time: 80.5 us -> 77.2 us (0.959)
  Pallas kernels: 48.6 us -> 39.4 us
  waiting for transfers between devices: 8.28 us -> 13.8 us
    pallas_call x4, Pallas kernels: 44.6 us -> 35.3 us  [run_step(): pl.pallas_call(functools.partial(step_kernel, kind, first, parts, spans),...]
    ppermute x9, waiting for transfers between devices: 8.27 us -> 13.8 us  [exchange(): lax.ppermute(blocks[k], 'member', [(i, partner(i, k, parts)) for i in ran...]
  transfers between devices with their start and end apart: 11 -> 11, of which waited for: 2 -> 3; matrix products, arithmetic and copies ran while one was open for 1% -> 1% of each run, Pallas kernels for 56% -> 46%
where the time goes in v5:
time: 77.2 us; the launch traced here: 76.5 us
  Pallas kernels  39.4 us (51%)
  starting transfers between devices  15.2 us (20%)
  waiting for transfers between devices  13.8 us (18%)
  local copies, waits for them, and re-layouts  7.26 us (9%)
    pallas_call x4, Pallas kernels, run_step(): pl.pallas_call(functools.partial(step_kernel, kind, first, parts, spans),...  35.3 us
    ppermute x9, waiting for transfers between devices, exchange(): lax.ppermute(blocks[k], 'member', [(i, partner(i, k, parts)) for i in ran...  13.8 us
    ppermute x9, starting transfers between devices, exchange(): lax.ppermute(blocks[k], 'member', [(i, partner(i, k, parts)) for i in ran...  10.6 us
    ppermute x1, starting transfers between devices, on_device(): lax.ppermute(head, 'space', [((i + 1) % count, i) for i in range(count)])  4.11 us
    pallas_call x1, Pallas kernels, run_correlate(): pl.pallas_call(functools.partial(correlate_kernel, count, len(mids)), out...  4.05 us
    slice x2, local copies, waits for them, and re-layouts, on_device(): head = state[:, :, :, :2, :].reshape(m_, 4, 2 * levels, cols)  3.7 us
    unnamed x12, local copies, waits for them, and re-layouts  2.84 us
  transfers between devices with their start and end apart: 11, of which 3 were waited for; matrix products, arithmetic and copies ran while one was open for 1% of the time, Pallas kernels for 46%

profile of v5, /device:TPU:0, one launch (start us, length us, event | category | flops | bytes accessed | tf_op | source)
XLA Modules:
  0.0 76.5 jit_solution(18404387810537663828)
XLA Ops:
  0.6 3.3 %fusion = (bf16[2,4,16,2,1024]{4,3,2,1,0:T(2,128)(2,1)S(1)}, bf16[2,4,16,2,1024]{4,3,2,1,0:T(2,128)(2,1)S(1)}) fusion(bf16[2,4,16,32,1024]{4,3,2,1,0:T(8,128)(2,1)} %above.7), kind=kLoop, calls=%fused_computation.1 | loop fusion | bytes 2097152 | tf_op jit(solution)/shard_map/slice | solution.py:242
  3.9 0.4 copy.13
  4.3 0.2 copy.14
  4.5 0.5 collective-permute-start
  5.0 0.4 copy.15
  5.4 0.2 copy.16
  5.6 4.1 %collective-permute-start.1 = (bf16[2,4,32,1024]{3,2,1,0:T(8,128)(2,1)S(1)}, bf16[2,4,32,1024]{3,2,1,0:T(8,128)(2,1)S(1)}, u32[]{:S(2)}, u32[]{:S(2)}) collective-permute-start(bf16[2,4,32,1024]{3,2,1,0:T(8,128)(2,1)S(1)} %copy.16), channel_id=1, source_target_pairs={{1,0},{2,1},{3,2},{4,3},{5,4},{6,5},{7,6},{0,7},{9,8},{10,9},{11,1... | collective-permute-start | bytes 1572872 | tf_op jit(solution)/shard_map/ppermute | solution.py:245
  9.7 0.1 pad_add_fusion.me_ref
  9.8 0.0 copy-start
  9.8 1.0 %copy-done = bf16[512,512]{1,0:T(8,128)(2,1)S(1)} copy-done((bf16[512,512]{1,0:T(8,128)(2,1)S(1)}, bf16[512,512]{1,0:T(8,128)(2,1)}, u32[]{:S(2)}) %copy-start) | copy-done | bytes 524312
  10.8 0.0 copy-start.2
  10.8 1.0 %copy-done.2 = bf16[4,192,192]{2,1,0:T(8,128)(2,1)S(1)} copy-done((bf16[4,192,192]{2,1,0:T(8,128)(2,1)S(1)}, bf16[4,192,192]{2,1,0:T(8,128)(2,1)}, u32[]{:S(2)}) %copy-start.2) | copy-done | bytes 294936
  11.8 0.0 copy-start.1
  11.8 0.0 copy-start.3
  11.8 6.5 %shard_map.104 = (bf16[1,2,16,16,1024]{4,3,2,1,0:T(8,128)(2,1)S(1)}, bf16[1,2,16,16,256]{4,3,2,1,0:T(8,128)(2,1)S(1)}, bf16[1,2,16,16,256]{4,3,2,1,0:T(8,128)(2,...) custom-call(s32[4]{0:T(128)S(1)} %pad_add_fusion.me_ref, ...), custom_call_target="tpu_custom_call" | custom-call | flops 6400000000 | bytes 4194304 | tf_op jit(solution)/shard_map/pallas_call | solution.py:179
  18.3 2.0 %collective-permute-start.2 = (bf16[1,2,16,16,256]{4,3,2,1,0:T(8,128)(2,1)S(1)}, bf16[1,2,16,16,256]{4,3,2,1,0:T(8,128)(2,1)S(1)}, u32[]{:S(2)}, u32[]{:S(2)}) collective-permute-start(bf16[1,2,16,16,256]{4,3,2,1,0:T(8,128)(2,1)S(1)} %get-tuple-element.21), channel_id=1, source_target_pairs={{0,8},{8,0},{16,24},{24,16},{1,9},{9,1},{17,25},{25,17},{2,10},{10... | collective-permute-start | bytes 786440 | tf_op jit(solution)/shard_map/ppermute | solution.py:252
  20.3 1.5 %collective-permute-start.3 = (bf16[1,2,16,16,256]{4,3,2,1,0:T(8,128)(2,1)S(1)}, bf16[1,2,16,16,256]{4,3,2,1,0:T(8,128)(2,1)S(1)}, u32[]{:S(2)}, u32[]{:S(2)}) collective-permute-start(bf16[1,2,16,16,256]{4,3,2,1,0:T(8,128)(2,1)S(1)} %get-tuple-element.22), channel_id=1, source_target_pairs={{0,16},{8,24},{16,0},{24,8},{1,17},{9,25},{17,1},{25,9},{2,18},{10... | collective-permute-start | bytes 786440 | tf_op jit(solution)/shard_map/ppermute | solution.py:252
  21.9 0.0 collective-permute-start.4
  21.9 0.0 collective-permute-done.rest_0_
  21.9 0.0 collective-permute-done.1.rest_1_
  21.9 0.0 copy-done.1
  21.9 0.0 copy-done.3
  21.9 7.4 %shard_map.105 = (bf16[2,4,16,32,1024]{4,3,2,1,0:T(8,128)(2,1)}, bf16[1,2,16,16,256]{4,3,2,1,0:T(8,128)(2,1)S(1)}, bf16[1,2,16,16,256]{4,3,2,1,0:T(8,128)(2,1)S(...) custom-call(s32[4]{0:T(128)S(1)} %pad_add_fusion.me_ref, bf16[4,192,256]{2,1,0:T(8,128)(2,1)S(1)} %copy-done.3, ...), custom_call_target="tpu_custom_call" | custom-call | flops 6400000000 | bytes 4194304 | tf_op jit(solution)/shard_map/pallas_call | solution.py:179
  29.3 2.0 %collective-permute-start.5 = (bf16[1,2,16,16,256]{4,3,2,1,0:T(8,128)(2,1)S(1)}, bf16[1,2,16,16,256]{4,3,2,1,0:T(8,128)(2,1)S(1)}, u32[]{:S(2)}, u32[]{:S(2)}) collective-permute-start(bf16[1,2,16,16,256]{4,3,2,1,0:T(8,128)(2,1)S(1)} %get-tuple-element.25), channel_id=1, source_target_pairs={{0,8},{8,0},{16,24},{24,16},{1,9},{9,1},{17,25},{25,17},{2,10},{10... | collective-permute-start | bytes 786440 | tf_op jit(solution)/shard_map/ppermute | solution.py:252
  31.3 1.5 %collective-permute-start.6 = (bf16[1,2,16,16,256]{4,3,2,1,0:T(8,128)(2,1)S(1)}, bf16[1,2,16,16,256]{4,3,2,1,0:T(8,128)(2,1)S(1)}, u32[]{:S(2)}, u32[]{:S(2)}) collective-permute-start(bf16[1,2,16,16,256]{4,3,2,1,0:T(8,128)(2,1)S(1)} %get-tuple-element.26), channel_id=1, source_target_pairs={{0,16},{8,24},{16,0},{24,8},{1,17},{9,25},{17,1},{25,9},{2,18},{10... | collective-permute-start | bytes 786440 | tf_op jit(solution)/shard_map/ppermute | solution.py:252
  32.8 0.0 copy-start.4
  32.8 8.3 %shard_map.106 = (bf16[2,4,16,32,1024]{4,3,2,1,0:T(8,128)(2,1)}, bf16[1,2,16,32,256]{4,3,2,1,0:T(8,128)(2,1)S(1)}, bf16[1,2,16,32,256]{4,3,2,1,0:T(8,128)(2,1)S(...) custom-call(s32[4]{0:T(128)S(1)} %pad_add_fusion.me_ref, ...), custom_call_target="tpu_custom_call", output_to_operand_aliasing={{0}: (8, {})} | custom-call | flops 12800000000 | bytes 8388608 | tf_op jit(solution)/shard_map/pallas_call | solution.py:179
  41.1 0.0 collective-permute-done.2.refs_1_
  41.1 0.0 collective-permute-start.7
  41.2 0.0 collective-permute-done.3.refs_2_
  41.2 2.0 %collective-permute-start.8 = (bf16[1,2,16,32,256]{4,3,2,1,0:T(8,128)(2,1)S(1)}, bf16[1,2,16,32,256]{4,3,2,1,0:T(8,128)(2,1)S(1)}, u32[]{:S(2)}, u32[]{:S(2)}) collective-permute-start(bf16[1,2,16,32,256]{4,3,2,1,0:T(8,128)(2,1)S(1)} %get-tuple-element.29), channel_id=1, source_target_pairs={{0,8},{8,0},{16,24},{24,16},{1,9},{9,1},{17,25},{25,17},{2,10},{10... | collective-permute-start | bytes 1572872 | tf_op jit(solution)/shard_map/ppermute | solution.py:252
  43.1 0.0 collective-permute-done.4.refs_3_
  43.1 1.5 %collective-permute-start.9 = (bf16[1,2,16,32,256]{4,3,2,1,0:T(8,128)(2,1)S(1)}, bf16[1,2,16,32,256]{4,3,2,1,0:T(8,128)(2,1)S(1)}, u32[]{:S(2)}, u32[]{:S(2)}) collective-permute-start(bf16[1,2,16,32,256]{4,3,2,1,0:T(8,128)(2,1)S(1)} %get-tuple-element.30), channel_id=1, source_target_pairs={{0,16},{8,24},{16,0},{24,8},{1,17},{9,25},{17,1},{25,9},{2,18},{10... | collective-permute-start | bytes 1572872 | tf_op jit(solution)/shard_map/ppermute | solution.py:252
  44.6 0.0 collective-permute-done.5.refs_5_
  44.6 0.1 collective-permute-start.10
  44.7 0.0 copy-done.4
  44.7 13.1 %shard_map.107 = bf16[2,4,16,32,1024]{4,3,2,1,0:T(8,128)(2,1)} custom-call(s32[4]{0:T(128)S(1)} %pad_add_fusion.me_ref, bf16[4,384,256]{2,1,0:T(8,128)(2,1)S(1)} %copy-done.4, bf16[512,512]{1,0:T(8,128)(2,1)S(1)} %copy-done.1, bf16[2,4,16,32,1024]{4,3,2,1,0:T(8,128)(2,1)} %above.7, ...), custom_call_target="tpu_custom_call", output_to_operand_aliasing={{}: (8, {})} | custom-call | flops 25600000000 | bytes 16777216 | tf_op jit(solution)/shard_map/pallas_call | solution.py:179
  57.8 0.0 collective-permute-done.6.refs_6_
  57.8 0.0 collective-permute-done.7.refs_7_
  57.8 3.8 %collective-permute-done.8.refs_9_ = bf16[1,2,16,32,256]{4,3,2,1,0:T(8,128)(2,1)S(1)} collective-permute-done((bf16[1,2,16,32,256]{4,3,2,1,0:T(8,128)(2,1)S(1)}, bf16[1,2,16,32,256]{4,3,2,1,0:T(8,128)(2,1)S(1)}, u32[]{:S(2)}, u32[]{:S(2)}) %collective-permute-start.8) | collective-permute-done | bytes 524320 | tf_op jit(solution)/shard_map/ppermute | solution.py:252
  61.6 0.8 %collective-permute-done.9.refs_10_ = bf16[1,2,16,32,256]{4,3,2,1,0:T(8,128)(2,1)S(1)} collective-permute-done((bf16[1,2,16,32,256]{4,3,2,1,0:T(8,128)(2,1)S(1)}, bf16[1,2,16,32,256]{4,3,2,1,0:T(8,128)(2,1)S(1)}, u32[]{:S(2)}, u32[]{:S(2)}) %collective-permute-start.9) | collective-permute-done | bytes 524320 | tf_op jit(solution)/shard_map/ppermute | solution.py:252
  62.4 9.2 %collective-permute-done.10.refs_11_ = bf16[1,2,16,32,256]{4,3,2,1,0:T(8,128)(2,1)S(1)} collective-permute-done((bf16[1,2,16,32,256]{4,3,2,1,0:T(8,128)(2,1)S(1)}, bf16[1,2,16,32,256]{4,3,2,1,0:T(8,128)(2,1)S(1)}, u32[]{:S(2)}, u32[]{:S(2)}) %collective-permute-start.10) | collective-permute-done | bytes 524320 | tf_op jit(solution)/shard_map/ppermute | solution.py:252
  71.7 0.0 copy-start.5
  71.7 0.8 %copy-done.5 = bf16[1,2,16,32,256]{4,3,2,1,0:T(8,128)(2,1)} copy-done((bf16[1,2,16,32,256]{4,3,2,1,0:T(8,128)(2,1)}, bf16[1,2,16,32,256]{4,3,2,1,0:T(8,128)(2,1)S(1)}, u32[]{:S(2)}) %copy-start.5) | copy-done | bytes 524312
  72.5 4.0 %shard_map.108 = f32[16,32,256]{2,1,0:T(8,128)} custom-call(bf16[1,2,16,16,256]{4,3,2,1,0:T(8,128)(2,1)S(1)} %get-tuple-element.20.refs_0_, bf16[1,2,16,16,256]{4,3,2,1,0:T(8,128)(2,1)S(1)} %collective-permute-done.2.refs_1_, bf16[1,2,16,16,256]{4,3,2,1,0:T(8,128)(2,1)S(1)} %collective-permute-done.3.refs_2_, ...), custom_call_target="tpu_custom_call" | custom-call | flops 100000000 | bytes 5242880 | tf_op jit(solution)/shard_map/pallas_call | solution.py:223
Async XLA Ops:
  4.5 17.4 %collective-permute-start = (bf16[2,4,32,1024]{3,2,1,0:T(8,128)(2,1)S(1)}, bf16[2,4,32,1024]{3,2,1,0:T(8,128)(2,1)S(1)}, u32[]{:S(2)}, u32[]{:S(2)}) collective-permute-start(bf16[2,4,32,1024]{3,2,1,0:T(8,128)(2,1)S(1)} %copy.14), channel_id=1, source_target_pairs={{0,1},{1,2},{2,3},{3,4},{4,5},{5,6},{6,7},{7,0},{8,9},{9,10},{10,1... | collective-permute-start | bytes 1572872 | tf_op jit(solution)/shard_map/ppermute | solution.py:244
  5.6 16.3 %collective-permute-start.1 = (bf16[2,4,32,1024]{3,2,1,0:T(8,128)(2,1)S(1)}, bf16[2,4,32,1024]{3,2,1,0:T(8,128)(2,1)S(1)}, u32[]{:S(2)}, u32[]{:S(2)}) collective-permute-start(bf16[2,4,32,1024]{3,2,1,0:T(8,128)(2,1)S(1)} %copy.16), channel_id=1, source_target_pairs={{1,0},{2,1},{3,2},{4,3},{5,4},{6,5},{7,6},{0,7},{9,8},{10,9},{11,1... | collective-permute-start | bytes 1572872 | tf_op jit(solution)/shard_map/ppermute | solution.py:245
  9.8 1.0 %copy-start = (bf16[512,512]{1,0:T(8,128)(2,1)S(1)}, bf16[512,512]{1,0:T(8,128)(2,1)}, u32[]{:S(2)}) copy-start(bf16[512,512]{1,0:T(8,128)(2,1)} %constant.20.clone.b_ref) | copy-start | bytes 1572868
  10.8 1.0 %copy-start.2 = (bf16[4,192,192]{2,1,0:T(8,128)(2,1)S(1)}, bf16[4,192,192]{2,1,0:T(8,128)(2,1)}, u32[]{:S(2)}) copy-start(bf16[4,192,192]{2,1,0:T(8,128)(2,1)} %constant.19.clone.a_ref) | copy-start | bytes 884740
  11.8 10.1 %copy-start.1 = (bf16[512,512]{1,0:T(8,128)(2,1)S(1)}, bf16[512,512]{1,0:T(8,128)(2,1)}, u32[]{:S(2)}) copy-start(bf16[512,512]{1,0:T(8,128)(2,1)} %constant.20.clone.b_ref) | copy-start | bytes 1572868
  11.8 10.1 %copy-start.3 = (bf16[4,192,256]{2,1,0:T(8,128)(2,1)S(1)}, bf16[4,192,256]{2,1,0:T(8,128)(2,1)}, u32[]{:S(2)}) copy-start(bf16[4,192,256]{2,1,0:T(8,128)(2,1)} %constant.21.clone.a_ref) | copy-start | bytes 1179652
  18.3 22.8 %collective-permute-start.2 = (bf16[1,2,16,16,256]{4,3,2,1,0:T(8,128)(2,1)S(1)}, bf16[1,2,16,16,256]{4,3,2,1,0:T(8,128)(2,1)S(1)}, u32[]{:S(2)}, u32[]{:S(2)}) collective-permute-start(bf16[1,2,16,16,256]{4,3,2,1,0:T(8,128)(2,1)S(1)} %get-tuple-element.21), channel_id=1, source_target_pairs={{0,8},{8,0},{16,24},{24,16},{1,9},{9,1},{17,25},{25,17},{2,10},{10... | collective-permute-start | bytes 786440 | tf_op jit(solution)/shard_map/ppermute | solution.py:252
  20.3 20.8 %collective-permute-start.3 = (bf16[1,2,16,16,256]{4,3,2,1,0:T(8,128)(2,1)S(1)}, bf16[1,2,16,16,256]{4,3,2,1,0:T(8,128)(2,1)S(1)}, u32[]{:S(2)}, u32[]{:S(2)}) collective-permute-start(bf16[1,2,16,16,256]{4,3,2,1,0:T(8,128)(2,1)S(1)} %get-tuple-element.22), channel_id=1, source_target_pairs={{0,16},{8,24},{16,0},{24,8},{1,17},{9,25},{17,1},{25,9},{2,18},{10... | collective-permute-start | bytes 786440 | tf_op jit(solution)/shard_map/ppermute | solution.py:252
  21.9 21.3 %collective-permute-start.4 = (bf16[1,2,16,16,256]{4,3,2,1,0:T(8,128)(2,1)S(1)}, bf16[1,2,16,16,256]{4,3,2,1,0:T(8,128)(2,1)S(1)}, u32[]{:S(2)}, u32[]{:S(2)}) collective-permute-start(bf16[1,2,16,16,256]{4,3,2,1,0:T(8,128)(2,1)S(1)} %get-tuple-element.23), channel_id=1, source_target_pairs={{0,24},{8,16},{16,8},{24,0},{1,25},{9,17},{17,9},{25,1},{2,26},{10... | collective-permute-start | bytes 786440 | tf_op jit(solution)/shard_map/ppermute | solution.py:252
  29.3 15.3 %collective-permute-start.5 = (bf16[1,2,16,16,256]{4,3,2,1,0:T(8,128)(2,1)S(1)}, bf16[1,2,16,16,256]{4,3,2,1,0:T(8,128)(2,1)S(1)}, u32[]{:S(2)}, u32[]{:S(2)}) collective-permute-start(bf16[1,2,16,16,256]{4,3,2,1,0:T(8,128)(2,1)S(1)} %get-tuple-element.25), channel_id=1, source_target_pairs={{0,8},{8,0},{16,24},{24,16},{1,9},{9,1},{17,25},{25,17},{2,10},{10... | collective-permute-start | bytes 786440 | tf_op jit(solution)/shard_map/ppermute | solution.py:252
  31.3 26.6 %collective-permute-start.6 = (bf16[1,2,16,16,256]{4,3,2,1,0:T(8,128)(2,1)S(1)}, bf16[1,2,16,16,256]{4,3,2,1,0:T(8,128)(2,1)S(1)}, u32[]{:S(2)}, u32[]{:S(2)}) collective-permute-start(bf16[1,2,16,16,256]{4,3,2,1,0:T(8,128)(2,1)S(1)} %get-tuple-element.26), channel_id=1, source_target_pairs={{0,16},{8,24},{16,0},{24,8},{1,17},{9,25},{17,1},{25,9},{2,18},{10... | collective-permute-start | bytes 786440 | tf_op jit(solution)/shard_map/ppermute | solution.py:252
  32.8 11.9 %copy-start.4 = (bf16[4,384,256]{2,1,0:T(8,128)(2,1)S(1)}, bf16[4,384,256]{2,1,0:T(8,128)(2,1)}, u32[]{:S(2)}) copy-start(bf16[4,384,256]{2,1,0:T(8,128)(2,1)} %constant.22.clone.a_ref) | copy-start | bytes 2359300
  41.1 16.7 %collective-permute-start.7 = (bf16[1,2,16,16,256]{4,3,2,1,0:T(8,128)(2,1)S(1)}, bf16[1,2,16,16,256]{4,3,2,1,0:T(8,128)(2,1)S(1)}, u32[]{:S(2)}, u32[]{:S(2)}) collective-permute-start(bf16[1,2,16,16,256]{4,3,2,1,0:T(8,128)(2,1)S(1)} %get-tuple-element.27), channel_id=1, source_target_pairs={{0,24},{8,16},{16,8},{24,0},{1,25},{9,17},{17,9},{25,1},{2,26},{10... | collective-permute-start | bytes 786440 | tf_op jit(solution)/shard_map/ppermute | solution.py:252
  41.2 20.4 %collective-permute-start.8 = (bf16[1,2,16,32,256]{4,3,2,1,0:T(8,128)(2,1)S(1)}, bf16[1,2,16,32,256]{4,3,2,1,0:T(8,128)(2,1)S(1)}, u32[]{:S(2)}, u32[]{:S(2)}) collective-permute-start(bf16[1,2,16,32,256]{4,3,2,1,0:T(8,128)(2,1)S(1)} %get-tuple-element.29), channel_id=1, source_target_pairs={{0,8},{8,0},{16,24},{24,16},{1,9},{9,1},{17,25},{25,17},{2,10},{10... | collective-permute-start | bytes 1572872 | tf_op jit(solution)/shard_map/ppermute | solution.py:252
  43.1 19.3 %collective-permute-start.9 = (bf16[1,2,16,32,256]{4,3,2,1,0:T(8,128)(2,1)S(1)}, bf16[1,2,16,32,256]{4,3,2,1,0:T(8,128)(2,1)S(1)}, u32[]{:S(2)}, u32[]{:S(2)}) collective-permute-start(bf16[1,2,16,32,256]{4,3,2,1,0:T(8,128)(2,1)S(1)} %get-tuple-element.30), channel_id=1, source_target_pairs={{0,16},{8,24},{16,0},{24,8},{1,17},{9,25},{17,1},{25,9},{2,18},{10... | collective-permute-start | bytes 1572872 | tf_op jit(solution)/shard_map/ppermute | solution.py:252
  44.6 27.1 %collective-permute-start.10 = (bf16[1,2,16,32,256]{4,3,2,1,0:T(8,128)(2,1)S(1)}, bf16[1,2,16,32,256]{4,3,2,1,0:T(8,128)(2,1)S(1)}, u32[]{:S(2)}, u32[]{:S(2)}) collective-permute-start(bf16[1,2,16,32,256]{4,3,2,1,0:T(8,128)(2,1)S(1)} %get-tuple-element.31), channel_id=1, source_target_pairs={{0,24},{8,16},{16,8},{24,0},{1,25},{9,17},{17,9},{25,1},{2,26},{10... | collective-permute-start | bytes 1572872 | tf_op jit(solution)/shard_map/ppermute | solution.py:252
  71.7 0.8 %copy-start.5 = (bf16[1,2,16,32,256]{4,3,2,1,0:T(8,128)(2,1)}, bf16[1,2,16,32,256]{4,3,2,1,0:T(8,128)(2,1)S(1)}, u32[]{:S(2)}) copy-start(bf16[1,2,16,32,256]{4,3,2,1,0:T(8,128)(2,1)S(1)} %collective-permute-done.10.refs_11_) | copy-start | bytes 1572868

commit v6 on v5

--- a/solution.py
+++ b/solution.py
@@ -184,7 +184,7 @@
         ),
         input_output_aliases=alias,
         compiler_params=pltpu.CompilerParams(vmem_limit_bytes=vmem),
-        cost_estimate=pl.CostEstimate(flops=share * 4 * 10**8, bytes_accessed=share * 2**18, transcendentals=0),
+        cost_estimate=pl.CostEstimate(flops=share * 4 * 10**9, bytes_accessed=share * 2**18, transcendentals=0),
     )(*args)
 
 
@@ -261,6 +261,7 @@
     edges = exchange(blocks)
     wholes = []
     if m_ > 1:
+        stepped, mids[1] = lax.optimization_barrier((stepped, mids[1]))
         stepped, *blocks = run_step("full", 2, (1, m_), parts, halves, order, state, lo, hi, None, stepped)
         wholes = exchange(blocks)
     (stepped,) = run_step("rest", 0, (0, m_), parts, halves, order, state, lo, hi, None, stepped)

time: 77.2 us -> 72.5 us (0.939)
  waiting for transfers between devices: 13.8 us -> 7.75 us
  Pallas kernels: 39.4 us -> 40.8 us
    ppermute x9, waiting for transfers between devices: 13.8 us -> 7.74 us  [exchange(): lax.ppermute(blocks[k], 'member', [(i, partner(i, k, parts)) for i in ran...]
    pallas_call x4, Pallas kernels: 35.3 us -> 36.4 us  [run_step(): pl.pallas_call(functools.partial(step_kernel, kind, first, parts, spans),...]
    unnamed x12 -> x14, local copies, waits for them, and re-layouts: 2.84 us -> 2.77 us
  transfers between devices with their start and end apart: 11 -> 11, of which waited for: 3 -> 1; matrix products, arithmetic and copies ran while one was open for 1% -> 1% of each run, Pallas kernels for 46% -> 51%
where the time goes in v6:
time: 72.5 us; the launch traced here: 71.7 us
  Pallas kernels  40.8 us (56%)
  starting transfers between devices  15.2 us (21%)
  waiting for transfers between devices  7.75 us (11%)
  local copies, waits for them, and re-layouts  7.2 us (10%)
    pallas_call x4, Pallas kernels, run_step(): pl.pallas_call(functools.partial(step_kernel, kind, first, parts, spans),...  36.4 us
    ppermute x9, starting transfers between devices, exchange(): lax.ppermute(blocks[k], 'member', [(i, partner(i, k, parts)) for i in ran...  10.6 us
    ppermute x9, waiting for transfers between devices, exchange(): lax.ppermute(blocks[k], 'member', [(i, partner(i, k, parts)) for i in ran...  7.74 us
    pallas_call x1, Pallas kernels, run_correlate(): pl.pallas_call(functools.partial(correlate_kernel, count, len(mids)), out...  4.4 us
    ppermute x1, starting transfers between devices, on_device(): lax.ppermute(head, 'space', [((i + 1) % count, i) for i in range(count)])  4.11 us
    slice x2, local copies, waits for them, and re-layouts, on_device(): head = state[:, :, :, :2, :].reshape(m_, 4, 2 * levels, cols)  3.7 us
    unnamed x14, local copies, waits for them, and re-layouts  2.77 us
  transfers between devices with their start and end apart: 11, of which 1 were waited for; matrix products, arithmetic and copies ran while one was open for 1% of the time, Pallas kernels for 51%

profile of v6, /device:TPU:0, one launch (start us, length us, event | category | flops | bytes accessed | tf_op | source)
XLA Modules:
  0.0 71.7 jit_solution(14257816471744931846)
XLA Ops:
  0.6 3.3 %fusion = (bf16[2,4,16,2,1024]{4,3,2,1,0:T(2,128)(2,1)S(1)}, bf16[2,4,16,2,1024]{4,3,2,1,0:T(2,128)(2,1)S(1)}) fusion(bf16[2,4,16,32,1024]{4,3,2,1,0:T(8,128)(2,1)} %above.7), kind=kLoop, calls=%fused_computation.1 | loop fusion | bytes 2097152 | tf_op jit(solution)/shard_map/slice | solution.py:242
  3.9 0.4 copy.13
  4.3 0.2 copy.14
  4.5 0.5 collective-permute-start
  5.0 0.4 copy.15
  5.4 0.2 copy.16
  5.6 4.1 %collective-permute-start.1 = (bf16[2,4,32,1024]{3,2,1,0:T(8,128)(2,1)S(1)}, bf16[2,4,32,1024]{3,2,1,0:T(8,128)(2,1)S(1)}, u32[]{:S(2)}, u32[]{:S(2)}) collective-permute-start(bf16[2,4,32,1024]{3,2,1,0:T(8,128)(2,1)S(1)} %copy.16), channel_id=1, source_target_pairs={{1,0},{2,1},{3,2},{4,3},{5,4},{6,5},{7,6},{0,7},{9,8},{10,9},{11,1... | collective-permute-start | bytes 1572872 | tf_op jit(solution)/shard_map/ppermute | solution.py:245
  9.7 0.1 pad_add_fusion.me_ref
  9.8 0.0 copy-start.3
  9.8 1.0 %copy-done.3 = bf16[512,512]{1,0:T(8,128)(2,1)S(1)} copy-done((bf16[512,512]{1,0:T(8,128)(2,1)S(1)}, bf16[512,512]{1,0:T(8,128)(2,1)}, u32[]{:S(2)}) %copy-start.3) | copy-done | bytes 524312
  10.8 0.0 copy-start.6
  10.8 1.0 %copy-done.6 = bf16[4,192,192]{2,1,0:T(8,128)(2,1)S(1)} copy-done((bf16[4,192,192]{2,1,0:T(8,128)(2,1)S(1)}, bf16[4,192,192]{2,1,0:T(8,128)(2,1)}, u32[]{:S(2)}) %copy-start.6) | copy-done | bytes 294936
  11.8 0.0 copy-start.4
  11.8 0.0 copy-start.5
  11.8 7.1 %shard_map.104 = (bf16[1,2,16,16,1024]{4,3,2,1,0:T(8,128)(2,1)S(1)}, bf16[1,2,16,16,256]{4,3,2,1,0:T(8,128)(2,1)S(1)}, bf16[1,2,16,16,256]{4,3,2,1,0:T(8,128)(2,...) custom-call(s32[4]{0:T(128)S(1)} %pad_add_fusion.me_ref, bf16[4,192,192]{2,1,0:T(8,128)(2,1)S(1)} %copy-done.6, ...), custom_call_target="tpu_custom_call" | custom-call | flops 64000000000 | bytes 4194304 | tf_op jit(solution)/shard_map/pallas_call | solution.py:179
  18.9 2.0 %collective-permute-start.2 = (bf16[1,2,16,16,256]{4,3,2,1,0:T(8,128)(2,1)S(1)}, bf16[1,2,16,16,256]{4,3,2,1,0:T(8,128)(2,1)S(1)}, u32[]{:S(2)}, u32[]{:S(2)}) collective-permute-start(bf16[1,2,16,16,256]{4,3,2,1,0:T(8,128)(2,1)S(1)} %get-tuple-element.21), channel_id=1, source_target_pairs={{0,8},{8,0},{16,24},{24,16},{1,9},{9,1},{17,25},{25,17},{2,10},{10... | collective-permute-start | bytes 786440 | tf_op jit(solution)/shard_map/ppermute | solution.py:252
  20.9 1.5 %collective-permute-start.3 = (bf16[1,2,16,16,256]{4,3,2,1,0:T(8,128)(2,1)}, bf16[1,2,16,16,256]{4,3,2,1,0:T(8,128)(2,1)}, u32[]{:S(2)}, u32[]{:S(2)}) collective-permute-start(bf16[1,2,16,16,256]{4,3,2,1,0:T(8,128)(2,1)} %get-tuple-element.26), channel_id=1, source_target_pairs={{0,16},{8,24},{16,0},{24,8},{1,17},{9,25},{17,1},{25,9},{2,18},{10... | collective-permute-start | bytes 786440 | tf_op jit(solution)/shard_map/ppermute | solution.py:252
  22.5 0.0 collective-permute-start.4
  22.5 0.0 collective-permute-done.rest_0_
  22.5 0.0 collective-permute-done.1.rest_1_
  22.5 0.0 copy-done.4
  22.5 0.0 copy-done.5
  22.5 7.5 %shard_map.105 = (bf16[2,4,16,32,1024]{4,3,2,1,0:T(8,128)(2,1)}, bf16[1,2,16,16,256]{4,3,2,1,0:T(8,128)(2,1)S(1)}, bf16[1,2,16,16,256]{4,3,2,1,0:T(8,128)(2,1)S(...) custom-call(s32[4]{0:T(128)S(1)} %pad_add_fusion.me_ref, bf16[4,192,256]{2,1,0:T(8,128)(2,1)S(1)} %copy-done.5, ...), custom_call_target="tpu_custom_call" | custom-call | flops 64000000000 | bytes 4194304 | tf_op jit(solution)/shard_map/pallas_call | solution.py:179
  30.0 0.0 collective-permute-done.2.refs_1_
  30.0 2.0 %collective-permute-start.5 = (bf16[1,2,16,16,256]{4,3,2,1,0:T(8,128)(2,1)S(1)}, bf16[1,2,16,16,256]{4,3,2,1,0:T(8,128)(2,1)S(1)}, u32[]{:S(2)}, u32[]{:S(2)}) collective-permute-start(bf16[1,2,16,16,256]{4,3,2,1,0:T(8,128)(2,1)S(1)} %get-tuple-element.29), channel_id=1, source_target_pairs={{0,8},{8,0},{16,24},{24,16},{1,9},{9,1},{17,25},{25,17},{2,10},{10... | collective-permute-start | bytes 786440 | tf_op jit(solution)/shard_map/ppermute | solution.py:252
  32.0 1.5 %collective-permute-start.6 = (bf16[1,2,16,16,256]{4,3,2,1,0:T(8,128)(2,1)}, bf16[1,2,16,16,256]{4,3,2,1,0:T(8,128)(2,1)}, u32[]{:S(2)}, u32[]{:S(2)}) collective-permute-start(bf16[1,2,16,16,256]{4,3,2,1,0:T(8,128)(2,1)} %get-tuple-element.30), channel_id=1, source_target_pairs={{0,16},{8,24},{16,0},{24,8},{1,17},{9,25},{17,1},{25,9},{2,18},{10... | collective-permute-start | bytes 786440 | tf_op jit(solution)/shard_map/ppermute | solution.py:252
  33.5 0.0 copy-start.2
  33.5 0.0 collective-permute-start.7
  33.5 8.6 %shard_map.106 = (bf16[2,4,16,32,1024]{4,3,2,1,0:T(8,128)(2,1)}, bf16[1,2,16,32,256]{4,3,2,1,0:T(8,128)(2,1)S(1)}, bf16[1,2,16,32,256]{4,3,2,1,0:T(8,128)(2,1)},...) custom-call(s32[4]{0:T(128)S(1)} %pad_add_fusion.me_ref, ...), custom_call_target="tpu_custom_call", output_to_operand_aliasing={{0}: (8, {})} | custom-call | flops 128000000000 | bytes 8388608 | tf_op jit(solution)/shard_map/pallas_call | solution.py:179
  42.1 0.0 collective-permute-done.3.refs_2_
  42.2 2.0 %collective-permute-start.8 = (bf16[1,2,16,32,256]{4,3,2,1,0:T(8,128)(2,1)}, bf16[1,2,16,32,256]{4,3,2,1,0:T(8,128)(2,1)}, u32[]{:S(2)}, u32[]{:S(2)}) collective-permute-start(bf16[1,2,16,32,256]{4,3,2,1,0:T(8,128)(2,1)} %get-tuple-element.33), channel_id=1, source_target_pairs={{0,8},{8,0},{16,24},{24,16},{1,9},{9,1},{17,25},{25,17},{2,10},{10... | collective-permute-start | bytes 1572872 | tf_op jit(solution)/shard_map/ppermute | solution.py:252
  44.2 0.0 collective-permute-done.4.refs_3_
  44.2 1.5 %collective-permute-start.9 = (bf16[1,2,16,32,256]{4,3,2,1,0:T(8,128)(2,1)}, bf16[1,2,16,32,256]{4,3,2,1,0:T(8,128)(2,1)}, u32[]{:S(2)}, u32[]{:S(2)}) collective-permute-start(bf16[1,2,16,32,256]{4,3,2,1,0:T(8,128)(2,1)} %get-tuple-element.34), channel_id=1, source_target_pairs={{0,16},{8,24},{16,0},{24,8},{1,17},{9,25},{17,1},{25,9},{2,18},{10... | collective-permute-start | bytes 1572872 | tf_op jit(solution)/shard_map/ppermute | solution.py:252
  45.7 0.0 collective-permute-done.5.refs_5_
  45.7 0.0 copy-start
  45.7 0.7 %copy-done = bf16[1,2,16,16,256]{4,3,2,1,0:T(8,128)(2,1)} copy-done((bf16[1,2,16,16,256]{4,3,2,1,0:T(8,128)(2,1)}, bf16[1,2,16,16,256]{4,3,2,1,0:T(8,128)(2,1)S(1)}, u32[]{:S(2)}) %copy-start) | copy-done | bytes 262168
  46.4 0.0 collective-permute-start.10
  46.5 0.0 copy-done.2
  46.5 0.0 copy-start.1
  46.5 13.1 %shard_map.107 = bf16[2,4,16,32,1024]{4,3,2,1,0:T(8,128)(2,1)} custom-call(s32[4]{0:T(128)S(1)} %pad_add_fusion.me_ref, bf16[4,384,256]{2,1,0:T(8,128)(2,1)S(1)} %copy-done.2, bf16[512,512]{1,0:T(8,128)(2,1)S(1)} %copy-done.4, bf16[2,4,16,32,1024]{4,3,2,1,0:T(8,128)(2,1)} %above.7, ...), custom_call_target="tpu_custom_call", output_to_operand_aliasing={{}: (8, {})} | custom-call | flops 256000000000 | bytes 16777216 | tf_op jit(solution)/shard_map/pallas_call | solution.py:179
  59.6 0.0 collective-permute-done.6.refs_6_
  59.6 0.0 collective-permute-done.7.refs_7_
  59.6 0.0 collective-permute-done.8.refs_9_
  59.6 7.7 %collective-permute-done.9.refs_10_ = bf16[1,2,16,32,256]{4,3,2,1,0:T(8,128)(2,1)} collective-permute-done((bf16[1,2,16,32,256]{4,3,2,1,0:T(8,128)(2,1)}, bf16[1,2,16,32,256]{4,3,2,1,0:T(8,128)(2,1)}, u32[]{:S(2)}, u32[]{:S(2)}) %collective-permute-start.9) | collective-permute-done | bytes 524320 | tf_op jit(solution)/shard_map/ppermute | solution.py:252
  67.3 0.0 collective-permute-done.10.refs_11_
  67.3 0.0 copy-done.1
  67.3 4.4 %shard_map.108 = f32[16,32,256]{2,1,0:T(8,128)} custom-call(bf16[1,2,16,16,256]{4,3,2,1,0:T(8,128)(2,1)S(1)} %get-tuple-element.24.refs_0_, bf16[1,2,16,16,256]{4,3,2,1,0:T(8,128)(2,1)S(1)} %collective-permute-done.2.refs_1_, bf16[1,2,16,16,256]{4,3,2,1,0:T(8,128)(2,1)} %collective-permute-done.3.refs_2_, ...), custom_call_target="tpu_custom_call" | custom-call | flops 100000000 | bytes 5242880 | tf_op jit(solution)/shard_map/pallas_call | solution.py:223
Async XLA Ops:
  4.5 17.9 %collective-permute-start = (bf16[2,4,32,1024]{3,2,1,0:T(8,128)(2,1)S(1)}, bf16[2,4,32,1024]{3,2,1,0:T(8,128)(2,1)S(1)}, u32[]{:S(2)}, u32[]{:S(2)}) collective-permute-start(bf16[2,4,32,1024]{3,2,1,0:T(8,128)(2,1)S(1)} %copy.14), channel_id=1, source_target_pairs={{0,1},{1,2},{2,3},{3,4},{4,5},{5,6},{6,7},{7,0},{8,9},{9,10},{10,1... | collective-permute-start | bytes 1572872 | tf_op jit(solution)/shard_map/ppermute | solution.py:244
  5.6 16.9 %collective-permute-start.1 = (bf16[2,4,32,1024]{3,2,1,0:T(8,128)(2,1)S(1)}, bf16[2,4,32,1024]{3,2,1,0:T(8,128)(2,1)S(1)}, u32[]{:S(2)}, u32[]{:S(2)}) collective-permute-start(bf16[2,4,32,1024]{3,2,1,0:T(8,128)(2,1)S(1)} %copy.16), channel_id=1, source_target_pairs={{1,0},{2,1},{3,2},{4,3},{5,4},{6,5},{7,6},{0,7},{9,8},{10,9},{11,1... | collective-permute-start | bytes 1572872 | tf_op jit(solution)/shard_map/ppermute | solution.py:245
  9.8 1.0 %copy-start.3 = (bf16[512,512]{1,0:T(8,128)(2,1)S(1)}, bf16[512,512]{1,0:T(8,128)(2,1)}, u32[]{:S(2)}) copy-start(bf16[512,512]{1,0:T(8,128)(2,1)} %constant.20.clone.b_ref) | copy-start | bytes 1572868
  10.8 1.0 %copy-start.6 = (bf16[4,192,192]{2,1,0:T(8,128)(2,1)S(1)}, bf16[4,192,192]{2,1,0:T(8,128)(2,1)}, u32[]{:S(2)}) copy-start(bf16[4,192,192]{2,1,0:T(8,128)(2,1)} %constant.19.clone.a_ref) | copy-start | bytes 884740
  11.8 10.7 %copy-start.4 = (bf16[512,512]{1,0:T(8,128)(2,1)S(1)}, bf16[512,512]{1,0:T(8,128)(2,1)}, u32[]{:S(2)}) copy-start(bf16[512,512]{1,0:T(8,128)(2,1)} %constant.20.clone.b_ref) | copy-start | bytes 1572868
  11.8 10.7 %copy-start.5 = (bf16[4,192,256]{2,1,0:T(8,128)(2,1)S(1)}, bf16[4,192,256]{2,1,0:T(8,128)(2,1)}, u32[]{:S(2)}) copy-start(bf16[4,192,256]{2,1,0:T(8,128)(2,1)} %constant.21.clone.a_ref) | copy-start | bytes 1179652
  18.9 11.0 %collective-permute-start.2 = (bf16[1,2,16,16,256]{4,3,2,1,0:T(8,128)(2,1)S(1)}, bf16[1,2,16,16,256]{4,3,2,1,0:T(8,128)(2,1)S(1)}, u32[]{:S(2)}, u32[]{:S(2)}) collective-permute-start(bf16[1,2,16,16,256]{4,3,2,1,0:T(8,128)(2,1)S(1)} %get-tuple-element.21), channel_id=1, source_target_pairs={{0,8},{8,0},{16,24},{24,16},{1,9},{9,1},{17,25},{25,17},{2,10},{10... | collective-permute-start | bytes 786440 | tf_op jit(solution)/shard_map/ppermute | solution.py:252
  20.9 21.2 %collective-permute-start.3 = (bf16[1,2,16,16,256]{4,3,2,1,0:T(8,128)(2,1)}, bf16[1,2,16,16,256]{4,3,2,1,0:T(8,128)(2,1)}, u32[]{:S(2)}, u32[]{:S(2)}) collective-permute-start(bf16[1,2,16,16,256]{4,3,2,1,0:T(8,128)(2,1)} %get-tuple-element.26), channel_id=1, source_target_pairs={{0,16},{8,24},{16,0},{24,8},{1,17},{9,25},{17,1},{25,9},{2,18},{10... | collective-permute-start | bytes 786440 | tf_op jit(solution)/shard_map/ppermute | solution.py:252
  22.5 21.7 %collective-permute-start.4 = (bf16[1,2,16,16,256]{4,3,2,1,0:T(8,128)(2,1)}, bf16[1,2,16,16,256]{4,3,2,1,0:T(8,128)(2,1)}, u32[]{:S(2)}, u32[]{:S(2)}) collective-permute-start(bf16[1,2,16,16,256]{4,3,2,1,0:T(8,128)(2,1)} %get-tuple-element.27), channel_id=1, source_target_pairs={{0,24},{8,16},{16,8},{24,0},{1,25},{9,17},{17,9},{25,1},{2,26},{10... | collective-permute-start | bytes 786440 | tf_op jit(solution)/shard_map/ppermute | solution.py:252
  30.0 15.7 %collective-permute-start.5 = (bf16[1,2,16,16,256]{4,3,2,1,0:T(8,128)(2,1)S(1)}, bf16[1,2,16,16,256]{4,3,2,1,0:T(8,128)(2,1)S(1)}, u32[]{:S(2)}, u32[]{:S(2)}) collective-permute-start(bf16[1,2,16,16,256]{4,3,2,1,0:T(8,128)(2,1)S(1)} %get-tuple-element.29), channel_id=1, source_target_pairs={{0,8},{8,0},{16,24},{24,16},{1,9},{9,1},{17,25},{25,17},{2,10},{10... | collective-permute-start | bytes 786440 | tf_op jit(solution)/shard_map/ppermute | solution.py:252
  32.0 27.6 %collective-permute-start.6 = (bf16[1,2,16,16,256]{4,3,2,1,0:T(8,128)(2,1)}, bf16[1,2,16,16,256]{4,3,2,1,0:T(8,128)(2,1)}, u32[]{:S(2)}, u32[]{:S(2)}) collective-permute-start(bf16[1,2,16,16,256]{4,3,2,1,0:T(8,128)(2,1)} %get-tuple-element.30), channel_id=1, source_target_pairs={{0,16},{8,24},{16,0},{24,8},{1,17},{9,25},{17,1},{25,9},{2,18},{10... | collective-permute-start | bytes 786440 | tf_op jit(solution)/shard_map/ppermute | solution.py:252
  33.5 12.9 %copy-start.2 = (bf16[4,384,256]{2,1,0:T(8,128)(2,1)S(1)}, bf16[4,384,256]{2,1,0:T(8,128)(2,1)}, u32[]{:S(2)}) copy-start(bf16[4,384,256]{2,1,0:T(8,128)(2,1)} %constant.22.clone.a_ref) | copy-start | bytes 2359300
  33.5 26.1 %collective-permute-start.7 = (bf16[1,2,16,16,256]{4,3,2,1,0:T(8,128)(2,1)}, bf16[1,2,16,16,256]{4,3,2,1,0:T(8,128)(2,1)}, u32[]{:S(2)}, u32[]{:S(2)}) collective-permute-start(bf16[1,2,16,16,256]{4,3,2,1,0:T(8,128)(2,1)} %get-tuple-element.31), channel_id=1, source_target_pairs={{0,24},{8,16},{16,8},{24,0},{1,25},{9,17},{17,9},{25,1},{2,26},{10... | collective-permute-start | bytes 786440 | tf_op jit(solution)/shard_map/ppermute | solution.py:252
  42.2 17.4 %collective-permute-start.8 = (bf16[1,2,16,32,256]{4,3,2,1,0:T(8,128)(2,1)}, bf16[1,2,16,32,256]{4,3,2,1,0:T(8,128)(2,1)}, u32[]{:S(2)}, u32[]{:S(2)}) collective-permute-start(bf16[1,2,16,32,256]{4,3,2,1,0:T(8,128)(2,1)} %get-tuple-element.33), channel_id=1, source_target_pairs={{0,8},{8,0},{16,24},{24,16},{1,9},{9,1},{17,25},{25,17},{2,10},{10... | collective-permute-start | bytes 1572872 | tf_op jit(solution)/shard_map/ppermute | solution.py:252
  44.2 23.2 %collective-permute-start.9 = (bf16[1,2,16,32,256]{4,3,2,1,0:T(8,128)(2,1)}, bf16[1,2,16,32,256]{4,3,2,1,0:T(8,128)(2,1)}, u32[]{:S(2)}, u32[]{:S(2)}) collective-permute-start(bf16[1,2,16,32,256]{4,3,2,1,0:T(8,128)(2,1)} %get-tuple-element.34), channel_id=1, source_target_pairs={{0,16},{8,24},{16,0},{24,8},{1,17},{9,25},{17,1},{25,9},{2,18},{10... | collective-permute-start | bytes 1572872 | tf_op jit(solution)/shard_map/ppermute | solution.py:252
  45.7 0.7 %copy-start = (bf16[1,2,16,16,256]{4,3,2,1,0:T(8,128)(2,1)}, bf16[1,2,16,16,256]{4,3,2,1,0:T(8,128)(2,1)S(1)}, u32[]{:S(2)}) copy-start(bf16[1,2,16,16,256]{4,3,2,1,0:T(8,128)(2,1)S(1)} %collective-permute-done.5.refs_5_) | copy-start | bytes 786436
  46.4 20.9 %collective-permute-start.10 = (bf16[1,2,16,32,256]{4,3,2,1,0:T(8,128)(2,1)}, bf16[1,2,16,32,256]{4,3,2,1,0:T(8,128)(2,1)}, u32[]{:S(2)}, u32[]{:S(2)}) collective-permute-start(bf16[1,2,16,32,256]{4,3,2,1,0:T(8,128)(2,1)} %get-tuple-element.35), channel_id=1, source_target_pairs={{0,24},{8,16},{16,8},{24,0},{1,25},{9,17},{17,9},{25,1},{2,26},{10... | collective-permute-start | bytes 1572872 | tf_op jit(solution)/shard_map/ppermute | solution.py:252
  46.5 20.9 %copy-start.1 = (bf16[1,2,16,16,256]{4,3,2,1,0:T(8,128)(2,1)S(1)}, bf16[1,2,16,16,256]{4,3,2,1,0:T(8,128)(2,1)}, u32[]{:S(2)}) copy-start(bf16[1,2,16,16,256]{4,3,2,1,0:T(8,128)(2,1)} %copy-done) | copy-start | bytes 786436
